TPU v7x, 32 devices: a whole 2x2x4 slice. The times are simulated.
32 devices in a mesh: seq: 4 (over y, x), dp: 8 (over z, core).
Axes of the slice: x: 2, y: 2, z: 4, core: 2. Of those that a mesh axis runs over, the one named last changes fastest.
Arguments:
- tokens: bfloat16 [16, 1536, 2048], P('dp', 'seq'), may hold values from -6 to 6
- cotangent: bfloat16 [16, 1536, 2048], P('dp', 'seq'), may hold values from -6 to 6
- weight: bfloat16 [2048, 6144], P('dp'), may hold values from -0.125 to 0.125
- forget_peep: float32 [2048], replicated, may hold values from -3 to 3
- reset_peep: float32 [2048], replicated, may hold values from -4 to 4
- forget_bias: float32 [2048], replicated, may hold values from 0 to 8.5
- reset_bias: float32 [2048], replicated, may hold values from -4 to 4
- norm_gain: float32 [2048], replicated, may hold values from 0.5 to 1.5
- norm_bias: float32 [2048], replicated, may hold values from -3 to 3
- lengths: int32 [16], P('dp'), may hold values from 384 to 1536, as said below
Outputs:
- activations: float32 [16, 1536, 2048], P('dp', 'seq')
- input_grad: float32 [16, 1536, 2048], P('dp', 'seq')
- weight_grad: float32 [2048, 6144], P('dp', 'seq')
- forget_peep_grad: float32 [2048], replicated
- reset_peep_grad: float32 [2048], replicated
- forget_bias_grad: float32 [2048], replicated
- reset_bias_grad: float32 [2048], replicated
- norm_gain_grad: float32 [2048], replicated
- norm_bias_grad: float32 [2048], replicated
Inputs may be any that keep to these rules, and one draw needn't show every extreme that they name: `lengths`: each micro-batch of 2 sequences holds one of full length 1536.
All inputs are finite; a program needn't handle non-finite values.
Results may differ from a plain program's by a relative error of at most 0.004.
Values may be sent and summed in bfloat16 or wider, within the bound.
No kernel may reach another device: no remote copies, remote signals or barrier semaphores. Data moves between devices by JAX's collectives and lax.ppermute only.
A program may use at most 256 MiB of HBM per device.

v0:
```python
import jax
import jax.numpy as jnp
from jax import lax
from jax.sharding import PartitionSpec as P

EPS = 1e-05


def prefix(value, axis, join, neutral, backward):
    count, mine = (lax.axis_size(axis), lax.axis_index(axis))
    pieces = jax.tree.map(lambda part: lax.all_gather(part, axis), value)
    if backward:
        pieces = jax.tree.map(lambda part: part[::-1], pieces)
        mine = count - 1 - mine
    subtotal = jax.tree.map(
        lambda part, zero: jnp.full_like(part, 0) + jnp.asarray(zero, part.dtype), value, neutral
    )

    def lap(position, subtotal):
        longer = join(subtotal, jax.tree.map(lambda part: part[position], pieces))
        return jax.tree.map(lambda new, old: jnp.where(position < mine, new, old), longer, subtotal)

    return lax.fori_loop(0, count - 1, lap, subtotal)


def combine(earlier, later):
    return (earlier[0] * later[0], later[0] * earlier[1] + later[1])


def local(
    tokens,
    cotangent,
    weight,
    forget_peep,
    reset_peep,
    forget_bias,
    reset_bias,
    norm_gain,
    norm_bias,
    lengths,
):
    seqs, span, width = tokens.shape
    nseq = lax.axis_size("seq")
    seq_index = lax.axis_index("seq")
    rows = seqs * span
    inputs = tokens.astype(jnp.float32)
    mean = jnp.mean(inputs, axis=-1, keepdims=True)
    centered = inputs - mean
    var = jnp.mean(centered * centered, axis=-1, keepdims=True)
    rstd = lax.rsqrt(var + EPS)
    normed = centered * rstd
    unit = normed * norm_gain + norm_bias
    unit_low = unit.astype(jnp.bfloat16).reshape(rows, width)
    columns = unit_low
    proj = jnp.dot(
        columns,
        lax.all_gather(weight, "dp", axis=0, tiled=True),
        preferred_element_type=jnp.float32,
    )
    proj = proj.reshape(seqs, span, 3 * width)
    cand = proj[..., :width]
    fpre = proj[..., width : 2 * width]
    rpre = proj[..., 2 * width :]
    places = seq_index * span + lax.iota(jnp.int32, span)
    live = (places[None, :] < lengths[:, None])[..., None]
    forget = jax.nn.sigmoid(fpre + forget_peep * unit + forget_bias)
    decay = jnp.where(live, forget, 1.0)
    inject = jnp.where(live, (1.0 - forget) * cand, 0.0)
    prod_fwd, local_fwd = lax.associative_scan(combine, (decay, inject), axis=1)
    summary = (prod_fwd[:, -1], local_fwd[:, -1])
    identity = (jnp.ones_like(summary[0]), jnp.zeros_like(summary[1]))
    incoming = prefix(summary, "seq", combine, identity, False)
    carry_in = incoming[1]
    state = local_fwd + prod_fwd * carry_in[:, None]
    before = jnp.concatenate([carry_in[:, None], state[:, :-1]], axis=1)
    reset = jax.nn.sigmoid(rpre + reset_peep * before + reset_bias)
    highway = reset * state + (1.0 - reset) * unit
    activations = inputs + jnp.where(live, highway, 0.0)
    counts = jnp.sum(lengths).astype(jnp.float32)
    scale = seqs * span * nseq / counts
    grad_out = jnp.where(live, cotangent.astype(jnp.float32), 0.0) * scale
    reset_logit_grad = grad_out * (state - unit) * reset * (1.0 - reset)
    state_direct = grad_out * reset
    unit_grad = grad_out * (1.0 - reset)
    source = decay * state_direct + reset_peep * reset_logit_grad
    prod_back, local_back = lax.associative_scan(combine, (decay, source), reverse=True, axis=1)
    summary_back = (prod_back[:, 0], local_back[:, 0])
    incoming_back = prefix(summary_back, "seq", combine, identity, True)
    after_in = incoming_back[1]
    ahead = jnp.concatenate(
        [local_back[:, 1:] + prod_back[:, 1:] * after_in[:, None], after_in[:, None]], axis=1
    )
    total = state_direct + ahead
    cand_grad = jnp.where(live, total * (1.0 - forget), 0.0)
    forget_logit_grad = jnp.where(live, total * (before - cand), 0.0) * forget * (1.0 - forget)
    unit_grad = unit_grad + forget_logit_grad * forget_peep
    proj_grad = (
        jnp.concatenate([cand_grad, forget_logit_grad, reset_logit_grad], axis=-1)
        .astype(jnp.bfloat16)
        .reshape(rows, 3 * width)
    )
    unit_matrix = lax.dot_general(
        proj_grad,
        lax.all_gather(weight, "dp", axis=0, tiled=True),
        (((1,), (1,)), ((), ())),
        preferred_element_type=jnp.float32,
    )
    unit_grad = unit_grad + unit_matrix.reshape(seqs, span, width)
    gain_part = jnp.sum(unit_grad * normed, axis=(0, 1))
    nbias_part = jnp.sum(unit_grad, axis=(0, 1))
    normed_grad = unit_grad * norm_gain
    input_grad = (
        rstd
        * (
            normed_grad
            - jnp.mean(normed_grad, axis=-1, keepdims=True)
            - normed * jnp.mean(normed_grad * normed, axis=-1, keepdims=True)
        )
        + grad_out
    )
    columns = unit_low
    partial_rows = lax.psum_scatter(
        lax.dot_general(
            columns, proj_grad, (((0,), (0,)), ((), ())), preferred_element_type=jnp.float32
        ),
        "dp",
        scatter_dimension=0,
        tiled=True,
    )
    weight_grad = lax.psum_scatter(partial_rows, "seq", scatter_dimension=1, tiled=True)
    sums = lax.psum(
        (
            jnp.sum(forget_logit_grad * unit, axis=(0, 1)),
            jnp.sum(reset_logit_grad * before, axis=(0, 1)),
            jnp.sum(forget_logit_grad, axis=(0, 1)),
            jnp.sum(reset_logit_grad, axis=(0, 1)),
            gain_part,
            nbias_part,
        ),
        ("seq", "dp"),
    )
    return (
        activations,
        input_grad,
        weight_grad,
        sums[0],
        sums[1],
        sums[2],
        sums[3],
        sums[4],
        sums[5],
    )


def solution(mesh):
    in_specs = (
        P("dp", "seq", None),
        P("dp", "seq", None),
        P("dp", None),
        P(),
        P(),
        P(),
        P(),
        P(),
        P(),
        P("dp"),
    )
    out_specs = (
        P("dp", "seq", None),
        P("dp", "seq", None),
        P("dp", "seq"),
        P(),
        P(),
        P(),
        P(),
        P(),
        P(),
    )
    return jax.shard_map(local, mesh=mesh, in_specs=in_specs, out_specs=out_specs, check_vma=False)
```

profile of v0, /device:TPU:10, one launch (start us, length us, event | category | flops | bytes accessed | tf_op | source)
XLA Modules:
  0.0 1963.5 jit_solution(3387813233018133657)
XLA Ops:
  14.3 213.7 %all-gather.6.cloned.1.call-done = bf16[2048,6144]{1,0:T(8,128)(2,1)} async-done(((bf16[256,6144]{1,0:T(8,128)(2,1)}), bf16[2048,6144]{1,0:T(8,128)(2,1)}) %all-gather.6.cloned.1.call-update) | async-done | bytes 25165840 | tf_op jit(solution)/shard_map/all_gather | solution.py:57
  228.0 23.2 %fusion.4 = f32[2,384,6144]{2,1,0:T(8,128)S(1)} fusion(bf16[2048,6144]{1,0:T(8,128)(2,1)} %all-gather.6.cloned.1.call-done, bf16[2,384,2048]{2,1,0:T(8,128)(2,1)S(1)} %copy-done.1, f32[2048]{0:T(1024)S(1)} %copy-done.46, f32[2048]{0:T(1024)S(1)} %copy-done.34, f32[2,384]{1,0:T(2,128)S(1)} %add_rsqrt_fusion, f32[2,384]{1,0:T(2,128)S(1)} %broadcast_multiply_fusion.2), kind=kOutput, calls=%fused_computation.9 | convolution fusion | flops 19336790016 | bytes 47208448 | tf_op jit(solution)/shard_map/dot_general | solution.py:55
  251.2 6.2 broadcast_select_fusion
  262.8 14.1 slice.530
  276.9 14.1 slice.529
  291.0 14.5 slice.565
  305.5 14.1 slice.609
  328.0 14.4 slice.605
  342.5 14.2 slice.570
  356.6 14.1 slice.569
  370.7 31.6 %slice.611 = f32[2,192,2048]{2,1,0:T(8,128)} reverse(f32[2,192,2048]{2,1,0:T(8,128)} %slice.529), dimensions={1} | reverse | bytes 6291456 | tf_op jit(solution)/shard_map/slice | solution.py:86
  402.2 31.6 %slice.617 = f32[2,192,2048]{2,1,0:T(8,128)} reverse(f32[2,192,2048]{2,1,0:T(8,128)} %slice.530), dimensions={1} | reverse | bytes 6291456 | tf_op jit(solution)/shard_map/slice | solution.py:86
  433.8 7.9 fusion.78
  444.1 7.8 slice.563
  451.8 7.6 slice.533
  459.4 7.6 slice.532
  468.5 7.7 slice.603
  476.3 7.6 slice.573
  483.9 7.6 slice.572
  663.4 6.2 pad.224
  672.4 6.3 pad.208
  684.8 6.3 pad.225
  699.0 10.7 add_multiply_fusion.3
  713.8 11.6 pad.226
  729.5 11.9 pad.210
  741.4 11.8 pad.211
  754.2 8.2 all-gather
  762.6 11.8 pad.227
  775.3 7.3 all-gather.1
  783.3 10.0 multiply_add_fusion.2
  793.4 11.7 fusion.70
  805.2 9.6 fusion.76
  817.5 14.1 slice.671
  831.6 12.1 slice.614
  843.7 14.1 slice.612
  857.9 31.5 %slice.613 = f32[2,192,2048]{2,1,0:T(8,128)} reverse(f32[2,192,2048]{2,1,0:T(8,128)} %slice.612), dimensions={1} | reverse | bytes 6291456 | tf_op jit(solution)/shard_map/slice | solution.py:86
  889.4 20.6 %slice.615 = f32[2,192,2048]{2,1,0:T(8,128)} reverse(f32[2,192,2048]{2,1,0:T(8,128)S(1)} %slice.614), dimensions={1} | reverse | bytes 6291456 | tf_op jit(solution)/shard_map/slice | solution.py:86
  918.2 7.8 slice.669
  926.0 7.6 slice.621
  933.5 7.6 slice.620
  1019.3 11.8 pad.467
  1031.1 11.9 pad.259
  1045.8 6.3 pad.240
  1052.1 6.2 pad.241
  1063.6 11.6 pad.469
  1075.2 11.8 pad.243
  1087.0 32.1 %slice.610 = f32[2,191,2048]{2,1,0:T(8,128)} reverse(f32[2,191,2048]{2,1,0:T(8,128)} %slice.609), dimensions={1} | reverse | bytes 6258688 | tf_op jit(solution)/shard_map/slice | solution.py:86
  1119.1 32.2 %slice.672 = f32[2,191,2048]{2,1,0:T(8,128)} reverse(f32[2,191,2048]{2,1,0:T(8,128)} %slice.671), dimensions={1} | reverse | bytes 6258688 | tf_op jit(solution)/shard_map/slice | solution.py:86
  1151.3 9.5 add_multiply_fusion
  1162.8 12.5 pad.242
  1177.3 11.8 pad.258
  1190.0 8.2 all-gather.2
  1198.4 9.2 slice_add_fusion
  1207.6 49.7 %slice.691 = f32[2,383,2048]{2,1,0:T(8,128)} reverse(f32[2,383,2048]{2,1,0:T(8,128)} %slice_add_fusion), dimensions={1} | reverse | bytes 12550144 | tf_op jit(solution)/shard_map/slice | solution.py:91
  1258.2 7.3 all-gather.3
  1265.9 9.2 slice_add_fusion.1
  1275.1 49.8 %slice.674 = f32[2,383,2048]{2,1,0:T(8,128)} reverse(f32[2,383,2048]{2,1,0:T(8,128)} %slice_add_fusion.1), dimensions={1} | reverse | bytes 12550144 | tf_op jit(solution)/shard_map/slice | solution.py:91
  1325.0 9.6 multiply_add_fusion
  1334.7 20.5 %fusion.74 = (bf16[2,384,2048]{2,1,0:T(8,128)(2,1)}, f32[2,384,2048]{2,1,0:T(8,128)}, bf16[2,384,2048]{2,1,0:T(8,128)(2,1)}, f32[2,384,2048]{2,1,0:T(8,128)}) fusion(f32[2,384,2048]{2,1,0:T(8,128)} %get-tuple-element.286, f32[2,384,6144]{2,1,0:T(8,128)} %copy-done.10, f32[2,383,2048]{2,1,0:T(8,128)S(1)} %bitcast.39, f32[2,1,2048]{2,1,0:T(1,128)S(1)} %copy-done.33, ...), kind=kLoop, calls=%fused_computation.187 | loop fusion | flops 44040192 | bytes 62937860 | tf_op jit(solution)/shard_map/convert.1
  1355.2 31.4 %convolution_bitcast_fusion = f32[2048,6144]{1,0:T(8,128)} fusion(bf16[2,384,2048]{2,1,0:T(8,128)(2,1)} %get-tuple-element.289, bf16[2,384,2048]{2,1,0:T(8,128)(2,1)} %get-tuple-element.275, bf16[2,384,2048]{2,1,0:T(8,128)(2,1)} %get-tuple-element.287, bf16[2,384,2048]{2,1,0:T(8,128)(2,1)} %param.14, f32[2048]{0:T(1024)S(1)} %copy-done.48, ...), kind=kOutput, calls=%fused_computation.6 | convolution fusion | flops 19365101568 | bytes 62937088 | tf_op jit(solution)/shard_map/dot_general | solution.py:123
  1386.7 481.3 %reduce-scatter.3.cloned.1.call-done = f32[256,6144]{1,0:T(8,128)} async-done(((f32[2048,6144]{1,0:T(8,128)}), f32[256,6144]{1,0:T(8,128)}) %reduce-scatter.3.cloned.1.call-update) | async-done | bytes 6291472 | tf_op jit(solution)/shard_map/reduce_scatter | solution.py:122
  1868.1 37.7 %fusion.71 = (f32[2048]{0:T(1024)S(1)}, f32[2048]{0:T(1024)S(1)}, f32[2048]{0:T(1024)S(1)}, f32[2,384]{1,0:T(2,128)S(1)}, f32[2,384]{1,0:T(2,128)S(1)}, /*index=5*/f32[2048]{0:T(1024)S(1)}, f32[2,384,2048]{2,1,0:T(8,128)}) fusion(f32[2,384,2048]{2,1,0:T(8,128)} %get-tuple-element.276, f32[2048]{0:T(1024)S(1)} %copy-done.48, f32[2048]{0:T(1024)S(1)} %copy-done.36, ...), kind=kOutput, calls=%fused_computation.186 | convolution fusion | flops 19391832064 | bytes 59839236 | tf_op jit(solution)/shard_map/dot_general | solution.py:102
  1905.8 44.1 %all-reduce.64 = (f32[2048]{0:T(1024)}, f32[2048]{0:T(1024)}, f32[2048]{0:T(1024)}, f32[2048]{0:T(1024)}, f32[2048]{0:T(1024)}, /*index=5*/f32[2048]{0:T(1024)}) all-reduce(f32[2048]{0:T(1024)S(1)} %get-tuple-element.242, f32[2048]{0:T(1024)S(1)} %copy-done.62, ...), channel_id=1, replica_groups=mesh['seq'=4,'dp'=8] {'seq','dp'}, use_global_device_ids=true, to_apply=%region_12.13 | all-reduce | flops 12288 | bytes 98304 | tf_op jit(solution)/shard_map/psum | solution.py:131
  1949.9 6.8 fusion.33
  (409 shorter events, 326.6 us)
Async XLA Ops:
  7.2 6.1 copy-start.1
  7.2 220.8 %copy-start.34 = (f32[2048]{0:T(1024)S(1)}, f32[2048]{0:T(1024)}, u32[]{:S(2)}) copy-start(f32[2048]{0:T(1024)} %param.21) | copy-start | bytes 24580
  7.2 220.8 %copy-start.46 = (f32[2048]{0:T(1024)S(1)}, f32[2048]{0:T(1024)}, u32[]{:S(2)}) copy-start(f32[2048]{0:T(1024)} %param.22) | copy-start | bytes 24580
  7.2 220.8 %all-gather.6.cloned.1.call-start = ((), (), s32[]{:S(2)}) async-start(), calls=%async_computation.2 | async-start | bytes 28311552 | tf_op jit(solution)/shard_map/all_gather | solution.py:57
  7.9 1860.0 %reduce-scatter.3.cloned.1.call-start = ((), (), s32[]{:S(2)}) async-start(), calls=%async_computation.3 | async-start | bytes 56623104 | tf_op jit(solution)/shard_map/reduce_scatter | solution.py:122
  10.9 308.7 %copy-start.43 = (pred[2,384]{1,0:T(4,128)(4,1)}, pred[2,384]{1,0:T(4,128)(4,1)S(1)}, u32[]{:S(2)}) copy-start(pred[2,384]{1,0:T(4,128)(4,1)S(1)} %broadcast_compare_fusion) | copy-start | bytes 2308
  13.3 237.9 %copy-start.37 = (f32[2,384]{1,0:T(2,128)}, f32[2,384]{1,0:T(2,128)S(1)}, u32[]{:S(2)}) copy-start(f32[2,384]{1,0:T(2,128)S(1)} %broadcast_multiply_fusion.2) | copy-start | bytes 9220
  14.3 236.9 %copy-start.40 = (f32[2,384]{1,0:T(2,128)}, f32[2,384]{1,0:T(2,128)S(1)}, u32[]{:S(2)}) copy-start(f32[2,384]{1,0:T(2,128)S(1)} %add_rsqrt_fusion) | copy-start | bytes 9220
  14.3 236.9 %copy-start.63 = (f32[2048]{0:T(1024)S(1)}, f32[2048]{0:T(1024)}, u32[]{:S(2)}) copy-start(f32[2048]{0:T(1024)} %param.19) | copy-start | bytes 24580
  14.3 236.9 %copy-start.64 = (f32[2048]{0:T(1024)S(1)}, f32[2048]{0:T(1024)}, u32[]{:S(2)}) copy-start(f32[2048]{0:T(1024)} %param.17) | copy-start | bytes 24580
  251.2 8.2 copy-start.10
  259.4 2.7 copy-start.4
  324.7 2.7 copy-start.9
  624.4 11.2 copy-start.56
  629.6 10.4 copy-start.54
  652.3 7.6 copy-start.16
  652.3 7.6 copy-start.17
  652.3 7.6 copy-start.18
  652.3 7.6 copy-start.20
  652.3 7.6 copy-start.24
  652.3 7.6 copy-start.26
  662.1 7.5 copy-start.51
  691.1 5.4 copy-start.12
  691.1 5.4 copy-start.13
  699.0 10.7 copy-start.49
  713.8 11.6 copy-start.59
  783.2 10.1 copy-start.6
  783.2 10.1 copy-start.35
  783.2 10.1 copy-start.38
  783.2 10.1 copy-start.41
  783.2 10.1 copy-start.44
  783.2 10.1 copy-start.47
  783.2 10.1 copy-start.60
  783.3 10.1 copy-start.66
  783.3 21.9 %slice-start.2 = ((s8[6291456]{0:T(1024)(128)(4,1)}), s8[4194304]{0:T(1024)(128)(4,1)S(1)}, s32[]{:S(2)}) async-start(s8[6291456]{0:T(1024)(128)(4,1)} %bitcast.40), calls=%async_computation.7 | async-start | bytes 8388608
  793.3 11.9 copy-start
  793.3 11.8 copy-start.32
  793.4 11.8 slice-start.3
  805.1 9.7 copy-start.5
  982.1 4.6 copy-start.57
  983.0 4.0 copy-start.55
  997.3 5.7 copy-start.19
  997.3 5.7 copy-start.21
  997.3 5.7 copy-start.25
  997.3 5.7 copy-start.27
  1031.1 11.9 copy-start.50
  1162.8 12.6 copy-start.22
  1162.8 12.6 copy-start.58
  1207.6 58.1 %copy-start.31 = (f32[2,2048]{1,0:T(2,128)S(1)}, f32[2,2048]{1,0:T(2,128)}, u32[]{:S(2)}) copy-start(f32[2,2048]{1,0:T(2,128)} %custom-call.1) | copy-start | bytes 49156
  1275.1 59.5 %slice-start = ((s8[6291456]{0:T(1024)(128)(4,1)}), s8[2097152]{0:T(1024)(128)(4,1)S(1)}, s32[]{:S(2)}) async-start(s8[6291456]{0:T(1024)(128)(4,1)} %bitcast.37), calls=%async_computation.5 | async-start | bytes 4194304
  1324.9 9.7 slice-start.1
  1324.9 9.7 copy-start.2
  1324.9 9.7 copy-start.7
  1325.0 9.7 copy-start.33
  1325.0 9.7 copy-start.36
  1325.0 9.7 copy-start.39
  1325.0 9.7 copy-start.42
  1325.0 9.7 copy-start.45
  1325.0 9.7 copy-start.48
  1386.6 481.4 %copy-start.3 = (bf16[2,384,2048]{2,1,0:T(8,128)(2,1)S(1)}, bf16[2,384,2048]{2,1,0:T(8,128)(2,1)}, u32[]{:S(2)}) copy-start(bf16[2,384,2048]{2,1,0:T(8,128)(2,1)} %param.14) | copy-start | bytes 9437188
  1386.6 481.4 %copy-start.65 = (f32[2048]{0:T(1024)S(1)}, f32[2048]{0:T(1024)}, u32[]{:S(2)}) copy-start(f32[2048]{0:T(1024)} %param.17) | copy-start | bytes 24580
  1386.6 570.1 %reduce-scatter.5.cloned.1.call-start = ((), (), s32[]{:S(2)}) async-start(), calls=%async_computation.4 | async-start | bytes 7864320 | tf_op jit(solution)/shard_map/reduce_scatter | solution.py:130
  1868.0 37.7 %copy-start.61 = (f32[2048]{0:T(1024)S(1)}, f32[2048]{0:T(1024)}, u32[]{:S(2)}) copy-start(f32[2048]{0:T(1024)} %get-tuple-element.239) | copy-start | bytes 24580
  1868.0 37.7 %copy-start.62 = (f32[2048]{0:T(1024)S(1)}, f32[2048]{0:T(1024)}, u32[]{:S(2)}) copy-start(f32[2048]{0:T(1024)} %get-tuple-element.240) | copy-start | bytes 24580
  (10 other events, 16.3 us)
Sparse Core Ops, SparseCore 0:
  9.7 218.2 all-gather.5
  1386.7 481.2 reduce-scatter.2
  1871.8 71.6 reduce-scatter.4
where the time goes:
time: 2000 us; the launch traced here: 1960 us
  local copies, waits for them, and re-layouts  825 us (41%)
  waiting for transfers between devices  696 us (35%)
  other arithmetic  259 us (13%)
  matrix products  92.2 us (5%)
  blocking collectives  75.1 us (4%)
    reduce_scatter x1, waiting for transfers between devices, local(): lax.psum_scatter(lax.dot_general(columns, proj_grad, (((0,), (0,)), ((),...  481 us
    slice x60, local copies, waits for them, and re-layouts, local(): lax.associative_scan(combine, (decay, source), reverse=True, axis=1)  288 us
    all_gather x1, waiting for transfers between devices, local(): lax.all_gather(weight, 'dp', axis=0, tiled=True)  214 us
    slice x55, local copies, waits for them, and re-layouts, local(): prod_fwd, local_fwd = lax.associative_scan(combine, (decay, inject), axis=1)  202 us
    pad x30, local copies, waits for them, and re-layouts, local(): prod_fwd, local_fwd = lax.associative_scan(combine, (decay, inject), axis=1)  113 us
    pad x30, local copies, waits for them, and re-layouts, local(): lax.associative_scan(combine, (decay, source), reverse=True, axis=1)  79.5 us
    mul x16, other arithmetic, combine(): return (earlier[0] * later[0], later[0] * earlier[1] + later[1])  52.5 us
    slice x1, local copies, waits for them, and re-layouts, local(): local_back[:, 1:] + prod_back[:, 1:] * after_in[:, None]  49.8 us
  transfers between devices with their start and end apart: 3, of which 2 were waited for; matrix products, arithmetic and copies ran while one was open for 3% of the time, Pallas kernels for 0%

commit v1 on v0

v1 whole, which is shorter than its diff:
```python
import functools

import jax
import jax.numpy as jnp
from jax import lax
from jax.experimental import pallas as pl
from jax.experimental.pallas import tpu as pltpu
from jax.sharding import PartitionSpec as P

EPS = 1e-05
F32 = jnp.float32
BF = jnp.bfloat16
STEPS = 16
BLK = 128
GATES = 3
QUARTERS = 4


def params(mib, dims=1):
    return pltpu.CompilerParams(
        vmem_limit_bytes=mib * 1024 * 1024, dimension_semantics=("arbitrary",) * dims
    )


def cost(flops, bytes_accessed, transcendentals=0):
    return pl.CostEstimate(
        flops=int(flops), bytes_accessed=int(bytes_accessed), transcendentals=int(transcendentals)
    )


def sds(shape, dtype):
    return jax.ShapeDtypeStruct(shape, dtype)


def sigmoid(v):
    return jax.nn.sigmoid(v)


def split_kernel(ids, w, mine, theirs):
    c = ids[2]
    for s in range(4):
        a, mp = divmod(s, 2)
        for g in range(GATES):
            for mm in range(2):
                dst = s * 768 + g * 256 + mm * BLK
                base = g * 2048 + (2 * mp + mm) * 512 + a * BLK
                here = pl.multiple_of(base + c * 256, BLK)
                there = pl.multiple_of(base + (1 - c) * 256, BLK)
                mine[:, dst : dst + BLK] = w[:, pl.ds(here, BLK)]
                theirs[:, dst : dst + BLK] = w[:, pl.ds(there, BLK)]


def split_weight(ids, weight):
    rows, cols = weight.shape
    tile = rows // 2
    out = sds((rows, cols // 2), BF)
    spec = pl.BlockSpec((tile, cols // 2), lambda i, ids: (i, 0))
    return pl.pallas_call(
        split_kernel,
        grid_spec=pltpu.PrefetchScalarGridSpec(
            num_scalar_prefetch=1,
            grid=(2,),
            in_specs=[pl.BlockSpec((tile, cols), lambda i, ids: (i, 0))],
            out_specs=[spec, spec],
        ),
        out_shape=[out, out],
        compiler_params=params(24),
        cost_estimate=cost(0, rows * cols * 4),
        name="split_weight",
    )(ids, weight)


def norm_of(x):
    mean = jnp.mean(x, axis=-1, keepdims=True)
    centered = x - mean
    var = jnp.mean(centered * centered, axis=-1, keepdims=True)
    rstd = lax.rsqrt(var + EPS)
    return centered * rstd, rstd


def norm_kernel(ids, own, other, gain, bias, ub, ubt, u32, scr):
    c = ids[2]
    seqs, parts = own.shape[0], own.shape[1]
    for k, ref in enumerate((own, other)):
        for s in range(seqs):
            for h in range(parts):
                x = ref[s, h].astype(F32)
                normed, _ = norm_of(x)
                stream = (k * seqs + s) * parts + h
                unit = normed * gain[...] + bias[...]
                for j in range(scr.shape[0]):
                    scr[j, pl.ds(stream, STEPS, stride=16), :] = unit[:, j * BLK : (j + 1) * BLK]
    for j in range(scr.shape[0]):
        low = scr[j].astype(BF)
        ub[:, j * BLK : (j + 1) * BLK] = low
        ubt[j * BLK : (j + 1) * BLK, :] = low.T
    for a in range(2):
        for m in range(QUARTERS):
            dst = (a * QUARTERS + m) * BLK
            u32[:, dst : dst + BLK] = scr[m * 4 + a + 2 * c]


def norm_tokens(ids, own, other, gain, bias):
    seqs, parts, steps, width = own.shape
    rows = 2 * seqs * parts * steps
    tiles = steps // STEPS
    nat = pl.BlockSpec((seqs, parts, STEPS, width), lambda i, ids: (0, 0, i, 0))
    vec = pl.BlockSpec((1, width), lambda i, ids: (0, 0))
    return pl.pallas_call(
        norm_kernel,
        grid_spec=pltpu.PrefetchScalarGridSpec(
            num_scalar_prefetch=1,
            grid=(tiles,),
            in_specs=[nat, nat, vec, vec],
            out_specs=[
                pl.BlockSpec((256, width), lambda i, ids: (i, 0)),
                pl.BlockSpec((width, 256), lambda i, ids: (0, i)),
                pl.BlockSpec((256, width // 2), lambda i, ids: (i, 0)),
            ],
            scratch_shapes=[pltpu.VMEM((width // BLK, 256, BLK), F32)],
        ),
        out_shape=[
            sds((rows, width), BF),
            sds((width, rows), BF),
            sds((rows, width // 2), F32),
        ],
        compiler_params=params(32),
        cost_estimate=cost(rows * width * 10, rows * width * 10),
        name="norm_tokens",
    )(ids, own, other, gain, bias)


def live_rows(lim, tile):
    step = lax.broadcasted_iota(jnp.int32, lim.shape, 0) // 16 + tile * STEPS
    live = step < lim[...]
    return jnp.concatenate([live, live], axis=1)


def proj_kernel(
    s, nz, ids, ub, u32, mine, recv, rel, gx, gy, dx, dy, lim, vf, bfor,
    cand, decay, rpre, wout, plout, summ, prod, loc, sems,
):
    i = pl.program_id(0)
    tiles = pl.num_programs(0)
    width = wout.shape[0]
    zb = width // nz
    zb2, qb = zb // 2, zb // 4

    @pl.when(i == 0)
    def _():
        q, z, c = ids[0], ids[1], ids[2]
        copies = []

        def put(src, row, lo=0, hi=768):
            dst = wout.at[pl.ds(pl.multiple_of(row, qb), src.shape[0]), lo:hi]
            copy = pltpu.make_async_copy(src, dst, sems.at[len(copies)])
            copy.start()
            copies.append(copy)

        put(mine.at[:, s * 768 : (s + 1) * 768], z * zb + c * zb2)
        put(recv.at[:, s * 768 : (s + 1) * 768], z * zb + (1 - c) * zb2)
        for r in range(1, nz):
            base = lax.rem(z + r, nz) * zb
            lo, hi = (r - 1) * qb, r * qb
            put(rel.at[lo:hi, :], base + q * qb)
            put(gx.at[lo:hi, :], base + (q ^ 1) * qb)
            put(gy.at[lo:hi, :], base + (q ^ 2) * qb)
            put(dx.at[lo:hi, :], base + (q ^ 3) * qb, 0, 384)
            put(dy.at[lo:hi, :], base + (q ^ 3) * qb, 384, 768)
        for copy in copies:
            copy.wait()
        prod[...] = jnp.ones_like(prod)
        loc[...] = jnp.zeros_like(loc)

    zz = jnp.dot(ub[...], wout[...], preferred_element_type=F32)
    cd = zz[:, :256]
    gate = sigmoid(zz[:, 256:512] + vf[...] * u32[...] + bfor[...])
    dec = jnp.where(live_rows(lim, i), gate, 1.0)
    cand[...] = cd
    decay[...] = dec
    rpre[...] = zz[:, 512:]
    inj = (1.0 - dec) * cd
    pr, lc = prod[...], loc[...]
    for t in range(STEPS):
        d = dec[t * 16 : (t + 1) * 16]
        lc = d * lc + inj[t * 16 : (t + 1) * 16]
        pr = d * pr
    prod[...] = pr
    loc[...] = lc

    @pl.when(i == tiles - 1)
    def _():
        plout[0:16, :] = pr
        plout[16:32, :] = lc
        parts = 4
        for ks in range(4):
            tp = pr[ks * parts : ks * parts + 1]
            tl = lc[ks * parts : ks * parts + 1]
            for h in range(1, parts):
                n = ks * parts + h
                tl = pr[n : n + 1] * tl + lc[n : n + 1]
                tp = pr[n : n + 1] * tp
            summ[ks : ks + 1, :] = tp
            summ[4 + ks : 5 + ks, :] = tl


def project(s, nz, ids, ub, u32, mine, recv, pieces, lim, vf, bfor):
    rows, width = ub.shape
    tiles = rows // 256
    rel, gx, gy, dx, dy = pieces
    anyspec = pl.BlockSpec(memory_space=pl.ANY)
    rowblk = pl.BlockSpec((256, 256), lambda i, ids: (i, 0))
    chan = pl.BlockSpec((1, 256), lambda i, ids: (0, s))
    return pl.pallas_call(
        functools.partial(proj_kernel, s, nz),
        grid_spec=pltpu.PrefetchScalarGridSpec(
            num_scalar_prefetch=1,
            grid=(tiles,),
            in_specs=[
                pl.BlockSpec((256, width), lambda i, ids: (i, 0)),
                pl.BlockSpec((256, 256), lambda i, ids: (i, s)),
            ]
            + [anyspec] * 7
            + [pl.BlockSpec((256, 128), lambda i, ids: (0, 0)), chan, chan],
            out_specs=[
                rowblk,
                rowblk,
                rowblk,
                pl.BlockSpec((width, 768), lambda i, ids: (0, 0)),
                pl.BlockSpec((32, 256), lambda i, ids: (0, 0)),
                pl.BlockSpec((8, 256), lambda i, ids: (0, 0)),
            ],
            scratch_shapes=[
                pltpu.VMEM((16, 256), F32),
                pltpu.VMEM((16, 256), F32),
                pltpu.SemaphoreType.DMA((2 + 5 * (nz - 1),)),
            ],
        ),
        out_shape=[
            sds((rows, 256), F32),
            sds((rows, 256), F32),
            sds((rows, 256), F32),
            sds((width, 768), BF),
            sds((32, 256), F32),
            sds((8, 256), F32),
        ],
        compiler_params=params(32),
        cost_estimate=cost(2 * rows * width * 768, rows * width * 2 + width * 768 * 4 + rows * 4096),
        name=f"project_{s}",
    )(ids, ub, u32, mine, recv, rel, gx, gy, dx, dy, lim, vf, bfor)


def state_kernel(
    s, first, n_in, ids, cand, decay, rpre, u32, own0, own1, oth0, oth1, lim, scl, vr, br, plin,
    *rest,
):
    carries = rest[:n_in]
    rest = rest[n_in:]
    if not first:
        rest = rest[2:]
    (hown, hoth, dstate, src, bc, du0, dz3, lbs, summ, acc, st, pp, lb, ac, scr) = rest
    i = pl.program_id(0)
    tiles = pl.num_programs(0)
    parts = 4

    @pl.when(i == 0)
    def _():
        carry = carries[-1][4:8, :]
        for ref in carries[-2::-1]:
            carry = ref[4:8, :] + ref[0:4, :] * carry
        for ks in range(4):
            cc = carry[ks : ks + 1]
            for h in range(parts):
                n = ks * parts + h
                st[n : n + 1, :] = cc
                cc = plin[n : n + 1, :] * cc + plin[16 + n : 17 + n, :]
        pp[...] = jnp.ones_like(pp)
        lb[...] = jnp.zeros_like(lb)
        ac[...] = jnp.zeros_like(ac)

    for k, halves in enumerate(((own0, own1), (oth0, oth1))):
        for b, ref in enumerate(halves):
            for sq in range(ref.shape[0]):
                for h in range(parts):
                    stream = (k * ref.shape[0] + sq) * parts + h
                    scr[b, pl.ds(stream, STEPS, stride=16), :] = ref[sq, h].astype(F32)
    live = live_rows(lim, i)
    sc = scl[...]
    gy = jnp.where(live, jnp.concatenate([scr[0] * sc, scr[1] * sc], axis=1), 0.0)
    dec = decay[...]
    cd = cand[...]
    inj = (1.0 - dec) * cd
    cur = st[...]
    befores, states = [], []
    for t in range(STEPS):
        befores.append(cur)
        cur = dec[t * 16 : (t + 1) * 16] * cur + inj[t * 16 : (t + 1) * 16]
        states.append(cur)
    st[...] = cur
    before = jnp.concatenate(befores, axis=0)
    state = jnp.concatenate(states, axis=0)
    u = u32[...]
    r = sigmoid(rpre[...] + vr[...] * before + br[...])
    hv = jnp.where(live, r * state + (1.0 - r) * u, 0.0)
    for t in range(STEPS):
        for b in range(2):
            part = hv[t * 16 : (t + 1) * 16, b * BLK : (b + 1) * BLK]
            hown[0, b, t * 8 : (t + 1) * 8, :] = part[:8]
            hoth[0, b, t * 8 : (t + 1) * 8, :] = part[8:]
    ds = gy * r
    dx = gy - ds
    drl = dx * r * (state - u)
    sr = dec * ds + vr[...] * drl
    dstate[...] = ds
    src[...] = sr
    bc[...] = before - cd
    du0[...] = dx
    dz3[...] = drl.astype(BF)
    p, l = pp[...], lb[...]
    for t in range(STEPS):
        l = l + p * sr[t * 16 : (t + 1) * 16]
        p = p * dec[t * 16 : (t + 1) * 16]
    pp[...] = p
    lb[...] = l
    ac[0:8, :] += jnp.sum((drl * before).reshape(32, 8, 256), axis=0)
    ac[8:16, :] += jnp.sum(drl.reshape(32, 8, 256), axis=0)

    @pl.when(i == tiles - 1)
    def _():
        acc[...] = ac[...]
        lbs[...] = l
        for ks in range(4):
            n = ks * parts + parts - 1
            tl, tp = l[n : n + 1], p[n : n + 1]
            for h in range(parts - 2, -1, -1):
                n = ks * parts + h
                tl = l[n : n + 1] + p[n : n + 1] * tl
                tp = p[n : n + 1] * tp
            summ[ks : ks + 1, :] = tp
            summ[4 + ks : 5 + ks, :] = tl


def states(s, ids, cand, decay, rpre, u32, cot_own, cot_oth, lim, scl, vr, br, plin, carries, held):
    rows = cand.shape[0]
    tiles = rows // 256
    a, mp = divmod(s, 2)
    seqs, parts = cot_own.shape[0], cot_own.shape[1]
    first = held is None
    rowblk = pl.BlockSpec((256, 256), lambda i, ids: (i, 0))
    fix = lambda shape: pl.BlockSpec(shape, lambda i, ids: (0,) * len(shape))
    chan = pl.BlockSpec((1, 256), lambda i, ids: (0, s))

    def nat_own(m):
        return pl.BlockSpec(
            (seqs, parts, STEPS, BLK), lambda i, ids: (0, 0, i, m * 4 + 2 * ids[2] + a)
        )

    def nat_oth(m):
        return pl.BlockSpec((seqs, parts, STEPS, BLK), lambda i, ids: (0, 0, i, m * 2 + a))

    hspec = pl.BlockSpec((1, 2, 128, BLK), lambda i, ids: (s, 0, i, 0))
    in_specs = (
        [rowblk, rowblk, rowblk, pl.BlockSpec((256, 256), lambda i, ids: (i, s))]
        + [nat_own(2 * mp), nat_own(2 * mp + 1), nat_oth(2 * mp), nat_oth(2 * mp + 1)]
        + [fix((256, 128)), fix((256, 128)), chan, chan, fix((32, 256))]
        + [fix((8, 256))] * len(carries)
    )
    args = [ids, cand, decay, rpre, u32, cot_own, cot_own, cot_oth, cot_oth, lim, scl, vr, br, plin]
    args += list(carries)
    aliases = {}
    if not first:
        in_specs = in_specs + [pl.BlockSpec(memory_space=pl.ANY)] * 2
        aliases = {len(args): 0, len(args) + 1: 1}
        args += list(held)
    return pl.pallas_call(
        functools.partial(state_kernel, s, first, len(carries)),
        grid_spec=pltpu.PrefetchScalarGridSpec(
            num_scalar_prefetch=1,
            grid=(tiles,),
            in_specs=in_specs,
            out_specs=[
                hspec,
                hspec,
                rowblk,
                rowblk,
                rowblk,
                rowblk,
                rowblk,
                fix((16, 256)),
                fix((8, 256)),
                fix((16, 256)),
            ],
            scratch_shapes=[pltpu.VMEM((16, 256), F32)] * 4 + [pltpu.VMEM((2, 256, BLK), F32)],
        ),
        out_shape=[
            sds((4, 2, rows // 2, BLK), F32),
            sds((4, 2, rows // 2, BLK), F32),
            sds((rows, 256), F32),
            sds((rows, 256), F32),
            sds((rows, 256), F32),
            sds((rows, 256), F32),
            sds((rows, 256), BF),
            sds((16, 256), F32),
            sds((8, 256), F32),
            sds((16, 256), F32),
        ],
        input_output_aliases=aliases,
        compiler_params=params(32),
        cost_estimate=cost(rows * 256 * 60, rows * 256 * 40, rows * 256 * 2),
        name=f"states_{s}",
    )(*args)


def adjoint_kernel(n_in, ids, decay, bc, dstate, src, du0, u32, vf, plin, lbs, *rest):
    carries = rest[:n_in]
    dz12, du, acc, adj, ac = rest[n_in:]
    i = pl.program_id(0)
    tiles = pl.num_programs(0)
    parts = 4

    @pl.when(i == 0)
    def _():
        after = carries[-1][4:8, :]
        for ref in carries[-2::-1]:
            after = ref[4:8, :] + ref[0:4, :] * after
        for ks in range(4):
            cc = after[ks : ks + 1]
            for h in range(parts - 1, -1, -1):
                n = ks * parts + h
                adj[n : n + 1, :] = cc
                cc = lbs[n : n + 1, :] + plin[n : n + 1, :] * cc
        ac[...] = jnp.zeros_like(ac)

    dec = decay[...]
    ds = dstate[...]
    sr = src[...]
    cur = adj[...]
    totals = [None] * STEPS
    for t in range(STEPS - 1, -1, -1):
        totals[t] = ds[t * 16 : (t + 1) * 16] + cur
        cur = dec[t * 16 : (t + 1) * 16] * cur + sr[t * 16 : (t + 1) * 16]
    adj[...] = cur
    total = jnp.concatenate(totals, axis=0)
    dcand = total * (1.0 - dec)
    dfl = dcand * bc[...] * dec
    dz12[:, :256] = dcand.astype(BF)
    dz12[:, 256:] = dfl.astype(BF)
    du[...] = du0[...] + dfl * vf[...]
    ac[0:8, :] += jnp.sum((dfl * u32[...]).reshape(32, 8, 256), axis=0)
    ac[8:16, :] += jnp.sum(dfl.reshape(32, 8, 256), axis=0)

    @pl.when(i == tiles - 1)
    def _():
        acc[...] = ac[...]


def adjoints(s, ids, decay, bc, dstate, src, du0, u32, vf, plin, lbs, carries):
    rows = decay.shape[0]
    tiles = rows // 256
    last = tiles - 1
    rowblk = pl.BlockSpec((256, 256), lambda i, ids: (last - i, 0))
    fix = lambda shape: pl.BlockSpec(shape, lambda i, ids: (0,) * len(shape))
    return pl.pallas_call(
        functools.partial(adjoint_kernel, len(carries)),
        grid_spec=pltpu.PrefetchScalarGridSpec(
            num_scalar_prefetch=1,
            grid=(tiles,),
            in_specs=[rowblk] * 5
            + [
                pl.BlockSpec((256, 256), lambda i, ids: (last - i, s)),
                pl.BlockSpec((1, 256), lambda i, ids: (0, s)),
                fix((32, 256)),
                fix((16, 256)),
            ]
            + [fix((8, 256))] * len(carries),
            out_specs=[
                pl.BlockSpec((256, 512), lambda i, ids: (last - i, 0)),
                rowblk,
                fix((16, 256)),
            ],
            scratch_shapes=[pltpu.VMEM((16, 256), F32)] * 2,
        ),
        out_shape=[sds((rows, 512), BF), sds((rows, 256), F32), sds((16, 256), F32)],
        compiler_params=params(32),
        cost_estimate=cost(rows * 256 * 20, rows * 256 * 32),
        name=f"adjoints_{s}",
    )(ids, decay, bc, dstate, src, du0, u32, vf, plin, lbs, *carries)


def wgrad_kernel(ids, ubt, za0, zb0, za1, zb1, out):
    q = ids[0]
    lhs = ubt[...]
    for mp, (za, zb) in enumerate(((za0, zb0), (za1, zb1))):
        left = jnp.dot(lhs, za[...], preferred_element_type=F32)
        right = jnp.dot(lhs, zb[...], preferred_element_type=F32)
        for g in range(GATES):
            for mm in range(2):
                n = g * QUARTERS + 2 * mp + mm
                val = left[:, g * 256 + mm * BLK : g * 256 + (mm + 1) * BLK] if g < 2 else right[
                    :, mm * BLK : (mm + 1) * BLK
                ]
                out[(n // 3) ^ q, n % 3] = val.astype(BF)


def weight_grad_part(flip, nz, ids, ubt, za0, zb0, za1, zb1):
    width, rows = ubt.shape
    half = width // nz // 2
    full = lambda v: pl.BlockSpec(v.shape, lambda i, ids: (0, 0))

    def pick(i, ids):
        rh = 1 - ids[2] if flip else ids[2]
        return (2 * i + rh, 0)

    return pl.pallas_call(
        wgrad_kernel,
        grid_spec=pltpu.PrefetchScalarGridSpec(
            num_scalar_prefetch=1,
            grid=(nz,),
            in_specs=[pl.BlockSpec((half, rows), pick), full(za0), full(zb0), full(za1), full(zb1)],
            out_specs=pl.BlockSpec((4, 3, half, BLK), lambda i, ids: (0, 0, i, 0)),
        ),
        out_shape=sds((4, 3, nz * half, BLK), BF),
        compiler_params=params(32),
        cost_estimate=cost(2 * rows * width // 2 * 1536, rows * width + rows * 3072 + width * 1536),
        name="weight_grad_part",
    )(ids, ubt, za0, zb0, za1, zb1)


def unit_grad_kernel(first, ids, za0, zb0, za1, zb1, w0, w1, *rest):
    dims = (((1,), (1,)), ((), ()))
    if first:
        own, oth = rest
    else:
        pown, poth, e0, e1, e2, e3, own, oth, scr = rest
    total = None
    for za, zb, w in ((za0, zb0, w0), (za1, zb1, w1)):
        part = lax.dot_general(za[...], w[:, :512], dims, preferred_element_type=F32)
        total = part if total is None else total + part
        total = total + lax.dot_general(zb[...], w[:, 512:], dims, preferred_element_type=F32)
    if first:
        for t in range(STEPS):
            own[t * 8 : (t + 1) * 8, :] = total[t * 16 : t * 16 + 8]
            oth[t * 8 : (t + 1) * 8, :] = total[t * 16 + 8 : t * 16 + 16]
        return
    scr[...] = total
    c = ids[2]
    for s, ref in enumerate((e0, e1, e2, e3)):
        a, mp = divmod(s, 2)
        for mm in range(2):
            lane = pl.multiple_of((2 * mp + mm) * 512 + a * BLK + c * 256, BLK)
            scr[:, pl.ds(lane, BLK)] += ref[:, mm * BLK : (mm + 1) * BLK]
    for t in range(STEPS):
        own[t * 8 : (t + 1) * 8, :] = scr[t * 16 : t * 16 + 8] + pown[t * 8 : (t + 1) * 8, :]
        oth[t * 8 : (t + 1) * 8, :] = scr[t * 16 + 8 : t * 16 + 16] + poth[t * 8 : (t + 1) * 8, :]


def unit_grads(ids, dz, ws, partial, elem):
    rows = dz[0][0].shape[0]
    width = ws[0].shape[0]
    tiles = rows // 256
    first = partial is None
    blk = lambda n: pl.BlockSpec((256, n), lambda i, ids: (i, 0))
    wspec = pl.BlockSpec((width, 768), lambda i, ids: (0, 0))
    out = pl.BlockSpec((128, width), lambda i, ids: (i, 0))
    in_specs = [blk(512), blk(256), blk(512), blk(256), wspec, wspec]
    args = [ids, dz[0][0], dz[0][1], dz[1][0], dz[1][1], ws[0], ws[1]]
    scratch = []
    if not first:
        in_specs += [out, out] + [blk(256)] * 4
        args += list(partial) + list(elem)
        scratch = [pltpu.VMEM((256, width), F32)]
    return pl.pallas_call(
        functools.partial(unit_grad_kernel, first),
        grid_spec=pltpu.PrefetchScalarGridSpec(
            num_scalar_prefetch=1,
            grid=(tiles,),
            in_specs=in_specs,
            out_specs=[out, out],
            scratch_shapes=scratch,
        ),
        out_shape=[sds((rows // 2, width), F32)] * 2,
        compiler_params=params(40),
        cost_estimate=cost(2 * rows * width * 1536, rows * 3072 + width * 3072 + rows * width * 8),
        name="unit_grads",
    )(*args)


def activation_kernel(ids, tok, hown, hrcv, out):
    c = ids[2]
    for s in range(4):
        a, mp = divmod(s, 2)
        for mm in range(2):
            base = (2 * mp + mm) * 512 + a * BLK
            for ref, core in ((hown, c), (hrcv, 1 - c)):
                lane = pl.ds(pl.multiple_of(base + core * 256, BLK), BLK)
                for st in range(8):
                    sq, h = divmod(st, 4)
                    val = ref[s, mm, pl.ds(st, STEPS, stride=8), :]
                    out[sq, h, :, lane] = tok[sq, h, :, lane].astype(F32) + val


def activations_of(ids, tok, hown, hrcv):
    seqs, parts, steps, width = tok.shape
    tiles = steps // STEPS
    nat = pl.BlockSpec((seqs, parts, STEPS, width), lambda i, ids: (0, 0, i, 0))
    hspec = pl.BlockSpec((4, 2, 128, BLK), lambda i, ids: (0, 0, i, 0))
    return pl.pallas_call(
        activation_kernel,
        grid_spec=pltpu.PrefetchScalarGridSpec(
            num_scalar_prefetch=1, grid=(tiles,), in_specs=[nat, hspec, hspec], out_specs=nat
        ),
        out_shape=sds(tok.shape, F32),
        compiler_params=params(24),
        cost_estimate=cost(seqs * parts * steps * width, seqs * parts * steps * width * 10),
        name="activations_of",
    )(ids, tok, hown, hrcv)


def input_grad_kernel(ids, duo, dur, tok, cot, lim, scl, gain, *rest):
    accs = rest[:8]
    out, sums, ga, ba, scr = rest[8:]
    i = pl.program_id(0)
    tiles = pl.num_programs(0)

    @pl.when(i == 0)
    def _():
        ga[...] = jnp.zeros_like(ga)
        ba[...] = jnp.zeros_like(ba)

    for j in range(scr.shape[0]):
        scr[j] = duo[:, j * BLK : (j + 1) * BLK] + dur[:, j * BLK : (j + 1) * BLK]
    step = lax.broadcasted_iota(jnp.int32, (STEPS, 1), 0) + i * STEPS
    for st in range(8):
        sq, h = divmod(st, 4)
        du = jnp.concatenate(
            [scr[j, pl.ds(st, STEPS, stride=8), :] for j in range(scr.shape[0])], axis=1
        )
        normed, rstd = norm_of(tok[sq, h].astype(F32))
        dn = du * gain[...]
        gn = du * normed
        m1 = jnp.mean(dn, axis=-1, keepdims=True)
        m2 = jnp.mean(dn * normed, axis=-1, keepdims=True)
        gy = jnp.where(step < lim[st], cot[sq, h].astype(F32) * scl[0], 0.0)
        out[sq, h] = rstd * (dn - m1 - normed * m2) + gy
        ga[...] += gn[0:8] + gn[8:16]
        ba[...] += du[0:8] + du[8:16]

    @pl.when(i == tiles - 1)
    def _():
        sums[...] = jnp.zeros_like(sums)
        sums[4:5, :] = jnp.sum(ga[...], axis=0, keepdims=True)
        sums[5:6, :] = jnp.sum(ba[...], axis=0, keepdims=True)
        c = ids[2]
        for s in range(4):
            a, mp = divmod(s, 2)
            accb, accc = accs[s], accs[4 + s]
            rows = (accc[0:8, :], accb[0:8, :], accc[8:16, :], accb[8:16, :])
            for j, val in enumerate(rows):
                val = jnp.sum(val, axis=0, keepdims=True)
                for mm in range(2):
                    lane = pl.multiple_of((2 * mp + mm) * 512 + a * BLK + c * 256, BLK)
                    sums[j : j + 1, pl.ds(lane, BLK)] = val[:, mm * BLK : (mm + 1) * BLK]


def input_grads(ids, duo, dur, tok, cot, lim8, scale, gain, accb, accc):
    seqs, parts, steps, width = tok.shape
    tiles = steps // STEPS
    nat = pl.BlockSpec((seqs, parts, STEPS, width), lambda i, ids: (0, 0, i, 0))
    fix = lambda shape: pl.BlockSpec(shape, lambda i, ids: (0,) * len(shape))
    smem = pl.BlockSpec(memory_space=pltpu.SMEM)
    dub = pl.BlockSpec((128, width), lambda i, ids: (i, 0))
    n = seqs * parts * steps * width
    return pl.pallas_call(
        input_grad_kernel,
        grid_spec=pltpu.PrefetchScalarGridSpec(
            num_scalar_prefetch=1,
            grid=(tiles,),
            in_specs=[dub, dub, nat, nat, smem, smem, fix((1, width))] + [fix((16, 256))] * 8,
            out_specs=[nat, fix((8, width))],
            scratch_shapes=[
                pltpu.VMEM((8, width), F32),
                pltpu.VMEM((8, width), F32),
                pltpu.VMEM((width // BLK, 128, BLK), F32),
            ],
        ),
        out_shape=[sds(tok.shape, F32), sds((8, width), F32)],
        compiler_params=params(32),
        cost_estimate=cost(n * 20, n * 16),
        name="input_grads",
    )(ids, duo, dur, tok, cot, lim8, scale, gain, *accb, *accc)


def assemble_kernel(ids, k0, k1, x0, x1, out):
    c = ids[2]
    for refs, core in (((k0, k1), c), ((x0, x1), 1 - c)):
        for a, ref in enumerate(refs):
            for j in range(3):
                lane = pl.multiple_of(j * 512 + a * BLK + core * 256, BLK)
                out[:, pl.ds(lane, BLK)] = ref[j]


def assemble(ids, kept, swapped):
    rows = kept[0].shape[1]
    return pl.pallas_call(
        assemble_kernel,
        grid_spec=pltpu.PrefetchScalarGridSpec(
            num_scalar_prefetch=1,
            grid=(1,),
            in_specs=[pl.BlockSpec((3, rows, BLK), lambda i, ids: (0, 0, 0))] * 4,
            out_specs=pl.BlockSpec((rows, 1536), lambda i, ids: (0, 0)),
        ),
        out_shape=sds((rows, 1536), F32),
        compiler_params=params(16),
        cost_estimate=cost(0, rows * 1536 * 8),
        name="assemble",
    )(ids, *kept, *swapped)


def local(
    nseq,
    ndp,
    tokens,
    cotangent,
    weight,
    forget_peep,
    reset_peep,
    forget_bias,
    reset_bias,
    norm_gain,
    norm_bias,
    lengths,
):
    axes = ("seq", "dp")
    nz = ndp // 2
    seqs, span, width = tokens.shape
    parts = 8 // seqs
    sub = span // parts
    q = lax.axis_index("seq").astype(jnp.int32)
    dp = lax.axis_index("dp").astype(jnp.int32)
    z, c = dp // 2, dp % 2
    ids = jnp.stack([q, z, c])

    def table(move):
        pairs = []
        for qq in range(nseq):
            for zz in range(nz):
                for cc in range(2):
                    to = move(qq, zz, cc)
                    if to is not None:
                        pairs.append(
                            (qq * ndp + zz * 2 + cc, to[0] * ndp + to[1] * 2 + to[2])
                        )
        return pairs

    def send(value, move):
        return lax.ppermute(value, axes, table(move))

    def to_core(qq, zz, cc):
        return (qq, zz, 1 - cc)

    def to_x(qq, zz, cc):
        return (qq ^ 1, zz, cc)

    def to_y(qq, zz, cc):
        return (qq ^ 2, zz, cc)

    def shift_z(k):
        return lambda qq, zz, cc: (qq, (zz + k) % nz, cc)

    def shift_q(k):
        return lambda qq, zz, cc: (qq + k, zz, cc) if 0 <= qq + k < nseq else None

    mine, theirs = split_weight(ids, weight)
    recv = send(theirs, to_core)
    tok4 = tokens.reshape(seqs, parts, sub, width)
    cot4 = cotangent.reshape(seqs, parts, sub, width)
    tok_oth = send(tokens, to_core).reshape(seqs, parts, sub, width)
    cot_cols = jnp.concatenate(
        [lax.dynamic_slice_in_dim(cotangent, m * 512 + (1 - c) * 256, 256, 2) for m in range(4)],
        axis=2,
    )
    cot_oth = send(cot_cols, to_core).reshape(seqs, parts, sub, width // 2)
    len_oth = send(lengths, to_core)

    lens = jnp.stack([lengths, len_oth])
    counts = jnp.sum(lens, axis=1).astype(F32)
    scale = (seqs * span * nseq) / counts
    lim16 = (
        lens[:, :, None] - q * span - sub * jnp.arange(parts, dtype=jnp.int32)[None, None, :]
    ).reshape(16)
    lim = jnp.broadcast_to(lim16[None, :, None], (STEPS, 16, BLK)).reshape(256, BLK)
    scl = jnp.broadcast_to(scale[None, :, None, None], (STEPS, 2, 8, BLK)).reshape(256, BLK)

    def by_core(vec):
        v = lax.dynamic_slice_in_dim(vec.reshape(4, 4, BLK), 2 * c, 2, 1)
        return v.transpose(1, 0, 2).reshape(1, width // 2)

    vf, vr, bfor, brst = (by_core(v) for v in (forget_peep, reset_peep, forget_bias, reset_bias))
    gain, bias = norm_gain.reshape(1, width), norm_bias.reshape(1, width)

    qb = weight.shape[0] // 2
    source = jnp.where(q // 2 == c, mine, recv)
    quarter = lax.dynamic_slice_in_dim(source, (q % 2) * qb, qb, 0)
    pieces = []
    for s in range(4):
        piece = quarter[:, s * 768 : (s + 1) * 768]
        if nz <= 4:
            rel = jnp.concatenate([send(piece, shift_z(-k)) for k in range(1, nz)], axis=0)
        else:
            groups = [[cc + 2 * zz for zz in range(nz)] for cc in range(2)]
            got = lax.all_gather(piece, "dp", axis=0, tiled=True, axis_index_groups=groups)
            rel = lax.dynamic_slice_in_dim(
                jnp.concatenate([got, got], axis=0), (z + 1) * qb, (nz - 1) * qb, 0
            )
        gx = send(rel, to_x)
        gy = send(rel, to_y)
        dx = send(gy[:, :384], to_x)
        dy = send(gx[:, 384:], to_y)
        pieces.append((rel, gx, gy, dx, dy))

    ub, ubt, u32 = norm_tokens(ids, tok4, tok_oth, gain, bias)

    held = None
    ws, elem, accb, accc = [], [], [], []
    kept, swapped = [], []
    partial = None
    for a in range(2):
        fwd = []
        for s in (2 * a, 2 * a + 1):
            fwd.append(project(s, nz, ids, ub, u32, mine, recv, pieces[s], lim, vf, bfor))
            ws.append(fwd[-1][3])
        both = jnp.stack([f[5] for f in fwd])
        got = [send(both, shift_q(k)) for k in range(1, nseq)]
        mid = []
        for n, s in enumerate((2 * a, 2 * a + 1)):
            cand, decay, rpre, _, plin, _ = fwd[n]
            mid.append(
                states(
                    s, ids, cand, decay, rpre, u32, cot4, cot_oth, lim, scl, vr, brst, plin,
                    [g[n] for g in got], held,
                )
            )
            held = mid[-1][:2]
            accb.append(mid[-1][9])
        both = jnp.stack([m[8] for m in mid])
        got = [send(both, shift_q(-k)) for k in range(1, nseq)]
        dz = []
        for n, s in enumerate((2 * a, 2 * a + 1)):
            _, _, dstate, src, bc, du0, dz3, lbs, _, _ = mid[n]
            dz12, du, acc = adjoints(
                s, ids, fwd[n][1], bc, dstate, src, du0, u32, vf, fwd[n][4], lbs,
                [g[n] for g in got],
            )
            elem.append(du)
            accc.append(acc)
            dz.append((dz12, dz3))
        for flip in (True, False):
            out = weight_grad_part(
                flip, nz, ids, ubt, dz[0][0], dz[0][1], dz[1][0], dz[1][1]
            )
            half = out.shape[2] // 2
            ra = send(out[3, :, :half], to_x)
            rb = send(out[3, :, half:], to_y)
            s1 = jnp.concatenate(
                [out[1, :, :half], (out[1, :, half:].astype(F32) + rb.astype(F32)).astype(BF)], 1
            )
            s2 = jnp.concatenate(
                [(out[2, :, :half].astype(F32) + ra.astype(F32)).astype(BF), out[2, :, half:]], 1
            )
            r1 = send(s1, to_x)
            r2 = send(s2, to_y)
            tot = out[0].astype(F32) + r1.astype(F32) + r2.astype(F32)
            rows = tot.shape[1] // nz
            if nz <= 4:
                low = tot.astype(BF)
                acc = lax.dynamic_slice_in_dim(tot, z * rows, rows, 1)
                for k in range(1, nz):
                    part = lax.dynamic_slice_in_dim(low, ((z + k) % nz) * rows, rows, 1)
                    acc = acc + send(part, shift_z(k)).astype(F32)
            else:
                groups = [[cc + 2 * zz for zz in range(nz)] for cc in range(2)]
                acc = lax.psum_scatter(
                    tot, "dp", scatter_dimension=1, axis_index_groups=groups, tiled=True
                )
            if flip:
                swapped.append(send(acc, to_core))
            else:
                kept.append(acc)
        partial = unit_grads(ids, dz, ws[2 * a :], partial, elem if a else None)

    hrcv = send(held[1], to_core)
    activations = activations_of(ids, tok4, held[0], hrcv)
    dur = send(partial[1], to_core)
    input_grad, sums = input_grads(
        ids, partial[0], dur, tok4, cot4, lim16[:8], scale[:1], gain, accb, accc
    )
    bit = 1
    while bit < nseq:
        sums = sums + send(sums, lambda qq, zz, cc, b=bit: (qq ^ b, zz, cc))
        bit *= 2
    bit = 1
    while bit < nz:
        sums = sums + send(sums, lambda qq, zz, cc, b=bit: (qq, zz ^ b, cc))
        bit *= 2
    sums = sums + send(sums, to_core)
    weight_grad = assemble(ids, kept, swapped)
    shape = tokens.shape
    return (
        activations.reshape(shape),
        input_grad.reshape(shape),
        weight_grad,
        sums[0],
        sums[1],
        sums[2],
        sums[3],
        sums[4],
        sums[5],
    )


def solution(mesh):
    whole = P("dp", "seq", None)
    in_specs = (whole, whole, P("dp", None)) + (P(),) * 6 + (P("dp"),)
    out_specs = (whole, whole, P("dp", "seq")) + (P(),) * 6
    step = functools.partial(local, mesh.shape["seq"], mesh.shape["dp"])
    return jax.shard_map(step, mesh=mesh, in_specs=in_specs, out_specs=out_specs, check_vma=False)
```

time: 2000 us -> 572 us (0.29); the launches traced: 1960 us -> 565 us
  local copies, waits for them, and re-layouts: 825 us -> 98.5 us
  waiting for transfers between devices: 696 us -> 173 us
  other arithmetic: 259 us -> 15 us
  Pallas kernels: 0 us -> 172 us
  starting transfers between devices: 0.12 us -> 105 us
  matrix products: 92.2 us -> 0 us
  blocking collectives: 75.1 us -> 0 us
    slice x119 -> x12, local copies, waits for them, and re-layouts: 592 us -> 8.43 us  [the longest x4 4.19 us: local(): dy = send(gx[:, 384:], to_y)]
    reduce_scatter x2 -> x0, waiting for transfers between devices: 481 us -> none  [the longest x1 481 us: local(): lax.psum_scatter(lax.dot_general(columns, proj_grad, (((0,), (0,)), ((),...]
    all_gather x1 -> x0, waiting for transfers between devices: 214 us -> none  [local(): lax.all_gather(weight, 'dp', axis=0, tiled=True)]
    pad x60 -> x0, local copies, waits for them, and re-layouts: 192 us -> none  [the longest x30 113 us: local(): prod_fwd, local_fwd = lax.associative_scan(combine, (decay, inject), axis=1)]
    ppermute x0 -> x81, waiting for transfers between devices: none -> 173 us  [send(): return lax.ppermute(value, axes, table(move))]
    pallas_call x0 -> x23, Pallas kernels: none -> 172 us  [the longest x4 41.6 us: project(): pl.pallas_call(functools.partial(proj_kernel, s, nz), grid_spec=pltpu.Pre...]
    add x49 -> x9, other arithmetic: 111 us -> 2.59 us  [the longest x4 2.55 us: local(): acc = acc + send(part, shift_z(k)).astype(F32)]
    ppermute x0 -> x81, starting transfers between devices: none -> 105 us  [send(): return lax.ppermute(value, axes, table(move))]
  transfers between devices with their start and end apart: 3 -> 81, of which waited for: 2 -> 33; matrix products, arithmetic and copies ran while one was open for 3% -> 5% of each run, Pallas kernels for 0% -> 26%
where the time goes in v1:
time: 572 us; the launch traced here: 565 us
  waiting for transfers between devices  173 us (30%)
  Pallas kernels  172 us (30%)
  starting transfers between devices  105 us (18%)
  local copies, waits for them, and re-layouts  98.5 us (17%)
  other arithmetic  15 us (3%)
    ppermute x81, waiting for transfers between devices, send(): return lax.ppermute(value, axes, table(move))  173 us
    ppermute x81, starting transfers between devices, send(): return lax.ppermute(value, axes, table(move))  105 us
    unnamed x262, local copies, waits for them, and re-layouts  85.4 us
    pallas_call x4, Pallas kernels, project(): pl.pallas_call(functools.partial(proj_kernel, s, nz), grid_spec=pltpu.Pre...  41.6 us
    pallas_call x2, Pallas kernels, unit_grads(): pl.pallas_call(functools.partial(unit_grad_kernel, first), grid_spec=pltp...  31.3 us
    pallas_call x4, Pallas kernels, states(): pl.pallas_call(functools.partial(state_kernel, s, first, len(carries)), g...  26.5 us
    pallas_call x4, Pallas kernels, weight_grad_part(): pl.pallas_call(wgrad_kernel, grid_spec=pltpu.PrefetchScalarGridSpec(num_s...  25.9 us
    pallas_call x1, Pallas kernels, norm_tokens(): pl.pallas_call(norm_kernel, grid_spec=pltpu.PrefetchScalarGridSpec(num_sc...  17.5 us
  transfers between devices with their start and end apart: 81, of which 33 were waited for; matrix products, arithmetic and copies ran while one was open for 5% of the time, Pallas kernels for 26%

profile of v1, /device:TPU:10, one launch (start us, length us, event | category | flops | bytes accessed | tf_op | source)
XLA Modules:
  0.0 565.2 jit_solution(8516198658800853701)
XLA Ops:
  2.6 2.3 split_weight.1
  6.8 3.0 collective-permute-done.1.recv
  14.7 4.4 collective-permute-start.29
  20.3 4.3 collective-permute-start.22
  26.4 6.0 %collective-permute-done.29 = bf16[128,768]{1,0:T(8,128)(2,1)S(1)} collective-permute-done((bf16[128,768]{1,0:T(8,128)(2,1)S(1)}, bf16[128,768]{1,0:T(8,128)(2,1)S(1)}, u32[]{:S(2)}, u32[]{:S(2)}) %collective-permute-start.29) | collective-permute-done | bytes 196640 | tf_op jit(solution)/shard_map/ppermute | solution.py:756
  32.4 7.9 %collective-permute-start.13 = (bf16[128,768]{1,0:T(8,128)(2,1)S(1)}, bf16[128,768]{1,0:T(8,128)(2,1)S(1)}, u32[]{:S(2)}, u32[]{:S(2)}) collective-permute-start(bf16[128,768]{1,0:T(8,128)(2,1)S(1)} %get-tuple-element.233), channel_id=1, source_target_pairs={{0,2},{1,3},{2,4},{3,5},{4,6},{5,7},{6,0},{7,1},{8,10},{9,11},{10,... | collective-permute-start | bytes 589832 | tf_op jit(solution)/shard_map/ppermute | solution.py:756
  40.3 5.2 collective-permute-done.23
  45.6 11.8 %collective-permute-done.22 = bf16[128,768]{1,0:T(8,128)(2,1)S(1)} collective-permute-done((bf16[128,768]{1,0:T(8,128)(2,1)S(1)}, bf16[128,768]{1,0:T(8,128)(2,1)S(1)}, u32[]{:S(2)}, u32[]{:S(2)}) %collective-permute-start.22) | collective-permute-done | bytes 196640 | tf_op jit(solution)/shard_map/ppermute | solution.py:756
  57.3 3.4 collective-permute-start.12
  64.3 2.3 collective-permute-done.12
  66.6 2.9 collective-permute-start.3
  69.5 9.3 %collective-permute-done.4 = bf16[128,768]{1,0:T(8,128)(2,1)S(1)} collective-permute-done((bf16[128,768]{1,0:T(8,128)(2,1)S(1)}, bf16[128,768]{1,0:T(8,128)(2,1)S(1)}, u32[]{:S(2)}, u32[]{:S(2)}) %collective-permute-start.4) | collective-permute-done | bytes 196640 | tf_op jit(solution)/shard_map/ppermute | solution.py:756
  78.8 3.4 collective-permute-done.3
  90.7 7.9 %collective-permute-done.25.gy = bf16[384,768]{1,0:T(8,128)(2,1)} collective-permute-done((bf16[384,768]{1,0:T(8,128)(2,1)S(1)}, bf16[384,768]{1,0:T(8,128)(2,1)}, u32[]{:S(2)}, u32[]{:S(2)}) %collective-permute-start.25) | collective-permute-done | bytes 589856 | tf_op jit(solution)/shard_map/ppermute | solution.py:756
  103.4 7.6 %collective-permute-done.15.gy = bf16[384,768]{1,0:T(8,128)(2,1)S(1)} collective-permute-done((bf16[384,768]{1,0:T(8,128)(2,1)}, bf16[384,768]{1,0:T(8,128)(2,1)S(1)}, u32[]{:S(2)}, u32[]{:S(2)}) %collective-permute-start.15) | collective-permute-done | bytes 589856 | tf_op jit(solution)/shard_map/ppermute | solution.py:756
  111.6 2.2 collective-permute-done.14.gx
  118.3 5.4 collective-permute-done.6.gy
  130.1 17.5 %norm_tokens.1 = (bf16[1536,2048]{1,0:T(8,128)(2,1)S(1)}, bf16[2048,1536]{1,0:T(8,128)(2,1)S(1)}, f32[1536,1024]{1,0:T(8,128)}) custom-call(s32[3]{0:T(128)S(1)} %pad_add_fusion.1.ids, bf16[2,4,96,2048]{3,2,1,0:T(8,128)(2,1)S(1)} %bitcast.207, bf16[2,4,96,2048]{3,2,1,0:T(8,128)(2,1)} %bitcast.4.other, f32[1,2048]{1,0:T(1,128)S(1)} %bitcast.232, ...), custom_call_target="tpu_custom_call" | custom-call | flops 31457280 | bytes 31457280 | tf_op jit(solution)/shard_map/norm_tokens/pallas_call | solution.py:109
  147.6 2.6 copy-done.74
  152.4 11.5 %project_0.1 = (f32[1536,256]{1,0:T(8,128)S(1)}, f32[1536,256]{1,0:T(8,128)S(1)}, f32[1536,256]{1,0:T(8,128)S(1)}, bf16[2048,768]{1,0:T(8,128)(2,1)S(1)}, f32[32,256]{1,0:T(8,128)S(1)}, /*index=5*/f32[8,256]{1,0:T(8,128)S(1)}) custom-call(s32[3]{0:T(128)S(1)} %pad_add_fusion.1.ids, bf16[1536,2048]{1,0:T(8,128)(2,1)S(1)} %get-tuple-element.96.ub, ...), custom_call_target="tpu_custom_call" | custom-call | flops 4831838208 | bytes 18874368 | tf_op jit(solution)/shard_map/project_0/pallas_call | solution.py:214
  167.6 10.1 %project_1.1 = (f32[1536,256]{1,0:T(8,128)S(1)}, f32[1536,256]{1,0:T(8,128)S(1)}, f32[1536,256]{1,0:T(8,128)S(1)}, bf16[2048,768]{1,0:T(8,128)(2,1)S(1)}, f32[32,256]{1,0:T(8,128)S(1)}, /*index=5*/f32[8,256]{1,0:T(8,128)S(1)}) custom-call(s32[3]{0:T(128)S(1)} %pad_add_fusion.1.ids, bf16[1536,2048]{1,0:T(8,128)(2,1)S(1)} %get-tuple-element.96.ub, ...), custom_call_target="tpu_custom_call" | custom-call | flops 4831838208 | bytes 18874368 | tf_op jit(solution)/shard_map/project_1/pallas_call | solution.py:214
  182.6 3.2 collective-permute-start.36
  185.8 10.2 %project_2.1 = (f32[1536,256]{1,0:T(8,128)S(1)}, f32[1536,256]{1,0:T(8,128)S(1)}, f32[1536,256]{1,0:T(8,128)S(1)}, bf16[2048,768]{1,0:T(8,128)(2,1)S(1)}, f32[32,256]{1,0:T(8,128)S(1)}, /*index=5*/f32[8,256]{1,0:T(8,128)S(1)}) custom-call(s32[3]{0:T(128)S(1)} %pad_add_fusion.1.ids, bf16[1536,2048]{1,0:T(8,128)(2,1)S(1)} %get-tuple-element.96.ub, ...), custom_call_target="tpu_custom_call" | custom-call | flops 4831838208 | bytes 18874368 | tf_op jit(solution)/shard_map/project_2/pallas_call | solution.py:214
  200.8 9.8 %project_3.1 = (f32[1536,256]{1,0:T(8,128)S(1)}, f32[1536,256]{1,0:T(8,128)S(1)}, f32[1536,256]{1,0:T(8,128)S(1)}, bf16[2048,768]{1,0:T(8,128)(2,1)S(1)}, f32[32,256]{1,0:T(8,128)S(1)}, /*index=5*/f32[8,256]{1,0:T(8,128)S(1)}) custom-call(s32[3]{0:T(128)S(1)} %pad_add_fusion.1.ids, bf16[1536,2048]{1,0:T(8,128)(2,1)S(1)} %get-tuple-element.96.ub, ...), custom_call_target="tpu_custom_call" | custom-call | flops 4831838208 | bytes 18874368 | tf_op jit(solution)/shard_map/project_3/pallas_call | solution.py:214
  216.6 2.9 collective-permute-start.18
  219.8 6.6 %states_0.1 = (f32[4,2,768,128]{3,2,1,0:T(8,128)S(1)}, f32[4,2,768,128]{3,2,1,0:T(8,128)S(1)}, f32[1536,256]{1,0:T(8,128)S(1)}, f32[1536,256]{1,0:T(8,128)S(1)},...) custom-call(s32[3]{0:T(128)S(1)} %pad_add_fusion.1.ids, ...), custom_call_target="tpu_custom_call" | custom-call | flops 23592960 | bytes 15728640 | tf_op jit(solution)/shard_map/states_0/pallas_call | solution.py:375
  229.6 2.5 copy-done.63
  232.1 6.6 %states_1.1 = (f32[4,2,768,128]{3,2,1,0:T(8,128)S(1)}, f32[4,2,768,128]{3,2,1,0:T(8,128)S(1)}, f32[1536,256]{1,0:T(8,128)S(1)}, f32[1536,256]{1,0:T(8,128)S(1)},...) custom-call(s32[3]{0:T(128)S(1)} %pad_add_fusion.1.ids, ...), custom_call_target="tpu_custom_call", output_to_operand_aliasing={{0}: (17, {}), {1}: (18, {})} | custom-call | flops 23592960 | bytes 15728640 | tf_op jit(solution)/shard_map/states_1/pallas_call | solution.py:375
  246.2 3.7 collective-permute-start.42
  250.0 6.6 %states_2.1 = (f32[4,2,768,128]{3,2,1,0:T(8,128)S(1)}, f32[4,2,768,128]{3,2,1,0:T(8,128)S(1)}, f32[1536,256]{1,0:T(8,128)S(1)}, f32[1536,256]{1,0:T(8,128)S(1)},...) custom-call(s32[3]{0:T(128)S(1)} %pad_add_fusion.1.ids, ...), custom_call_target="tpu_custom_call", output_to_operand_aliasing={{0}: (17, {}), {1}: (18, {})} | custom-call | flops 23592960 | bytes 15728640 | tf_op jit(solution)/shard_map/states_2/pallas_call | solution.py:375
  263.8 2.0 copy-done.6
  265.9 6.7 %states_3.1 = (f32[4,2,768,128]{3,2,1,0:T(8,128)S(1)}, f32[4,2,768,128]{3,2,1,0:T(8,128)S(1)}, f32[1536,256]{1,0:T(8,128)S(1)}, f32[1536,256]{1,0:T(8,128)S(1)},...) custom-call(s32[3]{0:T(128)S(1)} %pad_add_fusion.1.ids, ...), custom_call_target="tpu_custom_call", output_to_operand_aliasing={{0}: (17, {}), {1}: (18, {})} | custom-call | flops 23592960 | bytes 15728640 | tf_op jit(solution)/shard_map/states_3/pallas_call | solution.py:375
  302.2 12.8 %unit_grads.2 = (f32[768,2048]{1,0:T(8,128)}, f32[768,2048]{1,0:T(8,128)}) custom-call(s32[3]{0:T(128)S(1)} %pad_add_fusion.1.ids, bf16[1536,512]{1,0:T(8,128)(2,1)S(1)} %copy-done.84, bf16[1536,256]{1,0:T(8,128)(2,1)S(1)} %copy-done.102, bf16[1536,512]{1,0:T(8,128)(2,1)S(1)} %copy-done.87, bf16[1536,256]{1,0:T(8,128)(2,1)S(1)} %copy-done.105, ...), custom_call_target="tpu_custom_call" | custom-call | flops 9663676416 | bytes 36175872 | tf_op jit(solution)/shard_map/unit_grads/pallas_call | solution.py:572
  319.3 2.0 adjoints_2.1
  338.0 18.4 %unit_grads.3 = (f32[768,2048]{1,0:T(8,128)}, f32[768,2048]{1,0:T(8,128)}) custom-call(s32[3]{0:T(128)S(1)} %pad_add_fusion.1.ids, bf16[1536,512]{1,0:T(8,128)(2,1)S(1)} %copy-done.92, bf16[1536,256]{1,0:T(8,128)(2,1)S(1)} %copy-done.109, bf16[1536,512]{1,0:T(8,128)(2,1)S(1)} %copy-done.97, bf16[1536,256]{1,0:T(8,128)(2,1)S(1)} %copy-done.112, ...), custom_call_target="tpu_custom_call" | custom-call | flops 9663676416 | bytes 36175872 | tf_op jit(solution)/shard_map/unit_grads/pallas_call | solution.py:572
  356.5 2.8 copy-done.75
  359.3 6.4 %weight_grad_part.6 = bf16[4,3,1024,128]{3,2,1,0:T(8,128)(2,1)S(1)} custom-call(s32[3]{0:T(128)S(1)} %pad_add_fusion.1.ids, bf16[2048,1536]{1,0:T(8,128)(2,1)S(1)} %copy-done.75, bf16[1536,512]{1,0:T(8,128)(2,1)S(1)} %copy-done.85, bf16[1536,256]{1,0:T(8,128)(2,1)S(1)} %copy-done.103, bf16[1536,512]{1,0:T(8,128)(2,1)S(1)} %copy-done.88, ...), custom_call_target="tpu_custom_call" | custom-call | flops 4831838208 | bytes 11010048 | tf_op jit(solution)/shard_map/weight_grad_part/pallas_call | solution.py:514
  366.6 3.5 collective-permute-start.60
  370.0 6.4 %weight_grad_part.4 = bf16[4,3,1024,128]{3,2,1,0:T(8,128)(2,1)S(1)} custom-call(s32[3]{0:T(128)S(1)} %pad_add_fusion.1.ids, bf16[2048,1536]{1,0:T(8,128)(2,1)S(1)} %copy-done.75, bf16[1536,512]{1,0:T(8,128)(2,1)S(1)} %copy-done.85, bf16[1536,256]{1,0:T(8,128)(2,1)S(1)} %copy-done.103, bf16[1536,512]{1,0:T(8,128)(2,1)S(1)} %copy-done.88, ...), custom_call_target="tpu_custom_call" | custom-call | flops 4831838208 | bytes 11010048 | tf_op jit(solution)/shard_map/weight_grad_part/pallas_call | solution.py:514
  378.3 6.5 %weight_grad_part.7 = bf16[4,3,1024,128]{3,2,1,0:T(8,128)(2,1)S(1)} custom-call(s32[3]{0:T(128)S(1)} %pad_add_fusion.1.ids, bf16[2048,1536]{1,0:T(8,128)(2,1)S(1)} %bitcast.245, bf16[1536,512]{1,0:T(8,128)(2,1)S(1)} %copy-done.93, bf16[1536,256]{1,0:T(8,128)(2,1)S(1)} %copy-done.110, bf16[1536,512]{1,0:T(8,128)(2,1)S(1)} %copy-done.98, ...), custom_call_target="tpu_custom_call" | custom-call | flops 4831838208 | bytes 11010048 | tf_op jit(solution)/shard_map/weight_grad_part/pallas_call | solution.py:514
  384.8 6.7 %weight_grad_part.5 = bf16[4,3,1024,128]{3,2,1,0:T(8,128)(2,1)S(1)} custom-call(s32[3]{0:T(128)S(1)} %pad_add_fusion.1.ids, bf16[2048,1536]{1,0:T(8,128)(2,1)S(1)} %bitcast.245, bf16[1536,512]{1,0:T(8,128)(2,1)S(1)} %copy-done.93, bf16[1536,256]{1,0:T(8,128)(2,1)S(1)} %copy-done.110, bf16[1536,512]{1,0:T(8,128)(2,1)S(1)} %copy-done.98, ...), custom_call_target="tpu_custom_call" | custom-call | flops 4831838208 | bytes 11010048 | tf_op jit(solution)/shard_map/weight_grad_part/pallas_call | solution.py:514
  396.6 7.2 %collective-permute-done.55 = bf16[3,512,128]{2,1,0:T(8,128)(2,1)S(1)} collective-permute-done((bf16[3,512,128]{2,1,0:T(8,128)(2,1)S(1)}, bf16[3,512,128]{2,1,0:T(8,128)(2,1)S(1)}, u32[]{:S(2)}, u32[]{:S(2)}) %collective-permute-start.55) | collective-permute-done | bytes 393248 | tf_op jit(solution)/shard_map/ppermute | solution.py:756
  406.5 5.7 %collective-permute-done.70 = bf16[3,512,128]{2,1,0:T(8,128)(2,1)S(1)} collective-permute-done((bf16[3,512,128]{2,1,0:T(8,128)(2,1)S(1)}, bf16[3,512,128]{2,1,0:T(8,128)(2,1)S(1)}, u32[]{:S(2)}, u32[]{:S(2)}) %collective-permute-start.70) | collective-permute-done | bytes 393248 | tf_op jit(solution)/shard_map/ppermute | solution.py:756
  413.9 16.4 %collective-permute-done.68 = bf16[3,512,128]{2,1,0:T(8,128)(2,1)S(1)} collective-permute-done((bf16[3,512,128]{2,1,0:T(8,128)(2,1)S(1)}, bf16[3,512,128]{2,1,0:T(8,128)(2,1)S(1)}, u32[]{:S(2)}, u32[]{:S(2)}) %collective-permute-start.68) | collective-permute-done | bytes 393248 | tf_op jit(solution)/shard_map/ppermute | solution.py:756
  433.2 13.9 %collective-permute-done.49 = bf16[3,1024,128]{2,1,0:T(8,128)(2,1)S(1)} collective-permute-done((bf16[3,1024,128]{2,1,0:T(8,128)(2,1)S(1)}, bf16[3,1024,128]{2,1,0:T(8,128)(2,1)S(1)}, u32[]{:S(2)}, u32[]{:S(2)}) %collective-permute-start.49) | collective-permute-done | bytes 786464 | tf_op jit(solution)/shard_map/ppermute | solution.py:756
  448.0 2.7 fusion.19
  452.3 11.7 %collective-permute-done.56 = bf16[3,1024,128]{2,1,0:T(8,128)(2,1)S(1)} collective-permute-done((bf16[3,1024,128]{2,1,0:T(8,128)(2,1)S(1)}, bf16[3,1024,128]{2,1,0:T(8,128)(2,1)S(1)}, u32[]{:S(2)}, u32[]{:S(2)}) %collective-permute-start.56) | collective-permute-done | bytes 786464 | tf_op jit(solution)/shard_map/ppermute | solution.py:756
  466.1 2.0 collective-permute-start.64
  468.1 2.5 fusion.21
  470.6 8.9 %collective-permute-done.71 = bf16[3,1024,128]{2,1,0:T(8,128)(2,1)S(1)} collective-permute-done((bf16[3,1024,128]{2,1,0:T(8,128)(2,1)S(1)}, bf16[3,1024,128]{2,1,0:T(8,128)(2,1)S(1)}, u32[]{:S(2)}, u32[]{:S(2)}) %collective-permute-start.71) | collective-permute-done | bytes 786464 | tf_op jit(solution)/shard_map/ppermute | solution.py:756
  480.8 2.2 collective-permute-start.65
  484.8 11.9 %input_grads.1 = (f32[2,4,96,2048]{3,2,1,0:T(8,128)}, f32[8,2048]{1,0:T(8,128)S(1)}) custom-call(s32[3]{0:T(128)S(1)} %pad_add_fusion.1.ids, f32[768,2048]{1,0:T(8,128)S(1)} %bitcast.211, f32[768,2048]{1,0:T(8,128)} %collective-permute-done.45.dur, bf16[2,4,96,2048]{3,2,1,0:T(8,128)(2,1)S(1)} %bitcast.208, bf16[2,4,96,2048]{3,2,1,0:T(8,128)(2,1)S(1)} %bitcast.198, ...), custom_call_target="tpu_custom_call" | custom-call | flops 31457280 | bytes 25165824 | tf_op jit(solution)/shard_map/input_grads/pallas_call | solution.py:673
  498.7 2.3 collective-permute-done.76
  501.7 3.6 collective-permute-done.77
  507.1 2.0 collective-permute-start.72
  510.7 3.6 collective-permute-start.73
  517.2 11.0 %collective-permute-done.72 = bf16[3,256,128]{2,1,0:T(8,128)(2,1)S(1)} collective-permute-done((bf16[3,256,128]{2,1,0:T(8,128)(2,1)S(1)}, bf16[3,256,128]{2,1,0:T(8,128)(2,1)S(1)}, u32[]{:S(2)}, u32[]{:S(2)}) %collective-permute-start.72) | collective-permute-done | bytes 196640 | tf_op jit(solution)/shard_map/ppermute | solution.py:756
  528.2 3.0 collective-permute-start.57
  531.2 8.1 %collective-permute-done.73 = bf16[3,256,128]{2,1,0:T(8,128)(2,1)S(1)} collective-permute-done((bf16[3,256,128]{2,1,0:T(8,128)(2,1)S(1)}, bf16[3,256,128]{2,1,0:T(8,128)(2,1)S(1)}, u32[]{:S(2)}, u32[]{:S(2)}) %collective-permute-start.73) | collective-permute-done | bytes 196640 | tf_op jit(solution)/shard_map/ppermute | solution.py:756
  539.3 3.5 collective-permute-start.79
  544.4 2.6 collective-permute-start.58
  547.1 4.5 collective-permute-done.57
  552.4 4.6 collective-permute-done.59
  559.1 5.4 activations_of.1
  (472 shorter events, 166.3 us)
Async XLA Ops:
  6.1 122.7 %collective-permute-start = (bf16[2,384,2048]{2,1,0:T(8,128)(2,1)}, bf16[2,384,2048]{2,1,0:T(8,128)(2,1)}, u32[]{:S(2)}, u32[]{:S(2)}) collective-permute-start(bf16[2,384,2048]{2,1,0:T(8,128)(2,1)} %param.10), channel_id=1, source_target_pairs={{0,1},{1,0},{2,3},{3,2},{4,5},{5,4},{6,7},{7,6},{8,9},{9,8},{10,11... | collective-permute-start | bytes 9437192 | tf_op jit(solution)/shard_map/ppermute | solution.py:756
  14.7 17.7 %collective-permute-start.29 = (bf16[128,768]{1,0:T(8,128)(2,1)S(1)}, bf16[128,768]{1,0:T(8,128)(2,1)S(1)}, u32[]{:S(2)}, u32[]{:S(2)}) collective-permute-start(bf16[128,768]{1,0:T(8,128)(2,1)S(1)} %get-tuple-element.231), channel_id=1, source_target_pairs={{0,4},{1,5},{2,6},{3,7},{4,0},{5,1},{6,2},{7,3},{8,12},{9,13},{10,... | collective-permute-start | bytes 589832 | tf_op jit(solution)/shard_map/ppermute | solution.py:756
  19.1 26.4 %collective-permute-start.23 = (bf16[128,768]{1,0:T(8,128)(2,1)S(1)}, bf16[128,768]{1,0:T(8,128)(2,1)S(1)}, u32[]{:S(2)}, u32[]{:S(2)}) collective-permute-start(bf16[128,768]{1,0:T(8,128)(2,1)S(1)} %get-tuple-element.232), channel_id=1, source_target_pairs={{0,2},{1,3},{2,4},{3,5},{4,6},{5,7},{6,0},{7,1},{8,10},{9,11},{10,... | collective-permute-start | bytes 589832 | tf_op jit(solution)/shard_map/ppermute | solution.py:756
  20.3 37.0 %collective-permute-start.22 = (bf16[128,768]{1,0:T(8,128)(2,1)S(1)}, bf16[128,768]{1,0:T(8,128)(2,1)S(1)}, u32[]{:S(2)}, u32[]{:S(2)}) collective-permute-start(bf16[128,768]{1,0:T(8,128)(2,1)S(1)} %get-tuple-element.232), channel_id=1, source_target_pairs={{0,4},{1,5},{2,6},{3,7},{4,0},{5,1},{6,2},{7,3},{8,12},{9,13},{10,... | collective-permute-start | bytes 589832 | tf_op jit(solution)/shard_map/ppermute | solution.py:756
  25.3 35.4 %collective-permute-start.21 = (bf16[128,768]{1,0:T(8,128)(2,1)S(1)}, bf16[128,768]{1,0:T(8,128)(2,1)S(1)}, u32[]{:S(2)}, u32[]{:S(2)}) collective-permute-start(bf16[128,768]{1,0:T(8,128)(2,1)S(1)} %get-tuple-element.232), channel_id=1, source_target_pairs={{0,6},{1,7},{2,0},{3,1},{4,2},{5,3},{6,4},{7,5},{8,14},{9,15},{10,... | collective-permute-start | bytes 589832 | tf_op jit(solution)/shard_map/ppermute | solution.py:756
  32.4 29.1 %collective-permute-start.13 = (bf16[128,768]{1,0:T(8,128)(2,1)S(1)}, bf16[128,768]{1,0:T(8,128)(2,1)S(1)}, u32[]{:S(2)}, u32[]{:S(2)}) collective-permute-start(bf16[128,768]{1,0:T(8,128)(2,1)S(1)} %get-tuple-element.233), channel_id=1, source_target_pairs={{0,2},{1,3},{2,4},{3,5},{4,6},{5,7},{6,0},{7,1},{8,10},{9,11},{10,... | collective-permute-start | bytes 589832 | tf_op jit(solution)/shard_map/ppermute | solution.py:756
  45.5 17.5 %collective-permute-start.11 = (bf16[128,768]{1,0:T(8,128)(2,1)S(1)}, bf16[128,768]{1,0:T(8,128)(2,1)S(1)}, u32[]{:S(2)}, u32[]{:S(2)}) collective-permute-start(bf16[128,768]{1,0:T(8,128)(2,1)S(1)} %get-tuple-element.233), channel_id=1, source_target_pairs={{0,6},{1,7},{2,0},{3,1},{4,2},{5,3},{6,4},{7,5},{8,14},{9,15},{10,... | collective-permute-start | bytes 589832 | tf_op jit(solution)/shard_map/ppermute | solution.py:756
  60.7 18.0 %collective-permute-start.4 = (bf16[128,768]{1,0:T(8,128)(2,1)S(1)}, bf16[128,768]{1,0:T(8,128)(2,1)S(1)}, u32[]{:S(2)}, u32[]{:S(2)}) collective-permute-start(bf16[128,768]{1,0:T(8,128)(2,1)S(1)} %get-tuple-element.234), channel_id=1, source_target_pairs={{0,2},{1,3},{2,4},{3,5},{4,6},{5,7},{6,0},{7,1},{8,10},{9,11},{10,... | collective-permute-start | bytes 589832 | tf_op jit(solution)/shard_map/ppermute | solution.py:756
  61.5 25.3 %collective-permute-start.32 = (bf16[384,768]{1,0:T(8,128)(2,1)S(1)}, bf16[384,768]{1,0:T(8,128)(2,1)S(1)}, u32[]{:S(2)}, u32[]{:S(2)}) collective-permute-start(bf16[384,768]{1,0:T(8,128)(2,1)S(1)} %constant_dynamic-update-slice_fusion.9.rel), channel_id=1, source_target_pairs={{0,16},{1,17},{2,18},{3,19},{4,20},{5,21},{6,22},{7,23},{8,24},{9,... | collective-permute-start | bytes 1769480 | tf_op jit(solution)/shard_map/ppermute | solution.py:756
  63.0 25.3 %collective-permute-start.31 = (bf16[384,768]{1,0:T(8,128)(2,1)S(1)}, bf16[384,768]{1,0:T(8,128)(2,1)S(1)}, u32[]{:S(2)}, u32[]{:S(2)}) collective-permute-start(bf16[384,768]{1,0:T(8,128)(2,1)S(1)} %constant_dynamic-update-slice_fusion.9.rel), channel_id=1, source_target_pairs={{0,8},{1,9},{2,10},{3,11},{4,12},{5,13},{6,14},{7,15},{8,0},{9,1},... | collective-permute-start | bytes 1769480 | tf_op jit(solution)/shard_map/ppermute | solution.py:756
  66.6 15.6 %collective-permute-start.3 = (bf16[128,768]{1,0:T(8,128)(2,1)S(1)}, bf16[128,768]{1,0:T(8,128)(2,1)S(1)}, u32[]{:S(2)}, u32[]{:S(2)}) collective-permute-start(bf16[128,768]{1,0:T(8,128)(2,1)S(1)} %get-tuple-element.234), channel_id=1, source_target_pairs={{0,4},{1,5},{2,6},{3,7},{4,0},{5,1},{6,2},{7,3},{8,12},{9,13},{10,... | collective-permute-start | bytes 589832 | tf_op jit(solution)/shard_map/ppermute | solution.py:756
  82.2 16.4 %collective-permute-start.25 = (bf16[384,768]{1,0:T(8,128)(2,1)S(1)}, bf16[384,768]{1,0:T(8,128)(2,1)}, u32[]{:S(2)}, u32[]{:S(2)}) collective-permute-start(bf16[384,768]{1,0:T(8,128)(2,1)S(1)} %constant_dynamic-update-slice_fusion.6.rel), channel_id=1, source_target_pairs={{0,16},{1,17},{2,18},{3,19},{4,20},{5,21},{6,22},{7,23},{8,24},{9,... | collective-permute-start | bytes 1769480 | tf_op jit(solution)/shard_map/ppermute | solution.py:756
  84.9 16.4 %collective-permute-start.24 = (bf16[384,768]{1,0:T(8,128)(2,1)S(1)}, bf16[384,768]{1,0:T(8,128)(2,1)}, u32[]{:S(2)}, u32[]{:S(2)}) collective-permute-start(bf16[384,768]{1,0:T(8,128)(2,1)S(1)} %constant_dynamic-update-slice_fusion.6.rel), channel_id=1, source_target_pairs={{0,8},{1,9},{2,10},{3,11},{4,12},{5,13},{6,14},{7,15},{8,0},{9,1},... | collective-permute-start | bytes 1769480 | tf_op jit(solution)/shard_map/ppermute | solution.py:756
  86.8 24.3 %collective-permute-start.15 = (bf16[384,768]{1,0:T(8,128)(2,1)}, bf16[384,768]{1,0:T(8,128)(2,1)S(1)}, u32[]{:S(2)}, u32[]{:S(2)}) collective-permute-start(bf16[384,768]{1,0:T(8,128)(2,1)} %constant_dynamic-update-slice_fusion.3.rel), channel_id=1, source_target_pairs={{0,16},{1,17},{2,18},{3,19},{4,20},{5,21},{6,22},{7,23},{8,24},{9,... | collective-permute-start | bytes 1769480 | tf_op jit(solution)/shard_map/ppermute | solution.py:756
  88.3 25.5 %collective-permute-start.14 = (bf16[384,768]{1,0:T(8,128)(2,1)}, bf16[384,768]{1,0:T(8,128)(2,1)S(1)}, u32[]{:S(2)}, u32[]{:S(2)}) collective-permute-start(bf16[384,768]{1,0:T(8,128)(2,1)} %constant_dynamic-update-slice_fusion.3.rel), channel_id=1, source_target_pairs={{0,8},{1,9},{2,10},{3,11},{4,12},{5,13},{6,14},{7,15},{8,0},{9,1},... | collective-permute-start | bytes 1769480 | tf_op jit(solution)/shard_map/ppermute | solution.py:756
  98.5 25.2 %collective-permute-start.6 = (bf16[384,768]{1,0:T(8,128)(2,1)}, bf16[384,768]{1,0:T(8,128)(2,1)S(1)}, u32[]{:S(2)}, u32[]{:S(2)}) collective-permute-start(bf16[384,768]{1,0:T(8,128)(2,1)} %constant_dynamic-update-slice_fusion.rel), channel_id=1, source_target_pairs={{0,16},{1,17},{2,18},{3,19},{4,20},{5,21},{6,22},{7,23},{8,24},{9,... | collective-permute-start | bytes 1769480 | tf_op jit(solution)/shard_map/ppermute | solution.py:756
  101.2 25.1 %collective-permute-start.5 = (bf16[384,768]{1,0:T(8,128)(2,1)}, bf16[384,768]{1,0:T(8,128)(2,1)}, u32[]{:S(2)}, u32[]{:S(2)}) collective-permute-start(bf16[384,768]{1,0:T(8,128)(2,1)} %constant_dynamic-update-slice_fusion.rel), channel_id=1, source_target_pairs={{0,8},{1,9},{2,10},{3,11},{4,12},{5,13},{6,14},{7,15},{8,0},{9,1},... | collective-permute-start | bytes 1769480 | tf_op jit(solution)/shard_map/ppermute | solution.py:756
  111.1 39.2 %collective-permute-start.33 = (bf16[384,384]{1,0:T(8,128)(2,1)}, bf16[384,384]{1,0:T(8,128)(2,1)S(1)}, u32[]{:S(2)}, u32[]{:S(2)}) collective-permute-start(bf16[384,384]{1,0:T(8,128)(2,1)} %slice.308), channel_id=1, source_target_pairs={{0,8},{1,9},{2,10},{3,11},{4,12},{5,13},{6,14},{7,15},{8,0},{9,1},... | collective-permute-start | bytes 884744 | tf_op jit(solution)/shard_map/ppermute | solution.py:756
  113.8 37.0 %collective-permute-start.34 = (bf16[384,384]{1,0:T(8,128)(2,1)}, bf16[384,384]{1,0:T(8,128)(2,1)}, u32[]{:S(2)}, u32[]{:S(2)}) collective-permute-start(bf16[384,384]{1,0:T(8,128)(2,1)} %slice.309), channel_id=1, source_target_pairs={{0,16},{1,17},{2,18},{3,19},{4,20},{5,21},{6,22},{7,23},{8,24},{9,... | collective-permute-start | bytes 884744 | tf_op jit(solution)/shard_map/ppermute | solution.py:756
  123.7 95.9 %collective-permute-start.10 = (bf16[2,384,1024]{2,1,0:T(8,128)(2,1)}, bf16[2,384,1024]{2,1,0:T(8,128)(2,1)S(1)}, u32[]{:S(2)}, u32[]{:S(2)}) collective-permute-start(bf16[2,384,1024]{2,1,0:T(8,128)(2,1)} %pad_maximum_fusion), channel_id=1, source_target_pairs={{0,1},{1,0},{2,3},{3,2},{4,5},{5,4},{6,7},{7,6},{8,9},{9,8},{10,11... | collective-permute-start | bytes 4718600 | tf_op jit(solution)/shard_map/ppermute | solution.py:756
  126.3 39.3 %collective-permute-start.26 = (bf16[384,384]{1,0:T(8,128)(2,1)S(1)}, bf16[384,384]{1,0:T(8,128)(2,1)S(1)}, u32[]{:S(2)}, u32[]{:S(2)}) collective-permute-start(bf16[384,384]{1,0:T(8,128)(2,1)S(1)} %slice.305), channel_id=1, source_target_pairs={{0,8},{1,9},{2,10},{3,11},{4,12},{5,13},{6,14},{7,15},{8,0},{9,1},... | collective-permute-start | bytes 884744 | tf_op jit(solution)/shard_map/ppermute | solution.py:756
  128.7 37.6 %collective-permute-start.27 = (bf16[384,384]{1,0:T(8,128)(2,1)S(1)}, bf16[384,384]{1,0:T(8,128)(2,1)S(1)}, u32[]{:S(2)}, u32[]{:S(2)}) collective-permute-start(bf16[384,384]{1,0:T(8,128)(2,1)S(1)} %slice.306), channel_id=1, source_target_pairs={{0,16},{1,17},{2,18},{3,19},{4,20},{5,21},{6,22},{7,23},{8,24},{9,... | collective-permute-start | bytes 884744 | tf_op jit(solution)/shard_map/ppermute | solution.py:756
  150.3 31.5 %collective-permute-start.16 = (bf16[384,384]{1,0:T(8,128)(2,1)}, bf16[384,384]{1,0:T(8,128)(2,1)S(1)}, u32[]{:S(2)}, u32[]{:S(2)}) collective-permute-start(bf16[384,384]{1,0:T(8,128)(2,1)} %slice.296), channel_id=1, source_target_pairs={{0,8},{1,9},{2,10},{3,11},{4,12},{5,13},{6,14},{7,15},{8,0},{9,1},... | collective-permute-start | bytes 884744 | tf_op jit(solution)/shard_map/ppermute | solution.py:756
  150.7 31.8 %collective-permute-start.17 = (bf16[384,384]{1,0:T(8,128)(2,1)}, bf16[384,384]{1,0:T(8,128)(2,1)S(1)}, u32[]{:S(2)}, u32[]{:S(2)}) collective-permute-start(bf16[384,384]{1,0:T(8,128)(2,1)} %slice.297), channel_id=1, source_target_pairs={{0,16},{1,17},{2,18},{3,19},{4,20},{5,21},{6,22},{7,23},{8,24},{9,... | collective-permute-start | bytes 884744 | tf_op jit(solution)/shard_map/ppermute | solution.py:756
  165.6 33.3 %collective-permute-start.7 = (bf16[384,384]{1,0:T(8,128)(2,1)}, bf16[384,384]{1,0:T(8,128)(2,1)S(1)}, u32[]{:S(2)}, u32[]{:S(2)}) collective-permute-start(bf16[384,384]{1,0:T(8,128)(2,1)} %slice.293), channel_id=1, source_target_pairs={{0,8},{1,9},{2,10},{3,11},{4,12},{5,13},{6,14},{7,15},{8,0},{9,1},... | collective-permute-start | bytes 884744 | tf_op jit(solution)/shard_map/ppermute | solution.py:756
  166.3 34.4 %collective-permute-start.8 = (bf16[384,384]{1,0:T(8,128)(2,1)}, bf16[384,384]{1,0:T(8,128)(2,1)S(1)}, u32[]{:S(2)}, u32[]{:S(2)}) collective-permute-start(bf16[384,384]{1,0:T(8,128)(2,1)} %slice.294), channel_id=1, source_target_pairs={{0,16},{1,17},{2,18},{3,19},{4,20},{5,21},{6,22},{7,23},{8,24},{9,... | collective-permute-start | bytes 884744 | tf_op jit(solution)/shard_map/ppermute | solution.py:756
  181.8 33.5 %collective-permute-start.37 = (f32[2,8,256]{2,1,0:T(8,128)S(1)}, f32[2,8,256]{2,1,0:T(8,128)S(1)}, u32[]{:S(2)}, u32[]{:S(2)}) collective-permute-start(f32[2,8,256]{2,1,0:T(8,128)S(1)} %pad_maximum_fusion.10), channel_id=1, source_target_pairs={{0,24},{1,25},{2,26},{3,27},{4,28},{5,29},{6,30},{7,31}} | collective-permute-start | bytes 49160 | tf_op jit(solution)/shard_map/ppermute | solution.py:756
  182.6 34.0 %collective-permute-start.36 = (f32[2,8,256]{2,1,0:T(8,128)S(1)}, f32[2,8,256]{2,1,0:T(8,128)S(1)}, u32[]{:S(2)}, u32[]{:S(2)}) collective-permute-start(f32[2,8,256]{2,1,0:T(8,128)S(1)} %pad_maximum_fusion.10), channel_id=1, source_target_pairs={{0,16},{1,17},{2,18},{3,19},{4,20},{5,21},{6,22},{7,23},{8,24},{9,... | collective-permute-start | bytes 49160 | tf_op jit(solution)/shard_map/ppermute | solution.py:756
  198.8 20.8 %collective-permute-start.35 = (f32[2,8,256]{2,1,0:T(8,128)S(1)}, f32[2,8,256]{2,1,0:T(8,128)S(1)}, u32[]{:S(2)}, u32[]{:S(2)}) collective-permute-start(f32[2,8,256]{2,1,0:T(8,128)S(1)} %pad_maximum_fusion.10), channel_id=1, source_target_pairs={{0,8},{1,9},{2,10},{3,11},{4,12},{5,13},{6,14},{7,15},{8,16},{9,17... | collective-permute-start | bytes 49160 | tf_op jit(solution)/shard_map/ppermute | solution.py:756
  214.7 31.5 %collective-permute-start.20 = (f32[2,8,256]{2,1,0:T(8,128)S(1)}, f32[2,8,256]{2,1,0:T(8,128)S(1)}, u32[]{:S(2)}, u32[]{:S(2)}) collective-permute-start(f32[2,8,256]{2,1,0:T(8,128)S(1)} %pad_maximum_fusion.9), channel_id=1, source_target_pairs={{0,24},{1,25},{2,26},{3,27},{4,28},{5,29},{6,30},{7,31}} | collective-permute-start | bytes 49160 | tf_op jit(solution)/shard_map/ppermute | solution.py:756
  215.3 34.6 %collective-permute-start.19 = (f32[2,8,256]{2,1,0:T(8,128)S(1)}, f32[2,8,256]{2,1,0:T(8,128)S(1)}, u32[]{:S(2)}, u32[]{:S(2)}) collective-permute-start(f32[2,8,256]{2,1,0:T(8,128)S(1)} %pad_maximum_fusion.9), channel_id=1, source_target_pairs={{0,16},{1,17},{2,18},{3,19},{4,20},{5,21},{6,22},{7,23},{8,24},{9,... | collective-permute-start | bytes 49160 | tf_op jit(solution)/shard_map/ppermute | solution.py:756
  216.6 33.3 %collective-permute-start.18 = (f32[2,8,256]{2,1,0:T(8,128)S(1)}, f32[2,8,256]{2,1,0:T(8,128)S(1)}, u32[]{:S(2)}, u32[]{:S(2)}) collective-permute-start(f32[2,8,256]{2,1,0:T(8,128)S(1)} %pad_maximum_fusion.9), channel_id=1, source_target_pairs={{0,8},{1,9},{2,10},{3,11},{4,12},{5,13},{6,14},{7,15},{8,16},{9,17... | collective-permute-start | bytes 49160 | tf_op jit(solution)/shard_map/ppermute | solution.py:756
  244.2 36.6 %collective-permute-start.44 = (f32[2,8,256]{2,1,0:T(8,128)S(1)}, f32[2,8,256]{2,1,0:T(8,128)S(1)}, u32[]{:S(2)}, u32[]{:S(2)}) collective-permute-start(f32[2,8,256]{2,1,0:T(8,128)S(1)} %pad_maximum_fusion.12), channel_id=1, source_target_pairs={{24,0},{25,1},{26,2},{27,3},{28,4},{29,5},{30,6},{31,7}} | collective-permute-start | bytes 49160 | tf_op jit(solution)/shard_map/ppermute | solution.py:756
  244.9 37.9 %collective-permute-start.43 = (f32[2,8,256]{2,1,0:T(8,128)S(1)}, f32[2,8,256]{2,1,0:T(8,128)S(1)}, u32[]{:S(2)}, u32[]{:S(2)}) collective-permute-start(f32[2,8,256]{2,1,0:T(8,128)S(1)} %pad_maximum_fusion.12), channel_id=1, source_target_pairs={{16,0},{17,1},{18,2},{19,3},{20,4},{21,5},{22,6},{23,7},{24,8},{25... | collective-permute-start | bytes 49160 | tf_op jit(solution)/shard_map/ppermute | solution.py:756
  246.2 36.6 %collective-permute-start.42 = (f32[2,8,256]{2,1,0:T(8,128)S(1)}, f32[2,8,256]{2,1,0:T(8,128)S(1)}, u32[]{:S(2)}, u32[]{:S(2)}) collective-permute-start(f32[2,8,256]{2,1,0:T(8,128)S(1)} %pad_maximum_fusion.12), channel_id=1, source_target_pairs={{8,0},{9,1},{10,2},{11,3},{12,4},{13,5},{14,6},{15,7},{16,8},{17,9... | collective-permute-start | bytes 49160 | tf_op jit(solution)/shard_map/ppermute | solution.py:756
  278.8 36.2 %collective-permute-start.41 = (f32[2,8,256]{2,1,0:T(8,128)S(1)}, f32[2,8,256]{2,1,0:T(8,128)S(1)}, u32[]{:S(2)}, u32[]{:S(2)}) collective-permute-start(f32[2,8,256]{2,1,0:T(8,128)S(1)} %pad_maximum_fusion.11), channel_id=1, source_target_pairs={{24,0},{25,1},{26,2},{27,3},{28,4},{29,5},{30,6},{31,7}} | collective-permute-start | bytes 49160 | tf_op jit(solution)/shard_map/ppermute | solution.py:756
  279.5 35.6 %collective-permute-start.40 = (f32[2,8,256]{2,1,0:T(8,128)S(1)}, f32[2,8,256]{2,1,0:T(8,128)S(1)}, u32[]{:S(2)}, u32[]{:S(2)}) collective-permute-start(f32[2,8,256]{2,1,0:T(8,128)S(1)} %pad_maximum_fusion.11), channel_id=1, source_target_pairs={{16,0},{17,1},{18,2},{19,3},{20,4},{21,5},{22,6},{23,7},{24,8},{25... | collective-permute-start | bytes 49160 | tf_op jit(solution)/shard_map/ppermute | solution.py:756
  280.8 34.3 %collective-permute-start.39 = (f32[2,8,256]{2,1,0:T(8,128)S(1)}, f32[2,8,256]{2,1,0:T(8,128)S(1)}, u32[]{:S(2)}, u32[]{:S(2)}) collective-permute-start(f32[2,8,256]{2,1,0:T(8,128)S(1)} %pad_maximum_fusion.11), channel_id=1, source_target_pairs={{8,0},{9,1},{10,2},{11,3},{12,4},{13,5},{14,6},{15,7},{16,8},{17,9... | collective-permute-start | bytes 49160 | tf_op jit(solution)/shard_map/ppermute | solution.py:756
  356.4 128.3 %collective-permute-start.45 = (f32[768,2048]{1,0:T(8,128)}, f32[768,2048]{1,0:T(8,128)}, u32[]{:S(2)}, u32[]{:S(2)}) collective-permute-start(f32[768,2048]{1,0:T(8,128)} %get-tuple-element.171), channel_id=1, source_target_pairs={{0,1},{1,0},{2,3},{3,2},{4,5},{5,4},{6,7},{7,6},{8,9},{9,8},{10,11... | collective-permute-start | bytes 18874376 | tf_op jit(solution)/shard_map/ppermute | solution.py:756
  366.6 25.2 %collective-permute-start.62 = (bf16[3,512,128]{2,1,0:T(8,128)(2,1)}, bf16[3,512,128]{2,1,0:T(8,128)(2,1)S(1)}, u32[]{:S(2)}, u32[]{:S(2)}) collective-permute-start(bf16[3,512,128]{2,1,0:T(8,128)(2,1)} %get-tuple-element.199), channel_id=1, source_target_pairs={{0,8},{1,9},{2,10},{3,11},{4,12},{5,13},{6,14},{7,15},{8,0},{9,1},... | collective-permute-start | bytes 1179656 | tf_op jit(solution)/shard_map/ppermute | solution.py:756
  366.6 26.4 %collective-permute-start.60 = (bf16[3,512,128]{2,1,0:T(8,128)(2,1)S(1)}, bf16[3,512,128]{2,1,0:T(8,128)(2,1)S(1)}, u32[]{:S(2)}, u32[]{:S(2)}) collective-permute-start(bf16[3,512,128]{2,1,0:T(8,128)(2,1)S(1)} %get-tuple-element.200), channel_id=1, source_target_pairs={{0,16},{1,17},{2,18},{3,19},{4,20},{5,21},{6,22},{7,23},{8,24},{9,... | collective-permute-start | bytes 1179656 | tf_op jit(solution)/shard_map/ppermute | solution.py:756
  376.6 17.9 %collective-permute-start.48 = (bf16[3,512,128]{2,1,0:T(8,128)(2,1)S(1)}, bf16[3,512,128]{2,1,0:T(8,128)(2,1)S(1)}, u32[]{:S(2)}, u32[]{:S(2)}) collective-permute-start(bf16[3,512,128]{2,1,0:T(8,128)(2,1)S(1)} %get-tuple-element.211), channel_id=1, source_target_pairs={{0,8},{1,9},{2,10},{3,11},{4,12},{5,13},{6,14},{7,15},{8,0},{9,1},... | collective-permute-start | bytes 1179656 | tf_op jit(solution)/shard_map/ppermute | solution.py:756
  377.8 17.9 %collective-permute-start.46 = (bf16[3,512,128]{2,1,0:T(8,128)(2,1)S(1)}, bf16[3,512,128]{2,1,0:T(8,128)(2,1)S(1)}, u32[]{:S(2)}, u32[]{:S(2)}) collective-permute-start(bf16[3,512,128]{2,1,0:T(8,128)(2,1)S(1)} %get-tuple-element.212), channel_id=1, source_target_pairs={{0,16},{1,17},{2,18},{3,19},{4,20},{5,21},{6,22},{7,23},{8,24},{9,... | collective-permute-start | bytes 1179656 | tf_op jit(solution)/shard_map/ppermute | solution.py:756
  394.5 17.7 %collective-permute-start.70 = (bf16[3,512,128]{2,1,0:T(8,128)(2,1)S(1)}, bf16[3,512,128]{2,1,0:T(8,128)(2,1)S(1)}, u32[]{:S(2)}, u32[]{:S(2)}) collective-permute-start(bf16[3,512,128]{2,1,0:T(8,128)(2,1)S(1)} %get-tuple-element.193), channel_id=1, source_target_pairs={{0,8},{1,9},{2,10},{3,11},{4,12},{5,13},{6,14},{7,15},{8,0},{9,1},... | collective-permute-start | bytes 1179656 | tf_op jit(solution)/shard_map/ppermute | solution.py:756
  395.8 35.4 %collective-permute-start.63 = (bf16[3,1024,128]{2,1,0:T(8,128)(2,1)S(1)}, bf16[3,1024,128]{2,1,0:T(8,128)(2,1)S(1)}, u32[]{:S(2)}, u32[]{:S(2)}) collective-permute-start(bf16[3,1024,128]{2,1,0:T(8,128)(2,1)S(1)} %pad_maximum_fusion.6), channel_id=1, source_target_pairs={{0,16},{1,17},{2,18},{3,19},{4,20},{5,21},{6,22},{7,23},{8,24},{9,... | collective-permute-start | bytes 2359304 | tf_op jit(solution)/shard_map/ppermute | solution.py:756
  403.8 26.5 %collective-permute-start.68 = (bf16[3,512,128]{2,1,0:T(8,128)(2,1)S(1)}, bf16[3,512,128]{2,1,0:T(8,128)(2,1)S(1)}, u32[]{:S(2)}, u32[]{:S(2)}) collective-permute-start(bf16[3,512,128]{2,1,0:T(8,128)(2,1)S(1)} %get-tuple-element.194), channel_id=1, source_target_pairs={{0,16},{1,17},{2,18},{3,19},{4,20},{5,21},{6,22},{7,23},{8,24},{9,... | collective-permute-start | bytes 1179656 | tf_op jit(solution)/shard_map/ppermute | solution.py:756
  405.4 27.6 %collective-permute-start.61 = (bf16[3,1024,128]{2,1,0:T(8,128)(2,1)S(1)}, bf16[3,1024,128]{2,1,0:T(8,128)(2,1)S(1)}, u32[]{:S(2)}, u32[]{:S(2)}) collective-permute-start(bf16[3,1024,128]{2,1,0:T(8,128)(2,1)S(1)} %pad_maximum_fusion.5), channel_id=1, source_target_pairs={{0,8},{1,9},{2,10},{3,11},{4,12},{5,13},{6,14},{7,15},{8,0},{9,1},... | collective-permute-start | bytes 2359304 | tf_op jit(solution)/shard_map/ppermute | solution.py:756
  412.2 34.9 %collective-permute-start.49 = (bf16[3,1024,128]{2,1,0:T(8,128)(2,1)S(1)}, bf16[3,1024,128]{2,1,0:T(8,128)(2,1)S(1)}, u32[]{:S(2)}, u32[]{:S(2)}) collective-permute-start(bf16[3,1024,128]{2,1,0:T(8,128)(2,1)S(1)} %pad_maximum_fusion.2), channel_id=1, source_target_pairs={{0,16},{1,17},{2,18},{3,19},{4,20},{5,21},{6,22},{7,23},{8,24},{9,... | collective-permute-start | bytes 2359304 | tf_op jit(solution)/shard_map/ppermute | solution.py:756
  430.3 20.4 %collective-permute-start.47 = (bf16[3,1024,128]{2,1,0:T(8,128)(2,1)S(1)}, bf16[3,1024,128]{2,1,0:T(8,128)(2,1)S(1)}, u32[]{:S(2)}, u32[]{:S(2)}) collective-permute-start(bf16[3,1024,128]{2,1,0:T(8,128)(2,1)S(1)} %pad_maximum_fusion.1), channel_id=1, source_target_pairs={{0,8},{1,9},{2,10},{3,11},{4,12},{5,13},{6,14},{7,15},{8,0},{9,1},... | collective-permute-start | bytes 2359304 | tf_op jit(solution)/shard_map/ppermute | solution.py:756
  431.1 32.9 %collective-permute-start.56 = (bf16[3,1024,128]{2,1,0:T(8,128)(2,1)S(1)}, bf16[3,1024,128]{2,1,0:T(8,128)(2,1)S(1)}, u32[]{:S(2)}, u32[]{:S(2)}) collective-permute-start(bf16[3,1024,128]{2,1,0:T(8,128)(2,1)S(1)} %pad_maximum_fusion.4), channel_id=1, source_target_pairs={{0,16},{1,17},{2,18},{3,19},{4,20},{5,21},{6,22},{7,23},{8,24},{9,... | collective-permute-start | bytes 2359304 | tf_op jit(solution)/shard_map/ppermute | solution.py:756
  433.0 126.0 %collective-permute-start.38 = (f32[4,2,768,128]{3,2,1,0:T(8,128)S(1)}, f32[4,2,768,128]{3,2,1,0:T(8,128)S(1)}, u32[]{:S(2)}, u32[]{:S(2)}) collective-permute-start(f32[4,2,768,128]{3,2,1,0:T(8,128)S(1)} %copy-done.8), channel_id=1, source_target_pairs={{0,1},{1,0},{2,3},{3,2},{4,5},{5,4},{6,7},{7,6},{8,9},{9,8},{10,11... | collective-permute-start | bytes 9437192 | tf_op jit(solution)/shard_map/ppermute | solution.py:756
  447.2 18.9 %collective-permute-start.54 = (bf16[3,1024,128]{2,1,0:T(8,128)(2,1)S(1)}, bf16[3,1024,128]{2,1,0:T(8,128)(2,1)S(1)}, u32[]{:S(2)}, u32[]{:S(2)}) collective-permute-start(bf16[3,1024,128]{2,1,0:T(8,128)(2,1)S(1)} %pad_maximum_fusion.3), channel_id=1, source_target_pairs={{0,8},{1,9},{2,10},{3,11},{4,12},{5,13},{6,14},{7,15},{8,0},{9,1},... | collective-permute-start | bytes 2359304 | tf_op jit(solution)/shard_map/ppermute | solution.py:756
  450.7 28.8 %collective-permute-start.71 = (bf16[3,1024,128]{2,1,0:T(8,128)(2,1)S(1)}, bf16[3,1024,128]{2,1,0:T(8,128)(2,1)S(1)}, u32[]{:S(2)}, u32[]{:S(2)}) collective-permute-start(bf16[3,1024,128]{2,1,0:T(8,128)(2,1)S(1)} %pad_maximum_fusion.8), channel_id=1, source_target_pairs={{0,16},{1,17},{2,18},{3,19},{4,20},{5,21},{6,22},{7,23},{8,24},{9,... | collective-permute-start | bytes 2359304 | tf_op jit(solution)/shard_map/ppermute | solution.py:756
  464.0 16.8 %collective-permute-start.69 = (bf16[3,1024,128]{2,1,0:T(8,128)(2,1)S(1)}, bf16[3,1024,128]{2,1,0:T(8,128)(2,1)S(1)}, u32[]{:S(2)}, u32[]{:S(2)}) collective-permute-start(bf16[3,1024,128]{2,1,0:T(8,128)(2,1)S(1)} %pad_maximum_fusion.7), channel_id=1, source_target_pairs={{0,8},{1,9},{2,10},{3,11},{4,12},{5,13},{6,14},{7,15},{8,0},{9,1},... | collective-permute-start | bytes 2359304 | tf_op jit(solution)/shard_map/ppermute | solution.py:756
  466.1 40.6 %collective-permute-start.64 = (bf16[3,256,128]{2,1,0:T(8,128)(2,1)S(1)}, bf16[3,256,128]{2,1,0:T(8,128)(2,1)S(1)}, u32[]{:S(2)}, u32[]{:S(2)}) collective-permute-start(bf16[3,256,128]{2,1,0:T(8,128)(2,1)S(1)} %get-tuple-element.222), channel_id=1, source_target_pairs={{0,2},{1,3},{2,4},{3,5},{4,6},{5,7},{6,0},{7,1},{8,10},{9,11},{10,... | collective-permute-start | bytes 589832 | tf_op jit(solution)/shard_map/ppermute | solution.py:756
  479.5 27.6 %collective-permute-start.66 = (bf16[3,256,128]{2,1,0:T(8,128)(2,1)S(1)}, bf16[3,256,128]{2,1,0:T(8,128)(2,1)}, u32[]{:S(2)}, u32[]{:S(2)}) collective-permute-start(bf16[3,256,128]{2,1,0:T(8,128)(2,1)S(1)} %get-tuple-element.223), channel_id=1, source_target_pairs={{0,6},{1,7},{2,0},{3,1},{4,2},{5,3},{6,4},{7,5},{8,14},{9,15},{10,... | collective-permute-start | bytes 589832 | tf_op jit(solution)/shard_map/ppermute | solution.py:756
  480.8 28.3 %collective-permute-start.65 = (bf16[3,256,128]{2,1,0:T(8,128)(2,1)S(1)}, bf16[3,256,128]{2,1,0:T(8,128)(2,1)}, u32[]{:S(2)}, u32[]{:S(2)}) collective-permute-start(bf16[3,256,128]{2,1,0:T(8,128)(2,1)S(1)} %get-tuple-element.224), channel_id=1, source_target_pairs={{0,4},{1,5},{2,6},{3,7},{4,0},{5,1},{6,2},{7,3},{8,12},{9,13},{10,... | collective-permute-start | bytes 589832 | tf_op jit(solution)/shard_map/ppermute | solution.py:756
  507.1 21.1 %collective-permute-start.72 = (bf16[3,256,128]{2,1,0:T(8,128)(2,1)S(1)}, bf16[3,256,128]{2,1,0:T(8,128)(2,1)S(1)}, u32[]{:S(2)}, u32[]{:S(2)}) collective-permute-start(bf16[3,256,128]{2,1,0:T(8,128)(2,1)S(1)} %get-tuple-element.219), channel_id=1, source_target_pairs={{0,2},{1,3},{2,4},{3,5},{4,6},{5,7},{6,0},{7,1},{8,10},{9,11},{10,... | collective-permute-start | bytes 589832 | tf_op jit(solution)/shard_map/ppermute | solution.py:756
  509.1 19.1 %collective-permute-start.74 = (bf16[3,256,128]{2,1,0:T(8,128)(2,1)S(1)}, bf16[3,256,128]{2,1,0:T(8,128)(2,1)S(1)}, u32[]{:S(2)}, u32[]{:S(2)}) collective-permute-start(bf16[3,256,128]{2,1,0:T(8,128)(2,1)S(1)} %get-tuple-element.220), channel_id=1, source_target_pairs={{0,6},{1,7},{2,0},{3,1},{4,2},{5,3},{6,4},{7,5},{8,14},{9,15},{10,... | collective-permute-start | bytes 589832 | tf_op jit(solution)/shard_map/ppermute | solution.py:756
  510.7 28.7 %collective-permute-start.73 = (bf16[3,256,128]{2,1,0:T(8,128)(2,1)S(1)}, bf16[3,256,128]{2,1,0:T(8,128)(2,1)S(1)}, u32[]{:S(2)}, u32[]{:S(2)}) collective-permute-start(bf16[3,256,128]{2,1,0:T(8,128)(2,1)S(1)} %get-tuple-element.221), channel_id=1, source_target_pairs={{0,4},{1,5},{2,6},{3,7},{4,0},{5,1},{6,2},{7,3},{8,12},{9,13},{10,... | collective-permute-start | bytes 589832 | tf_op jit(solution)/shard_map/ppermute | solution.py:756
  515.5 28.9 %collective-permute-start.52 = (bf16[3,256,128]{2,1,0:T(8,128)(2,1)S(1)}, bf16[3,256,128]{2,1,0:T(8,128)(2,1)S(1)}, u32[]{:S(2)}, u32[]{:S(2)}) collective-permute-start(bf16[3,256,128]{2,1,0:T(8,128)(2,1)S(1)} %get-tuple-element.229), channel_id=1, source_target_pairs={{0,6},{1,7},{2,0},{3,1},{4,2},{5,3},{6,4},{7,5},{8,14},{9,15},{10,... | collective-permute-start | bytes 589832 | tf_op jit(solution)/shard_map/ppermute | solution.py:756
  528.2 16.2 %collective-permute-start.51 = (bf16[3,256,128]{2,1,0:T(8,128)(2,1)S(1)}, bf16[3,256,128]{2,1,0:T(8,128)(2,1)S(1)}, u32[]{:S(2)}, u32[]{:S(2)}) collective-permute-start(bf16[3,256,128]{2,1,0:T(8,128)(2,1)S(1)} %get-tuple-element.230), channel_id=1, source_target_pairs={{0,4},{1,5},{2,6},{3,7},{4,0},{5,1},{6,2},{7,3},{8,12},{9,13},{10,... | collective-permute-start | bytes 589832 | tf_op jit(solution)/shard_map/ppermute | solution.py:756
  528.2 23.4 %collective-permute-start.57 = (bf16[3,256,128]{2,1,0:T(8,128)(2,1)S(1)}, bf16[3,256,128]{2,1,0:T(8,128)(2,1)S(1)}, u32[]{:S(2)}, u32[]{:S(2)}) collective-permute-start(bf16[3,256,128]{2,1,0:T(8,128)(2,1)S(1)} %get-tuple-element.225), channel_id=1, source_target_pairs={{0,2},{1,3},{2,4},{3,5},{4,6},{5,7},{6,0},{7,1},{8,10},{9,11},{10,... | collective-permute-start | bytes 589832 | tf_op jit(solution)/shard_map/ppermute | solution.py:756
  539.3 13.0 %collective-permute-start.79 = (f32[8,2048]{1,0:T(8,128)S(1)}, f32[8,2048]{1,0:T(8,128)S(1)}, u32[]{:S(2)}, u32[]{:S(2)}) collective-permute-start(f32[8,2048]{1,0:T(8,128)S(1)} %add.247), channel_id=1, source_target_pairs={{0,4},{1,5},{2,6},{3,7},{4,0},{5,1},{6,2},{7,3},{8,12},{9,13},{10,... | collective-permute-start | bytes 196616 | tf_op jit(solution)/shard_map/ppermute | solution.py:756
  (144 other events, 1212.0 us)

commit v2 on v0

v2 whole, which is shorter than its diff:
```python
import functools

import jax
import jax.numpy as jnp
from jax import lax
from jax.experimental import pallas as pl
from jax.experimental.pallas import tpu as pltpu
from jax.sharding import PartitionSpec as P

EPS = 1e-05
F32 = jnp.float32
BF = jnp.bfloat16
STEPS = 16
BLK = 128
GATES = 3
QUARTERS = 4
PARTS = 4


def params(mib, dims=1):
    return pltpu.CompilerParams(
        vmem_limit_bytes=mib * 1024 * 1024, dimension_semantics=("arbitrary",) * dims
    )


def cost(flops, bytes_accessed, transcendentals=0):
    return pl.CostEstimate(
        flops=int(flops), bytes_accessed=int(bytes_accessed), transcendentals=int(transcendentals)
    )


def sds(shape, dtype):
    return jax.ShapeDtypeStruct(shape, dtype)


def far(shape, dtype):
    return pltpu.HBM(shape, dtype)


def near(shape, dtype):
    return pltpu.VMEM(shape, dtype)


def far_in(*values):
    return [pltpu.with_memory_space_constraint(v, pltpu.HBM) for v in values]


def near_in(*values):
    return [pltpu.with_memory_space_constraint(v, pltpu.VMEM) for v in values]


ANY = pl.BlockSpec(memory_space=pl.ANY)
NEAR = pl.BlockSpec(memory_space=pltpu.VMEM)
SMEM = pl.BlockSpec(memory_space=pltpu.SMEM)


def ordered(kernel, deps):
    n = len(deps)

    def body(ids, *refs):
        return kernel(ids, *refs[n:])

    return body, list(deps), [ANY] * n


def call(kernel, name, grid, ids, deps, args, in_specs, out_specs, out_shape, mib, est, scratch=()):
    body, deps, dep_specs = ordered(kernel, deps)
    return pl.pallas_call(
        body,
        grid_spec=pltpu.PrefetchScalarGridSpec(
            num_scalar_prefetch=1,
            grid=grid,
            in_specs=dep_specs + in_specs,
            out_specs=out_specs,
            scratch_shapes=list(scratch),
        ),
        out_shape=out_shape,
        compiler_params=params(mib, len(grid)),
        cost_estimate=est,
        name=name,
    )(ids, *deps, *args)


def call_flat(kernel, name, ids, deps, args, in_specs, out_shape, mib, est, scratch=(), out_specs=None, aliases=None):
    body, deps, dep_specs = ordered(kernel, deps)
    many = isinstance(out_shape, (list, tuple))
    if out_specs is None:
        out_specs = [NEAR] * len(out_shape) if many else NEAR
    shift = 1 + len(deps)
    return pl.pallas_call(
        body,
        in_specs=[SMEM] + dep_specs + in_specs,
        out_specs=out_specs,
        out_shape=out_shape,
        scratch_shapes=list(scratch),
        input_output_aliases={k + shift: v for k, v in (aliases or {}).items()},
        compiler_params=pltpu.CompilerParams(vmem_limit_bytes=mib * 1024 * 1024),
        cost_estimate=est,
        name=name,
    )(ids, *deps, *args)


def split_kernel(ids, w, mine, theirs):
    c = ids[2]
    for s in range(4):
        a, mp = divmod(s, 2)
        for g in range(GATES):
            for mm in range(2):
                dst = s * 768 + g * 256 + mm * BLK
                base = g * 2048 + (2 * mp + mm) * 512 + a * BLK
                here = pl.multiple_of(base + c * 256, BLK)
                there = pl.multiple_of(base + (1 - c) * 256, BLK)
                mine[:, dst : dst + BLK] = w[:, pl.ds(here, BLK)]
                theirs[:, dst : dst + BLK] = w[:, pl.ds(there, BLK)]


def split_weight(ids, weight):
    rows, cols = weight.shape
    tile = rows // 2
    spec = pl.BlockSpec((tile, cols // 2), lambda i, ids: (i, 0))
    return call(
        split_kernel, "split_weight", (2,), ids, (), far_in(weight),
        [pl.BlockSpec((tile, cols), lambda i, ids: (i, 0))], [spec, spec],
        [sds((rows, cols // 2), BF)] * 2, 16, cost(0, rows * cols * 4),
    )


def quarter_kernel(ids, mine, recv, out, p0, p1):
    q, c = ids[0], ids[2]
    half = out.shape[0]
    at = pl.ds(pl.multiple_of(lax.rem(q, 2) * half, half), half)
    first = (lax.div(q, 2) == c).astype(jnp.int32) == 1
    val = jnp.where(first, mine[at, :], recv[at, :])
    out[...] = val[:, 1536:]
    p0[...] = val[:, :768]
    p1[...] = val[:, 768:1536]


def quarter_of(ids, deps, mine, recv):
    rows, cols = mine.shape
    half = rows // 2
    return call_flat(
        quarter_kernel, "quarter_of", ids, deps, [mine, recv], [NEAR, NEAR],
        [sds((half, 1536), BF), sds((half, 768), BF), sds((half, 768), BF)], 16,
        cost(0, rows * cols * 4),
    )


def copy_kernel(ids, src, dst):
    dst[...] = src[...]


def hand_on(ids, deps, value):
    return call_flat(
        copy_kernel, "hand_on", ids, deps, [value], [NEAR], sds(value.shape, value.dtype), 16,
        cost(0, value.size * 4),
    )


def plane_kernel(ids, *refs):
    rel = refs[-1]
    row = 0
    for ref in refs[:-1]:
        rel[row : row + ref.shape[0], :] = ref[...]
        row += ref.shape[0]


def plane_pieces(s, ids, deps, parts):
    rows = sum(p.shape[0] for p in parts)
    return call_flat(
        plane_kernel, f"plane_pieces_{s}", ids, deps, list(parts), [NEAR] * len(parts),
        sds((rows, 768), BF), 16, cost(0, rows * 768 * 4),
    )


def cross_kernel(ids, gx, gy, tox, toy):
    tox[...] = gy[:, :384]
    toy[...] = gx[:, 384:]


def cross_pieces(s, ids, deps, gx, gy):
    rows = gx.shape[0]
    return call_flat(
        cross_kernel, f"cross_pieces_{s}", ids, deps, [gx, gy], [NEAR, NEAR],
        [sds((rows, 384), BF)] * 2, 16, cost(0, rows * 768 * 4),
    )


def norm_of(x):
    mean = jnp.mean(x, axis=-1, keepdims=True)
    centered = x - mean
    var = jnp.mean(centered * centered, axis=-1, keepdims=True)
    rstd = lax.rsqrt(var + EPS)
    return centered * rstd, rstd


def norm_kernel(ids, own, other, gain, bias, ub, ubt, ulo, scr):
    c = ids[2]
    seqs = own.shape[0]
    for k, ref in enumerate((own, other)):
        for st in range(8):
            sq, h = divmod(st, PARTS)
            normed, _ = norm_of(ref[sq, h].astype(F32))
            unit = normed * gain[...] + bias[...]
            for j in range(scr.shape[0]):
                scr[j, pl.ds(k * 128 + st, STEPS, stride=8), :] = unit[:, j * BLK : (j + 1) * BLK]
    for j in range(scr.shape[0]):
        low = scr[j].astype(BF)
        ub[0, :, :, j * BLK : (j + 1) * BLK] = low.reshape(2, 128, BLK)
        ubt[j * BLK : (j + 1) * BLK, :] = low.T
    for a in range(2):
        for m in range(QUARTERS):
            unit = scr[m * 4 + a + 2 * c]
            rest = (unit - unit.astype(BF).astype(F32)).astype(BF)
            dst = (a * QUARTERS + m) * BLK
            ulo[0, :, :, dst : dst + BLK] = rest.reshape(2, 128, BLK)


def tile_block(cols):
    return pl.BlockSpec((1, 2, 128, cols), lambda i, ids: (i, 0, 0, 0))


def norm_tokens(ids, deps, own, other, gain, bias):
    seqs, parts, steps, width = own.shape
    rows = seqs * parts * steps
    tiles = steps // STEPS
    nat = pl.BlockSpec((seqs, parts, STEPS, width), lambda i, ids: (0, 0, i, 0))
    vec = pl.BlockSpec((1, width), lambda i, ids: (0, 0))
    return call(
        norm_kernel, "norm_tokens", (tiles,), ids, deps, [*far_in(own, other), gain, bias],
        [nat, nat, vec, vec],
        [
            tile_block(width),
            pl.BlockSpec((width, 256), lambda i, ids: (0, i)),
            tile_block(width // 2),
        ],
        [
            far((tiles, 2, 128, width), BF),
            far((width, 2 * rows), BF),
            far((tiles, 2, 128, width // 2), BF),
        ],
        20, cost(rows * width * 20, rows * width * 14),
        scratch=[pltpu.VMEM((width // BLK, 256, BLK), F32)],
    )


def flat(ref):
    value = ref[...]
    return value.reshape(256, value.shape[-1])


def core_lane(a, m, c):
    return pl.multiple_of(m * 512 + a * BLK + c * 256, BLK)


def pairs():
    for tp in range(STEPS // 2):
        for k in range(2):
            yield k, tp * 16, k * 128 + tp * 16


def live_pair(lim, row, tile):
    live = lim[row : row + 16, :] > tile * STEPS
    return jnp.concatenate([live, live], axis=1)


def fold_streams(pr, lc, ahead):
    out = []
    order = range(PARTS) if ahead else range(PARTS - 1, -1, -1)
    for sq in range(2):
        tp = tl = None
        for h in order:
            n = sq * PARTS + h
            p, l = pr[n : n + 1], lc[n : n + 1]
            tp, tl = (p, l) if tp is None else ((p * tp, p * tl + l) if ahead else (p * tp, l + p * tl))
        out.append((tp, tl))
    return out


def proj_kernel(s, nz, joined, ids, ub, ulo, *rest):
    n_w = 1 if joined else 7
    weights, rest = rest[:n_w], rest[n_w:]
    lim, vf, bfor = rest[:3]
    rest = rest[3:]
    before = rest[0] if s % 2 else None
    cand, decay, rpre, plout, summ = rest[s % 2 : s % 2 + 5]
    rest = rest[s % 2 + 5 :]
    if joined:
        zbuf, prod, loc, wbuf, sems = rest
    else:
        wall, zbuf, prod, loc, wbuf, sems = rest
    tiles = cand.shape[0]
    width = wbuf.shape[0]
    q, z, c = ids[0], ids[1], ids[2]
    a, mp = divmod(s, 2)
    cols = slice(mp * 768, mp * 768 + 768)
    copies = []

    def put(src, row, rows, lo=0, hi=768):
        dst = wbuf.at[pl.ds(row, rows), lo:hi]
        copy = pltpu.make_async_copy(src, dst, sems.at[len(copies)])
        copy.start()
        copies.append(copy)

    if joined:
        put(weights[0].at[:, cols], 0, width)
    else:
        mine, recv, rel, gx, gy, dx, dy = weights
        zb = width // nz
        zb2, qb = zb // 2, zb // 4
        mult = lambda v: pl.multiple_of(v, qb)
        put(mine.at[:, s * 768 : (s + 1) * 768], mult(z * zb + c * zb2), zb2)
        put(recv.at[:, s * 768 : (s + 1) * 768], mult(z * zb + (1 - c) * zb2), zb2)
        for r in range(1, nz):
            base = lax.rem(z + r, nz) * zb
            lo, hi = (r - 1) * qb, r * qb
            put(rel.at[lo:hi, :], mult(base + q * qb), qb)
            put(gx.at[lo:hi, :], mult(base + (q ^ 1) * qb), qb)
            put(gy.at[lo:hi, :], mult(base + (q ^ 2) * qb), qb)
            put(dx.at[lo:hi, :], mult(base + (q ^ 3) * qb), qb, 0, 384)
            put(dy.at[lo:hi, :], mult(base + (q ^ 3) * qb), qb, 384, 768)
    for copy in copies:
        copy.wait()
    if not joined:
        keep = pltpu.make_async_copy(wbuf, wall, sems.at[len(copies)])
        keep.start()
    prod[...] = jnp.ones_like(prod)
    loc[...] = jnp.zeros_like(loc)

    def tile(ubr, ulor):
        i = pl.program_id(0)
        zbuf[:, :768] = jnp.dot(flat(ubr), wbuf[...], preferred_element_type=F32)
        low = flat(ulor).astype(F32)
        for mm in range(2):
            high = ubr[:, :, :, pl.ds(core_lane(a, 2 * mp + mm, c), BLK)].reshape(256, BLK)
            zbuf[:, 768 + mm * BLK : 768 + (mm + 1) * BLK] = (
                high.astype(F32) + low[:, mm * BLK : (mm + 1) * BLK]
            )
        pr = [prod[0:8, :], prod[8:16, :]]
        lc = [loc[0:8, :], loc[8:16, :]]
        for k, r0, row in pairs():
            cd = zbuf[row : row + 16, :256]
            logit = zbuf[row : row + 16, 256:512] + vf[...] * zbuf[row : row + 16, 768:] + bfor[...]
            dec = jnp.where(live_pair(lim, row, i), jax.nn.sigmoid(logit), 1.0)
            inj = (1.0 - dec) * cd
            cand[i, k, r0 : r0 + 16, :] = cd
            decay[i, k, r0 : r0 + 16, :] = dec
            rpre[i, k, r0 : r0 + 16, :] = zbuf[row : row + 16, 512:768]
            for t in range(2):
                d = dec[t * 8 : t * 8 + 8]
                lc[k] = d * lc[k] + inj[t * 8 : t * 8 + 8]
                pr[k] = d * pr[k]
        for k in range(2):
            prod[k * 8 : k * 8 + 8, :] = pr[k]
            loc[k * 8 : k * 8 + 8, :] = lc[k]

    pltpu.emit_pipeline(
        tile,
        grid=(tiles,),
        in_specs=[
            pl.BlockSpec((1, 2, 128, width), lambda i: (i, 0, 0, 0)),
            pl.BlockSpec((1, 2, 128, 256), lambda i: (i, 0, 0, s)),
        ],
    )(ub, ulo)
    if s % 2:
        summ[0] = before[0]
    plout[0:16, :] = prod[...]
    plout[16:32, :] = loc[...]
    for k in range(2):
        pr, lc = prod[k * 8 : k * 8 + 8, :], loc[k * 8 : k * 8 + 8, :]
        for sq, (tp, tl) in enumerate(fold_streams(pr, lc, True)):
            ks = k * 2 + sq
            summ[s % 2, ks : ks + 1, :] = tp
            summ[s % 2, 4 + ks : 5 + ks, :] = tl
    if not joined:
        keep.wait()


def project(s, nz, ids, deps, ub, ulo, weights, lim, vf, bfor, before):
    tiles, _, _, width = ub.shape
    joined = len(weights) == 1
    shape = (tiles, 2, 128, 256)
    rows = tiles * 256
    chan = slice(s * 256, s * 256 + 256)
    args = far_in(ub, ulo, *weights) + [lim, vf[:, chan], bfor[:, chan]]
    in_specs = [ANY] * (2 + len(weights)) + [NEAR] * 3
    if s % 2:
        args.append(before)
        in_specs.append(NEAR)
    out_shape = [near(shape, F32)] * 3 + [sds((32, 256), F32), sds((2, 8, 256), F32)]
    out_specs = [NEAR] * 5
    if not joined:
        out_shape.append(far((width, 768), BF))
        out_specs.append(ANY)
    return call_flat(
        functools.partial(proj_kernel, s, nz, joined), f"project_{s}", ids, deps, args, in_specs,
        out_shape, 16, cost(2 * rows * width * 768, rows * width * 2 + width * 768 * 4),
        scratch=[
            pltpu.VMEM((256, 1024), F32),
            pltpu.VMEM((16, 256), F32),
            pltpu.VMEM((16, 256), F32),
            pltpu.VMEM((width, 768), BF),
            pltpu.SemaphoreType.DMA((3 + 5 * (nz - 1),)),
        ],
        out_specs=out_specs,
    )


def halves(v):
    return v[:8], v[8:]


def enter(got, n, ahead, q, count):
    value = jnp.zeros((4, 256), F32)
    for j in range(count) if ahead else range(count - 1, -1, -1):
        used = (j < q) if ahead else (j > q)
        longer = got[j, n, 4:8, :] + got[j, n, 0:4, :] * value
        value = jnp.where(used, longer, value)
    return value


def state_kernel(a, count, held, ids, *refs):
    fwd = (refs[0:4], refs[4:8])
    ub, cot_own, cot_oth, lim, scl, vr, br, got = refs[8:16]
    rest = refs[16 + (2 if held else 0) :]
    hown, hoth = rest[:2]
    out = (rest[2:6], rest[6:10])
    dzr, uu, lbs, summ, acc, st, pp, lb, ac, scr = rest[10:]
    tiles = dzr.shape[0]
    q, c = ids[0], ids[2]
    for n in range(2):
        cand, decay, rpre, plin = fwd[n]
        bc, src, dstate, du0 = out[n]
        lanes = slice(n * 256, n * 256 + 256)
        carry = enter(got, n, True, q, count)
        for ks in range(4):
            cc = carry[ks : ks + 1]
            for h in range(PARTS):
                m = ks * PARTS + h
                st[m : m + 1, :] = cc
                cc = plin[m : m + 1, :] * cc + plin[16 + m : 17 + m, :]
        pp[...] = jnp.ones_like(pp)
        lb[...] = jnp.zeros_like(lb)
        ac[...] = jnp.zeros_like(ac)

        def tile(u0, u1, own0, own1, oth0, oth1, ho, ht):
            i = pl.program_id(0)
            for k, pair in enumerate(((own0, own1), (oth0, oth1))):
                for b, ref in enumerate(pair):
                    for m in range(8):
                        sq, h = divmod(m, PARTS)
                        scr[b, pl.ds(k * 128 + m, STEPS, stride=8), :] = ref[sq, h].astype(F32)
            cur = [st[0:8, :], st[8:16, :]]
            p = [pp[0:8, :], pp[8:16, :]]
            l = [lb[0:8, :], lb[8:16, :]]
            peep = [jnp.zeros((8, 256), F32)] * 2
            bias = [jnp.zeros((8, 256), F32)] * 2
            wr, wb = vr[:, lanes], br[:, lanes]
            for k, r0, row in pairs():
                at = slice(r0, r0 + 16)
                dec = decay[i, k, at, :]
                cd = cand[i, k, at, :]
                inj = (1.0 - dec) * cd
                befores, states = [], []
                for d, v in zip(halves(dec), halves(inj)):
                    befores.append(cur[k])
                    cur[k] = d * cur[k] + v
                    states.append(cur[k])
                before = jnp.concatenate(befores, axis=0)
                state = jnp.concatenate(states, axis=0)
                low = jnp.concatenate([u0[0, k, at, :], u1[0, k, at, :]], axis=1)
                uu[i, k, at, lanes] = low
                u = low.astype(F32)
                live = lim[row : row + 16, :] > i * STEPS
                sc = jnp.where(live, scl[row : row + 16, :], 0.0)
                gy = jnp.concatenate(
                    [scr[0, row : row + 16, :] * sc, scr[1, row : row + 16, :] * sc], axis=1
                )
                r = jax.nn.sigmoid(rpre[i, k, at, :] + wr * before + wb)
                gap = state - u
                hv = jnp.where(jnp.concatenate([live, live], axis=1), u + r * gap, 0.0).astype(BF)
                href = ht if k else ho
                href[0, 0, at, :] = hv[:, :BLK]
                href[0, 1, at, :] = hv[:, BLK:]
                ds = gy * r
                drl = ds * (1.0 - r) * gap
                sr = dec * ds + wr * drl
                dstate[i, k, at, :] = ds
                src[i, k, at, :] = sr
                bc[i, k, at, :] = before - cd
                du0[i, k, at, :] = gy - ds
                dzr[i, k, at, lanes] = drl.astype(BF)
                for d, v in zip(halves(dec), halves(sr)):
                    l[k] = l[k] + p[k] * v
                    p[k] = p[k] * d
                for e, w in zip(halves(drl), befores):
                    peep[k] = peep[k] + e * w
                    bias[k] = bias[k] + e
            for k in range(2):
                st[k * 8 : k * 8 + 8, :] = cur[k]
                pp[k * 8 : k * 8 + 8, :] = p[k]
                lb[k * 8 : k * 8 + 8, :] = l[k]
            ac[0:8, :] += peep[0] + peep[1]
            ac[8:16, :] += bias[0] + bias[1]

        nat = cot_own.shape[:2]

        def unit(mm):
            return pl.BlockSpec(
                (1, 2, 128, BLK), lambda i: (i, 0, 0, (2 * n + mm) * 4 + 2 * c + a)
            )

        def nat_own(mm):
            return pl.BlockSpec(
                (*nat, STEPS, BLK), lambda i: (0, 0, i, (2 * n + mm) * 4 + 2 * c + a)
            )

        def nat_oth(mm):
            return pl.BlockSpec((*nat, STEPS, BLK), lambda i: (0, 0, i, (2 * n + mm) * 2 + a))

        hspec = pl.BlockSpec((1, 2, 128, BLK), lambda i: (2 * a + n, 0, i, 0))
        pltpu.emit_pipeline(
            tile,
            grid=(tiles,),
            in_specs=[unit(0), unit(1), nat_own(0), nat_own(1), nat_oth(0), nat_oth(1)],
            out_specs=[hspec, hspec],
        )(ub, ub, cot_own, cot_own, cot_oth, cot_oth, hown, hoth)
        acc[n] = ac[...]
        lbs[n] = lb[...]
        for k in range(2):
            p, l = pp[k * 8 : k * 8 + 8, :], lb[k * 8 : k * 8 + 8, :]
            for sq, (tp, tl) in enumerate(fold_streams(p, l, False)):
                ks = k * 2 + sq
                summ[n, ks : ks + 1, :] = tp
                summ[n, 4 + ks : 5 + ks, :] = tl


def states(a, count, ids, deps, fwd, ub, cot_own, cot_oth, lim, scl, vr, br, got, held):
    tiles = ub.shape[0]
    rows = tiles * 128
    one = (tiles, 2, 128, 256)
    two = (tiles, 2, 128, 512)
    chan = slice(a * 512, a * 512 + 512)
    args, in_specs = [], []
    for f in fwd:
        args += near_in(*f[:3]) + [f[3]]
        in_specs += [NEAR] * 4
    args += far_in(ub, cot_own, cot_oth) + [lim, scl, vr[:, chan], br[:, chan], got]
    in_specs += [ANY] * 3 + [NEAR] * 5
    aliases = {}
    if held:
        aliases = {len(args): 0, len(args) + 1: 1}
        args += far_in(*held)
        in_specs += [ANY] * 2
    small = sds((2, 16, 256), F32)
    return call_flat(
        functools.partial(state_kernel, a, count, bool(held)), f"states_{a}", ids, deps, args,
        in_specs,
        [far((4, 2, rows, BLK), BF)] * 2
        + [near(one, F32)] * 8
        + [near(two, BF)] * 2
        + [small, sds((2, 8, 256), F32), small],
        16, cost(rows * 1024 * 60, rows * 1024 * 10, rows * 1024 * 2),
        scratch=[pltpu.VMEM((16, 256), F32)] * 4 + [pltpu.VMEM((2, 256, BLK), F32)],
        out_specs=[ANY] * 2 + [NEAR] * 13,
        aliases=aliases,
    )


def adjoint_kernel(count, ids, *refs):
    ins = (refs[0:6], refs[6:12])
    uu, vf, lbs, got, du, dzc, dzf, acc, adj = refs[12:]
    tiles = du.shape[0]
    q = ids[0]
    for n in range(2):
        decay, bc, src, dstate, du0, plin = ins[n]
        lanes = slice(n * 256, n * 256 + 256)
        wf = vf[:, lanes]
        after = enter(got, n, False, q, count)
        for ks in range(4):
            cc = after[ks : ks + 1]
            for h in range(PARTS - 1, -1, -1):
                m = ks * PARTS + h
                adj[m : m + 1, :] = cc
                cc = lbs[n, m : m + 1, :] + plin[m : m + 1, :] * cc

        def tile(step, state):
            i = tiles - 1 - step
            cur, peep, bias = [state[0], state[1]], state[2], state[3]
            for k, r0, _ in reversed(list(pairs())):
                at = slice(r0, r0 + 16)
                dec = decay[i, k, at, :]
                ds = dstate[i, k, at, :]
                sr = src[i, k, at, :]
                late = ds[8:] + cur[k]
                cur[k] = dec[8:] * cur[k] + sr[8:]
                early = ds[:8] + cur[k]
                cur[k] = dec[:8] * cur[k] + sr[:8]
                dcand = jnp.concatenate([early, late], axis=0) * (1.0 - dec)
                dfl = dcand * bc[i, k, at, :] * dec
                dzc[i, k, at, lanes] = dcand.astype(BF)
                dzf[i, k, at, lanes] = dfl.astype(BF)
                du[i, k, at, lanes] = du0[i, k, at, :] + dfl * wf
                w = dfl * uu[i, k, at, lanes].astype(F32)
                peep = peep + (w[:8] + w[8:])
                bias = bias + (dfl[:8] + dfl[8:])
            return cur[0], cur[1], peep, bias

        zero = jnp.zeros((8, 256), F32)
        end = lax.fori_loop(0, tiles, tile, (adj[0:8, :], adj[8:16, :], zero, zero))
        acc[n, 0:8, :] = end[2]
        acc[n, 8:16, :] = end[3]


def adjoints(a, count, ids, deps, fwd, mid, uu, vf, lbs, got):
    tiles = uu.shape[0]
    rows = tiles * 128
    shape = (tiles, 2, 128, 512)
    args = []
    for f, m in zip(fwd, mid):
        args += near_in(f[1], *m) + [f[3]]
    args += near_in(uu) + [vf[:, a * 512 : a * 512 + 512], lbs, got]
    return call_flat(
        functools.partial(adjoint_kernel, count), f"adjoints_{a}", ids, deps, args,
        [NEAR] * len(args),
        [near(shape, F32), near(shape, BF), near(shape, BF), sds((2, 16, 256), F32)],
        16, cost(rows * 1024 * 20, rows * 1024 * 4), scratch=[pltpu.VMEM((16, 256), F32)],
    )


def wgrad_kernel(which, nz, ids, ubt, dzc, dzf, dzr, own, xp, yp, da, db, scr):
    q, c = ids[0], ids[2]
    rh = 1 - c if which == "other" else c
    half = scr.shape[0]
    rows = ubt.shape[1]

    def tile(lhs):
        i = pl.program_id(0)
        for g, dz in enumerate((dzc, dzf, dzr)):
            rhs = dz[...].reshape(rows, 512)
            scr[:, g * 512 : (g + 1) * 512] = jnp.dot(
                lhs[...], rhs, preferred_element_type=F32
            ).astype(BF)

        def block(r, j):
            return scr[:, pl.ds(pl.multiple_of(((q ^ r) * 3 + j) * BLK, BLK), BLK)]

        at = pl.ds(pl.multiple_of(i * half, half), half)
        for j in range(3):
            own[j, at, :] = block(0, j)
            xp[j, at, :] = block(1, j)
            yp[j, at, :] = block(2, j)

        @pl.when(i < nz // 2)
        def _():
            for j in range(3):
                da[j, at, :] = block(3, j)

        @pl.when(i >= nz // 2)
        def _():
            back = pl.ds(pl.multiple_of((i - nz // 2) * half, half), half)
            for j in range(3):
                db[j, back, :] = block(3, j)

    pltpu.emit_pipeline(
        tile, grid=(nz,), in_specs=[pl.BlockSpec((half, rows), lambda i: (2 * i + rh, 0))]
    )(ubt)


def weight_grad_part(which, nz, ids, deps, ubt, dz):
    width, rows = ubt.shape
    half = width // nz // 2
    return call_flat(
        functools.partial(wgrad_kernel, which, nz), "weight_grad_part", ids, deps,
        [*far_in(ubt), *near_in(*dz)], [ANY] + [NEAR] * 3,
        [sds((3, nz * half, BLK), BF)] * 3 + [sds((3, nz * half // 2, BLK), BF)] * 2,
        16, cost(2 * rows * nz * half * 1536, rows * width + width * 1536),
        scratch=[pltpu.VMEM((half, 1536), BF)],
    )


def relay_kernel(ids, xp, yp, ra, rb, s1, s2):
    half = ra.shape[1]
    s1[:, :half, :] = xp[:, :half, :]
    s1[:, half:, :] = (xp[:, half:, :].astype(F32) + rb[...].astype(F32)).astype(BF)
    s2[:, :half, :] = (yp[:, :half, :].astype(F32) + ra[...].astype(F32)).astype(BF)
    s2[:, half:, :] = yp[:, half:, :]


def relay_sums(ids, deps, xp, yp, ra, rb):
    rows = xp.shape[1]
    return call_flat(
        relay_kernel, "relay_sums", ids, deps, [xp, yp, ra, rb], [NEAR] * 4,
        [sds(xp.shape, BF)] * 2, 16, cost(rows * 768, rows * 384 * 10),
    )


def plane_sum_kernel(nz, ids, own, r1, r2, *outs):
    rows = outs[0].shape[1]
    for k, out in enumerate(outs):
        start = lax.rem(ids[1] + k, nz) * rows
        at = pl.ds(pl.multiple_of(start, rows), rows)
        tot = own[:, at, :].astype(F32) + r1[:, at, :].astype(F32) + r2[:, at, :].astype(F32)
        out[...] = tot.astype(out.dtype)


def plane_sums(nz, ids, deps, own, r1, r2):
    rows = own.shape[1] // nz
    return call_flat(
        functools.partial(plane_sum_kernel, nz), "plane_sums", ids, deps, [own, r1, r2], [NEAR] * 3,
        [sds((3, rows, BLK), F32)] + [sds((3, rows, BLK), BF)] * (nz - 1), 16,
        cost(rows * 768 * nz, rows * 384 * 8 * nz),
    )


def total_kernel(ids, *refs):
    total = refs[0][...].astype(F32)
    for ref in refs[1:-1]:
        total = total + ref[...].astype(F32)
    refs[-1][...] = total


def total_of(ids, deps, parts):
    return call_flat(
        total_kernel, "total_of", ids, deps, list(parts), [NEAR] * len(parts),
        sds(parts[0].shape, F32), 16, cost(parts[0].size * 4, parts[0].size * 14),
    )


DIMS = (((1,), (1,)), ((), ()))
TILE_N = 512


def unit_kernel(k, ids, c0, f0, r0, c1, f1, r1, e0, e1, w0, w1, w2, out, lhs, acc):
    c = ids[2]
    rows = acc.shape[0]
    for a, refs in enumerate(((c0, f0, r0), (c1, f1, r1))):
        for mp in range(2):
            for g, ref in enumerate(refs):
                dst = a * 1536 + mp * 768 + g * 256
                val = ref[:, k, :, mp * 256 : (mp + 1) * 256]
                lhs[:, dst : dst + 256] = val.reshape(rows, 256)

    def tile(wa, wb, wc):
        m = pl.program_id(0)
        acc[:, :TILE_N] = lax.dot_general(
            lhs[:, :768], wa[...], DIMS, preferred_element_type=F32
        ) + lax.dot_general(lhs[:, 768:1536], wb[...], DIMS, preferred_element_type=F32)
        acc[:, :TILE_N] += lax.dot_general(lhs[:, 1536:], wc[...], DIMS, preferred_element_type=F32)
        for a, ref in enumerate((e0, e1)):
            val = ref[:, k, :, pl.ds(pl.multiple_of(m * BLK, BLK), BLK)]
            acc[:, pl.ds(core_lane(a, 0, c), BLK)] += val.reshape(rows, BLK)
        out[:, pl.ds(pl.multiple_of(m * TILE_N, TILE_N), TILE_N)] = acc[...].astype(out.dtype)

    blk = lambda w: pl.BlockSpec((TILE_N, w.shape[1]), lambda i: (i, 0))
    pltpu.emit_pipeline(
        tile, grid=(w0.shape[0] // TILE_N,), in_specs=[blk(w0), blk(w1), blk(w2)]
    )(w0, w1, w2)


def unit_grads(k, ids, deps, dz0, dz1, e0, e1, ws):
    tiles = e0.shape[0]
    rows, width = tiles * 128, ws[0].shape[0]
    return call_flat(
        functools.partial(unit_kernel, k), f"unit_grads_{k}", ids, deps,
        [*near_in(*dz0, *dz1, e0, e1), *far_in(*ws)], [NEAR] * 8 + [ANY] * 3,
        near((rows, width), BF if k else F32), 24,
        cost(2 * rows * width * 3072, width * 3072 * 2),
        scratch=[pltpu.VMEM((rows, 3072), BF), pltpu.VMEM((rows, TILE_N), F32)],
    )


def norm_grad_kernel(ids, du_own, recv, tok, cot, lim, scl, gain, *rest):
    accb, accc = rest[:2], rest[2:4]
    out, sums, ga, ba, scr = rest[4:]
    c = ids[2]
    ga[...] = jnp.zeros_like(ga)
    ba[...] = jnp.zeros_like(ba)

    def tile(tokr, cotr, outr):
        i = pl.program_id(0)
        rows = pl.ds(pl.multiple_of(i * 128, 128), 128)
        for j in range(scr.shape[0]):
            lanes = slice(j * BLK, (j + 1) * BLK)
            scr[j] = du_own[rows, lanes] + recv[rows, lanes].astype(F32)
        step = lax.broadcasted_iota(jnp.int32, (STEPS, 1), 0) + i * STEPS
        gsum = jnp.zeros(ga.shape, F32)
        bsum = jnp.zeros(ba.shape, F32)
        for st in range(8):
            sq, h = divmod(st, PARTS)
            x16 = tokr[sq, h].astype(F32)
            c16 = cotr[sq, h].astype(F32)
            for part in range(2):
                cut = slice(part * 8, part * 8 + 8)
                du = jnp.concatenate(
                    [scr[j, pl.ds(st + part * 64, 8, stride=8), :] for j in range(scr.shape[0])],
                    axis=1,
                )
                normed, rstd = norm_of(x16[cut])
                dn = du * gain[...]
                m1 = jnp.mean(dn, axis=-1, keepdims=True)
                m2 = jnp.mean(dn * normed, axis=-1, keepdims=True)
                gy = jnp.where(step[cut] < lim[st], c16[cut] * scl[0], 0.0)
                outr[sq, h, cut, :] = rstd * (dn - m1 - normed * m2) + gy
                gsum = gsum + du * normed
                bsum = bsum + du
        ga[...] += gsum
        ba[...] += bsum

    seqs, parts, steps, width = tok.shape
    nat = pl.BlockSpec((seqs, parts, STEPS, width), lambda i: (0, 0, i, 0))
    pltpu.emit_pipeline(
        tile, grid=(steps // STEPS,), in_specs=[nat, nat], out_specs=[nat]
    )(tok, cot, out)
    sums[...] = jnp.zeros_like(sums)
    sums[4:5, :] = jnp.sum(ga[...], axis=0, keepdims=True)
    sums[5:6, :] = jnp.sum(ba[...], axis=0, keepdims=True)
    for s in range(4):
        a, mp = divmod(s, 2)
        rows = (
            accc[a][mp, 0:8, :],
            accb[a][mp, 0:8, :],
            accc[a][mp, 8:16, :],
            accb[a][mp, 8:16, :],
        )
        for j, val in enumerate(rows):
            val = jnp.sum(val, axis=0, keepdims=True)
            for mm in range(2):
                lane = pl.ds(core_lane(a, 2 * mp + mm, c), BLK)
                sums[j : j + 1, lane] = val[:, mm * BLK : (mm + 1) * BLK]


def norm_grads(ids, deps, du_own, recv, tok, cot, lim8, scale, gain, accb, accc):
    rows, width = du_own.shape
    n = rows * width
    return call_flat(
        norm_grad_kernel, "norm_grads", ids, deps,
        [*near_in(du_own, recv), *far_in(tok, cot), lim8, scale, gain, *accb, *accc],
        [NEAR] * 2 + [ANY] * 2 + [SMEM] * 2 + [NEAR] * 5,
        [far(tok.shape, F32), sds((8, width), F32)], 20, cost(n * 20, n * 8),
        scratch=[
            pltpu.VMEM((8, width), F32),
            pltpu.VMEM((8, width), F32),
            pltpu.VMEM((width // BLK, 128, BLK), F32),
        ],
        out_specs=[ANY, NEAR],
    )


def activation_kernel(ids, tok, hown, hrcv, out, scr):
    c = ids[2]
    for s in range(4):
        a, mp = divmod(s, 2)
        for mm in range(2):
            for n, (ref, core) in enumerate(((hown, c), (hrcv, 1 - c))):
                scr[n] = ref[s, mm].astype(F32)
                lane = pl.ds(core_lane(a, 2 * mp + mm, core), BLK)
                for st in range(8):
                    sq, h = divmod(st, PARTS)
                    val = scr[n, pl.ds(st, STEPS, stride=8), :]
                    out[sq, h, :, lane] = tok[sq, h, :, lane].astype(F32) + val


def activations_of(ids, deps, tok, hown, hrcv):
    seqs, parts, steps, width = tok.shape
    tiles = steps // STEPS
    nat = pl.BlockSpec((seqs, parts, STEPS, width), lambda i, ids: (0, 0, i, 0))
    hspec = pl.BlockSpec((4, 2, 128, BLK), lambda i, ids: (0, 0, i, 0))
    n = seqs * parts * steps * width
    return call(
        activation_kernel, "activations_of", (tiles,), ids, deps, far_in(tok, hown, hrcv),
        [nat, hspec, hspec], nat, far(tok.shape, F32), 16, cost(n, n * 8),
        scratch=[pltpu.VMEM((2, 128, BLK), F32)],
    )


def assemble_kernel(counts, ids, *refs):
    out = refs[-1]
    c = ids[2]
    start = 0
    for b, n in enumerate(counts):
        group = refs[start : start + n]
        start += n
        a, core = b % 2, c if b < 2 else 1 - c
        for j in range(3):
            total = group[0][j]
            for ref in group[1:]:
                total = total + ref[j].astype(F32)
            lane = pl.multiple_of(j * 512 + a * BLK + core * 256, BLK)
            out[:, pl.ds(lane, BLK)] = total


def assemble(ids, deps, groups):
    rows = groups[0][0].shape[1]
    counts = [len(g) for g in groups]
    args = [ref for group in groups for ref in group]
    return call_flat(
        functools.partial(assemble_kernel, counts), "assemble", ids, deps, args,
        [NEAR] * len(args), sds((rows, 1536), F32), 16, cost(0, rows * 1536 * 8),
    )


def local(
    nseq,
    ndp,
    tokens,
    cotangent,
    weight,
    forget_peep,
    reset_peep,
    forget_bias,
    reset_bias,
    norm_gain,
    norm_bias,
    lengths,
):
    axes = ("seq", "dp")
    nz = ndp // 2
    seqs, span, width = tokens.shape
    sub = span // PARTS
    q = lax.axis_index("seq").astype(jnp.int32)
    dp = lax.axis_index("dp").astype(jnp.int32)
    z, c = dp // 2, dp % 2
    ids = jnp.stack([q, z, c])

    def table(move):
        pairs = []
        for qq in range(nseq):
            for zz in range(nz):
                for cc in range(2):
                    to = move(qq, zz, cc)
                    if to is not None:
                        pairs.append((qq * ndp + zz * 2 + cc, to[0] * ndp + to[1] * 2 + to[2]))
        return pairs

    def send(value, move):
        return lax.ppermute(value, axes, table(move))

    def to_core(qq, zz, cc):
        return (qq, zz, 1 - cc)

    def to_x(qq, zz, cc):
        return (qq ^ 1, zz, cc)

    def to_y(qq, zz, cc):
        return (qq ^ 2, zz, cc)

    def shift_z(k):
        return lambda qq, zz, cc: (qq, (zz + k) % nz, cc)

    def shift_zc(k):
        return lambda qq, zz, cc: (qq, (zz + k) % nz, 1 - cc)

    def shift_q(k):
        return lambda qq, zz, cc: (qq + k, zz, cc) if 0 <= qq + k < nseq else None

    mine, theirs = split_weight(ids, weight)
    recv = send(theirs, to_core)
    nat = (seqs, PARTS, sub, width)
    tok4 = tokens.reshape(nat)
    cot4 = cotangent.reshape(nat)
    tok_oth = send(tokens, to_core).reshape(nat)
    cot_cols = jnp.concatenate(
        [lax.dynamic_slice_in_dim(cotangent, m * 512 + (1 - c) * 256, 256, 2) for m in range(4)],
        axis=2,
    )
    cot_oth = send(cot_cols, to_core).reshape(seqs, PARTS, sub, width // 2)
    len_oth = send(lengths, to_core)

    lens = jnp.stack([lengths, len_oth])
    counts = jnp.sum(lens, axis=1).astype(F32)
    scale = (seqs * span * nseq) / counts
    lim16 = (
        lens[:, :, None] - q * span - sub * jnp.arange(PARTS, dtype=jnp.int32)[None, None, :]
    ).reshape(2, 8)
    spread_rows = lambda v: jnp.broadcast_to(v, (2, STEPS, 8, BLK)).reshape(256, BLK)
    step_in_tile = jnp.arange(STEPS, dtype=jnp.int32)[None, :, None, None]
    lim = spread_rows(lim16[:, None, :, None] - step_in_tile)
    scl = spread_rows(scale[:, None, None, None])

    def by_core(vec):
        v = lax.dynamic_slice_in_dim(vec.reshape(4, 4, BLK), 2 * c, 2, 1)
        return v.transpose(1, 0, 2).reshape(1, width // 2)

    vf, vr, bfor, brst = (by_core(v) for v in (forget_peep, reset_peep, forget_bias, reset_bias))
    gain, bias = norm_gain.reshape(1, width), norm_bias.reshape(1, width)

    tail = [mine]

    def run(kernel, *head, rest=(), token=-1, after=()):
        out = kernel(*head, ids, (tail[0], *after), *rest)
        tail[0] = out[token] if isinstance(out, (list, tuple)) else out
        return out

    groups = [[cc + 2 * zz for zz in range(nz)] for cc in range(2)]

    def along_z(piece):
        if nz <= 4:
            return [send(piece, shift_z(-k)) for k in range(1, nz)]
        got = lax.all_gather(piece, "dp", axis=0, tiled=True, axis_index_groups=groups)
        n = got.shape[0] // nz
        twice = jnp.concatenate([got, got], axis=0)
        return [lax.dynamic_slice_in_dim(twice, (z + 1) * n, n * (nz - 1), 0)]

    def gather_1(s, zs):
        rel = run(plane_pieces, s, rest=(zs,))
        return rel, send(rel, to_x), send(rel, to_y)

    def gather_2(s, got):
        rel, gx, gy = got
        tox, toy = run(cross_pieces, s, rest=(gx, gy))
        return rel, gx, gy, send(tox, to_x), send(toy, to_y)

    def spread(both):
        return lax.all_gather(both, "seq")

    def run_project(s, weights, before=None, after=()):
        rest = (ub, ulo, weights, lim, vf, bfor, before)
        return run(project, s, nz, rest=rest, token=4, after=after)

    def run_states(a, fwd, got, held, after=()):
        rest = (fwd, ub, cot4, cot_oth, lim, scl, vr, brst, got, held)
        out = run(states, a, nseq, rest=rest, after=after)
        return {
            "h": out[:2], "mid": (out[2:6], out[6:10]), "dzr": out[10], "u": out[11],
            "lbs": out[12], "summ": out[13], "acc": out[14],
        }

    def run_adjoints(a, fwd, m, got, after=()):
        rest = (fwd, m["mid"], m["u"], vf, m["lbs"], got)
        du, dzc, dzf, acc = run(adjoints, a, nseq, rest=rest, after=after)
        return {"du": du, "dz": (dzc, dzf, m["dzr"]), "acc": acc}

    def sum_1(which, dz, after=()):
        own, xp, yp, da, db = run(weight_grad_part, which, nz, rest=(ubt, dz), after=after)
        return own, xp, yp, send(da, to_x), send(db, to_y)

    def sum_2(got):
        own, xp, yp, ra, rb = got
        s1, s2 = run(relay_sums, rest=(xp, yp, ra, rb))
        return own, send(s1, to_x), send(s2, to_y)

    def sum_3(got, cross):
        if nz > 4:
            own, r1, r2 = got
            total = own.astype(F32) + r1.astype(F32) + r2.astype(F32)
            total = lax.psum_scatter(
                total, "dp", scatter_dimension=1, axis_index_groups=groups, tiled=True
            )
            return [send(total, to_core) if cross else total]
        parts = list(run(plane_sums, nz, rest=got))
        if cross:
            return [send(parts[k], shift_zc(k)) for k in range(nz)]
        return parts[:1] + [send(parts[k], shift_z(k)) for k in range(1, nz)]

    def sum_4(got):
        return [run(total_of, rest=(got,))]

    last, p0, p1 = run(quarter_of, rest=(mine, recv))
    z0 = along_z(p0)
    z1 = along_z(p1)
    ub, ubt, ulo = run(norm_tokens, rest=(tok4, tok_oth, gain, bias), after=(cot_oth,))
    g0 = gather_1(0, z0)
    every = [
        [qq * ndp + zz * 2 + cc for zz in range(nz) for qq in range(nseq)] for cc in range(2)
    ]
    last = run(hand_on, rest=(last,))
    w_hi = lax.all_gather(last, axes, axis=0, tiled=True, axis_index_groups=every)
    g0 = gather_2(0, g0)
    g1 = gather_1(1, z1)
    f0 = run_project(0, (mine, recv, *g0))
    g1 = gather_2(1, g1)
    f1 = run_project(1, (mine, recv, *g1), f0[4])
    m0 = run_states(0, (f0, f1), spread(f1[4]), ())
    d0 = run_adjoints(0, (f0, f1), m0, spread(m0["summ"]))
    s0 = sum_1("other", d0["dz"])
    f2 = run_project(2, (w_hi,))
    s0 = sum_2(s0)
    f3 = run_project(3, (w_hi,), f2[4])
    got = spread(f3[4])
    s1 = sum_1("own", d0["dz"], after=(got,))
    m1 = run_states(1, (f2, f3), got, m0["h"])
    got = spread(m1["summ"])
    d1 = run_adjoints(1, (f2, f3), m1, got)
    s1 = sum_2(s1)
    s0 = sum_3(s0, True)
    s2 = sum_1("other", d1["dz"])
    s3 = sum_1("own", d1["dz"])
    s0 = sum_4(s0)
    s1 = sum_3(s1, False)
    s2 = sum_2(s2)
    parts = (d0["dz"], d1["dz"], d0["du"], d1["du"], (f0[5], f1[5], w_hi))
    dur = send(run(unit_grads, 1, rest=parts), to_core)
    s3 = sum_2(s3)
    s1 = sum_4(s1)
    s2 = sum_3(s2, True)
    own = run(unit_grads, 0, rest=parts)
    s3 = sum_3(s3, False)
    input_grad, sums = run(
        norm_grads,
        rest=(
            own, dur, tok4, cot4, lim16[0], scale[:1], gain, (m0["acc"], m1["acc"]),
            (d0["acc"], d1["acc"]),
        ),
    )
    hrcv = send(m1["h"][1], to_core)
    bit = 1
    while bit < nseq:
        sums = sums + send(sums, lambda qq, zz, cc, b=bit: (qq ^ b, zz, cc))
        bit *= 2
    bit = 1
    while bit < nz:
        sums = sums + send(sums, lambda qq, zz, cc, b=bit: (qq, zz ^ b, cc))
        bit *= 2
    sums = sums + send(sums, to_core)
    activations = run(activations_of, rest=(tok4, m1["h"][0], hrcv))
    weight_grad = run(assemble, rest=((s1, s3, s0, s2),))
    shape = tokens.shape
    return (
        activations.reshape(shape),
        input_grad.reshape(shape),
        weight_grad,
        sums[0],
        sums[1],
        sums[2],
        sums[3],
        sums[4],
        sums[5],
    )


def solution(mesh):
    whole = P("dp", "seq", None)
    in_specs = (whole, whole, P("dp", None)) + (P(),) * 6 + (P("dp"),)
    out_specs = (whole, whole, P("dp", "seq")) + (P(),) * 6
    step = functools.partial(local, mesh.shape["seq"], mesh.shape["dp"])
    return jax.shard_map(step, mesh=mesh, in_specs=in_specs, out_specs=out_specs, check_vma=False)
```

time: 2000 us -> 414 us (0.21); the launches traced: 1960 us -> 410 us
  local copies, waits for them, and re-layouts: 825 us -> 26.5 us
  waiting for transfers between devices: 696 us -> 86.6 us
  other arithmetic: 259 us -> 1.09 us
  Pallas kernels: 0 us -> 191 us
  matrix products: 92.2 us -> 0 us
  starting transfers between devices: 0.12 us -> 55.8 us
  blocking collectives: 75.1 us -> 34.1 us
    slice x119 -> x7, local copies, waits for them, and re-layouts: 592 us -> 0.65 us  [the longest x1 0.64 us: local(): sums[5]]
    reduce_scatter x2 -> x0, waiting for transfers between devices: 481 us -> none  [the longest x1 481 us: local(): lax.psum_scatter(lax.dot_general(columns, proj_grad, (((0,), (0,)), ((),...]
    all_gather x1, waiting for transfers between devices: 214 us -> 0.01 us  [local(): lax.all_gather(last, axes, axis=0, tiled=True, axis_index_groups=every)]
    pad x60 -> x0, local copies, waits for them, and re-layouts: 192 us -> none  [the longest x30 113 us: local(): prod_fwd, local_fwd = lax.associative_scan(combine, (decay, inject), axis=1)]
    pallas_call x0 -> x35, Pallas kernels: none -> 191 us  [the longest x32 166 us: call_flat(): pl.pallas_call(body, in_specs=[SMEM] + dep_specs + in_specs, out_specs=ou...]
    add x49 -> x5, other arithmetic: 111 us -> 0.04 us  [the longest x2 0.02 us: local(): sums = sums + send(sums, lambda qq, zz, cc, b=bit: (qq ^ b, zz, cc))]
    dot_general x3 -> x0, matrix products: 92.2 us -> none  [the longest x1 37.7 us: local(): lax.dot_general(proj_grad, lax.all_gather(weight, 'dp', axis=0, tiled=Tru...]
    ppermute x0 -> x55, waiting for transfers between devices: none -> 86.6 us  [send(): return lax.ppermute(value, axes, table(move))]
  transfers between devices with their start and end apart: 3 -> 56, of which waited for: 2 -> 20; matrix products, arithmetic and copies ran while one was open for 3% -> 1% of each run, Pallas kernels for 0% -> 41%
where the time goes in v2:
time: 414 us; the launch traced here: 410 us
  Pallas kernels  191 us (46%)
  waiting for transfers between devices  86.6 us (21%)
  starting transfers between devices  55.8 us (13%)
  blocking collectives  34.1 us (8%)
  local copies, waits for them, and re-layouts  26.5 us (6%)
  between operations  15.2 us (4%)
    pallas_call x32, Pallas kernels, call_flat(): pl.pallas_call(body, in_specs=[SMEM] + dep_specs + in_specs, out_specs=ou...  166 us
    ppermute x55, waiting for transfers between devices, send(): return lax.ppermute(value, axes, table(move))  86.6 us
    ppermute x55, starting transfers between devices, send(): return lax.ppermute(value, axes, table(move))  55.7 us
    all_gather x4, blocking collectives, spread(): return lax.all_gather(both, 'seq')  34.1 us
    pallas_call x3, Pallas kernels, call(): pl.pallas_call(body, grid_spec=pltpu.PrefetchScalarGridSpec(num_scalar_pr...  24.4 us
    unnamed x138, local copies, waits for them, and re-layouts  22.3 us
  transfers between devices with their start and end apart: 56, of which 20 were waited for; matrix products, arithmetic and copies ran while one was open for 1% of the time, Pallas kernels for 41%

profile of v2, /device:TPU:10, one launch (start us, length us, event | category | flops | bytes accessed | tf_op | source)
XLA Modules:
  0.0 409.9 jit_solution(6357071975536891011)
XLA Ops:
  7.4 3.7 split_weight.1
  11.6 1.5 constant_dynamic-slice_fusion.3
  13.9 1.6 collective-permute-done.refs_2_.refs_4_
  15.5 1.5 quarter_of.1
  17.6 2.6 collective-permute-start.4
  20.2 2.5 collective-permute-start.5
  22.7 12.6 %norm_tokens.1 = (bf16[6,2,128,2048]{3,2,1,0:T(8,128)(2,1)}, bf16[2048,1536]{1,0:T(8,128)(2,1)}, bf16[6,2,128,1024]{3,2,1,0:T(8,128)(2,1)}) custom-call(s32[3]{0:T(128)S(1)} %pad_add_fusion.1.ids, bf16[128,768]{1,0:T(8,128)(2,1)S(1)} %get-tuple-element.129.refs_0_, bf16[2,4,96,1024]{3,2,1,0:T(8,128)(2,1)S(1)} %bitcast.41, bf16[2,4,96,2048]{3,2,1,0:T(8,128)(2,1)} %bitcast.56, ...), custom_call_target="tpu_custom_call" | custom-call | flops 31457280 | bytes 22020096 | tf_op jit(solution)/shard_map/norm_tokens/pallas_call | solution.py:68
  35.3 1.7 collective-permute-done.5.refs_3_
  37.0 1.9 copy-done.3
  41.8 1.5 collective-permute-start.7
  44.1 2.5 collective-permute-start.10
  46.6 1.5 collective-permute-start.9
  48.0 11.7 %collective-permute-done.6.refs_1_.refs_6_ = bf16[384,768]{1,0:T(8,128)(2,1)S(1)} collective-permute-done((bf16[384,768]{1,0:T(8,128)(2,1)S(1)}, bf16[384,768]{1,0:T(8,128)(2,1)S(1)}, u32[]{:S(2)}, u32[]{:S(2)}) %collective-permute-start.6) | collective-permute-done | bytes 589856 | tf_op jit(solution)/shard_map/ppermute | solution.py:937
  60.6 1.6 collective-permute-start.11
  62.2 1.5 collective-permute-start.12
  66.0 5.9 %collective-permute-done.9.refs_2_ = bf16[128,768]{1,0:T(8,128)(2,1)S(1)} collective-permute-done((bf16[128,768]{1,0:T(8,128)(2,1)S(1)}, bf16[128,768]{1,0:T(8,128)(2,1)S(1)}, u32[]{:S(2)}, u32[]{:S(2)}) %collective-permute-start.9) | collective-permute-done | bytes 196640 | tf_op jit(solution)/shard_map/ppermute | solution.py:937
  76.3 11.4 %project_0.1 = (f32[6,2,128,256]{3,2,1,0:T(8,128)S(1)}, f32[6,2,128,256]{3,2,1,0:T(8,128)S(1)}, f32[6,2,128,256]{3,2,1,0:T(8,128)S(1)}, f32[32,256]{1,0:T(8,128)...) custom-call(s32[3]{0:T(128)S(1)} %pad_add_fusion.1.ids, bf16[384,768]{1,0:T(8,128)(2,1)} %plane_pieces_1.1.refs_0_.refs_5_, ...), custom_call_target="tpu_custom_call" | custom-call | flops 4831838208 | bytes 12582912 | tf_op jit(solution)/shard_map/project_0/pallas_call | solution.py:90
  88.8 8.5 %collective-permute-done.14.refs_1_.refs_6_ = bf16[384,768]{1,0:T(8,128)(2,1)} collective-permute-done((bf16[384,768]{1,0:T(8,128)(2,1)}, bf16[384,768]{1,0:T(8,128)(2,1)}, u32[]{:S(2)}, u32[]{:S(2)}) %collective-permute-start.14) | collective-permute-done | bytes 589856 | tf_op jit(solution)/shard_map/ppermute | solution.py:937
  97.3 2.1 cross_pieces_1.1
  99.5 1.9 collective-permute-start.16
  101.5 5.0 %collective-permute-done.16.refs_8_ = bf16[384,384]{1,0:T(8,128)(2,1)} collective-permute-done((bf16[384,384]{1,0:T(8,128)(2,1)}, bf16[384,384]{1,0:T(8,128)(2,1)}, u32[]{:S(2)}, u32[]{:S(2)}) %collective-permute-start.16) | collective-permute-done | bytes 294944 | tf_op jit(solution)/shard_map/ppermute | solution.py:937
  106.5 1.9 collective-permute-done.17.refs_9_
  108.4 11.6 %project_1.1 = (f32[6,2,128,256]{3,2,1,0:T(8,128)S(1)}, f32[6,2,128,256]{3,2,1,0:T(8,128)S(1)}, f32[6,2,128,256]{3,2,1,0:T(8,128)S(1)}, f32[32,256]{1,0:T(8,128)...) custom-call(s32[3]{0:T(128)S(1)} %pad_add_fusion.1.ids, bf16[384,384]{1,0:T(8,128)(2,1)} %get-tuple-element.137.refs_0_, ...), custom_call_target="tpu_custom_call" | custom-call | flops 4831838208 | bytes 12582912 | tf_op jit(solution)/shard_map/project_1/pallas_call | solution.py:90
  120.0 7.3 %all-gather = f32[8,8,256]{2,1,0:T(8,128)S(1)} all-gather(f32[2,8,256]{2,1,0:T(8,128)S(1)} %get-tuple-element.139.refs_0_), channel_id=2, replica_groups=mesh['seq'=4,'dp'=8] {'seq'}, dimensions={0}, use_global_device_ids=true | all-gather | bytes 81920 | tf_op jit(solution)/shard_map/all_gather | solution.py:1015
  127.4 10.8 %states_0.1 = (bf16[4,2,768,128]{3,2,1,0:T(8,128)(2,1)}, bf16[4,2,768,128]{3,2,1,0:T(8,128)(2,1)}, f32[6,2,128,256]{3,2,1,0:T(8,128)S(1)}, f32[6,2,128,256]{3,2,...) custom-call(s32[3]{0:T(128)S(1)} %pad_add_fusion.1.ids, ...), custom_call_target="tpu_custom_call" | custom-call | flops 47185920 | bytes 7864320 | tf_op jit(solution)/shard_map/states_0/pallas_call | solution.py:90
  138.2 8.6 %all-gather.1 = f32[8,8,256]{2,1,0:T(8,128)S(1)} all-gather(f32[2,8,256]{2,1,0:T(8,128)S(1)} %get-tuple-element.159), channel_id=3, replica_groups=mesh['seq'=4,'dp'=8] {'seq'}, dimensions={0}, use_global_device_ids=true | all-gather | bytes 81920 | tf_op jit(solution)/shard_map/all_gather | solution.py:1015
  146.8 2.1 adjoints_0.1
  149.0 9.3 %weight_grad_part.4 = (bf16[3,1024,128]{2,1,0:T(8,128)(2,1)S(1)}, bf16[3,1024,128]{2,1,0:T(8,128)(2,1)S(1)}, bf16[3,1024,128]{2,1,0:T(8,128)(2,1)S(1)}, bf16[3,512,128]{2,1,0:T(8,128)(2,1)}, bf16[3,512,128]{2,1,0:T(8,128)(2,1)}) custom-call(s32[3]{0:T(128)S(1)} %pad_add_fusion.1.ids, f32[2,16,256]{2,1,0:T(8,128)S(1)} %get-tuple-element.160.refs_0_.refs_10_, ...), custom_call_target="tpu_custom_call" | custom-call | flops 4831838208 | bytes 6291456 | tf_op jit(solution)/shard_map/weight_grad_part/pallas_call | solution.py:90
  158.6 1.9 collective-permute-start.19
  160.5 10.5 %project_2.1 = (f32[6,2,128,256]{3,2,1,0:T(8,128)S(1)}, f32[6,2,128,256]{3,2,1,0:T(8,128)S(1)}, f32[6,2,128,256]{3,2,1,0:T(8,128)S(1)}, f32[32,256]{1,0:T(8,128)S(1)}, f32[2,8,256]{2,1,0:T(8,128)S(1)}) custom-call(s32[3]{0:T(128)S(1)} %pad_add_fusion.1.ids, bf16[3,512,128]{2,1,0:T(8,128)(2,1)} %get-tuple-element.165.refs_0_, ...), custom_call_target="tpu_custom_call" | custom-call | flops 4831838208 | bytes 12582912 | tf_op jit(solution)/shard_map/project_2/pallas_call | solution.py:90
  172.0 10.8 %project_3.1 = (f32[6,2,128,256]{3,2,1,0:T(8,128)S(1)}, f32[6,2,128,256]{3,2,1,0:T(8,128)S(1)}, f32[6,2,128,256]{3,2,1,0:T(8,128)S(1)}, f32[32,256]{1,0:T(8,128)S(1)}, f32[2,8,256]{2,1,0:T(8,128)S(1)}) custom-call(s32[3]{0:T(128)S(1)} %pad_add_fusion.1.ids, bf16[3,1024,128]{2,1,0:T(8,128)(2,1)S(1)} %get-tuple-element.170.refs_0_, ...), custom_call_target="tpu_custom_call" | custom-call | flops 4831838208 | bytes 12582912 | tf_op jit(solution)/shard_map/project_3/pallas_call | solution.py:90
  182.8 9.2 %all-gather.2 = f32[8,8,256]{2,1,0:T(8,128)S(1)} all-gather(f32[2,8,256]{2,1,0:T(8,128)S(1)} %get-tuple-element.171.refs_0_), channel_id=4, replica_groups=mesh['seq'=4,'dp'=8] {'seq'}, dimensions={0}, use_global_device_ids=true | all-gather | bytes 81920 | tf_op jit(solution)/shard_map/all_gather | solution.py:1015
  192.1 7.9 %weight_grad_part.5 = (bf16[3,1024,128]{2,1,0:T(8,128)(2,1)S(1)}, bf16[3,1024,128]{2,1,0:T(8,128)(2,1)S(1)}, bf16[3,1024,128]{2,1,0:T(8,128)(2,1)S(1)}, bf16[3,5...) custom-call(s32[3]{0:T(128)S(1)} %pad_add_fusion.1.ids, f32[2,8,256]{2,1,0:T(8,128)S(1)} %get-tuple-element.171.refs_0_, ...), custom_call_target="tpu_custom_call" | custom-call | flops 4831838208 | bytes 6291456 | tf_op jit(solution)/shard_map/weight_grad_part/pallas_call | solution.py:90
  200.1 1.9 collective-permute-start.20
  202.1 10.7 %states_1.1 = (bf16[4,2,768,128]{3,2,1,0:T(8,128)(2,1)}, bf16[4,2,768,128]{3,2,1,0:T(8,128)(2,1)}, f32[6,2,128,256]{3,2,1,0:T(8,128)S(1)}, f32[6,2,128,256]{3,2,...) custom-call(s32[3]{0:T(128)S(1)} %pad_add_fusion.1.ids, ...), custom_call_target="tpu_custom_call", output_to_operand_aliasing={{0}: (18, {}), {1}: (19, {})} | custom-call | flops 47185920 | bytes 7864320 | tf_op jit(solution)/shard_map/states_1/pallas_call | solution.py:90
  212.9 9.0 %all-gather.3 = f32[8,8,256]{2,1,0:T(8,128)S(1)} all-gather(f32[2,8,256]{2,1,0:T(8,128)S(1)} %get-tuple-element.194), channel_id=5, replica_groups=mesh['seq'=4,'dp'=8] {'seq'}, dimensions={0}, use_global_device_ids=true | all-gather | bytes 81920 | tf_op jit(solution)/shard_map/all_gather | solution.py:1015
  221.9 2.2 adjoints_1.1
  225.1 1.9 collective-permute-start.29
  227.9 7.7 %collective-permute-start.26 = (bf16[3,256,128]{2,1,0:T(8,128)(2,1)S(1)}, bf16[3,256,128]{2,1,0:T(8,128)(2,1)S(1)}, u32[]{:S(2)}, u32[]{:S(2)}) collective-permute-start(bf16[3,256,128]{2,1,0:T(8,128)(2,1)S(1)} %get-tuple-element.210), channel_id=1, source_target_pairs={{0,5},{1,4},{2,7},{3,6},{4,1},{5,0},{6,3},{7,2},{8,13},{9,12},{10,... | collective-permute-start | bytes 589832 | tf_op jit(solution)/shard_map/ppermute | solution.py:937
  235.6 7.9 %weight_grad_part.6 = (bf16[3,1024,128]{2,1,0:T(8,128)(2,1)S(1)}, bf16[3,1024,128]{2,1,0:T(8,128)(2,1)S(1)}, bf16[3,1024,128]{2,1,0:T(8,128)(2,1)S(1)}, bf16[3,5...) custom-call(s32[3]{0:T(128)S(1)} %pad_add_fusion.1.ids, bf16[3,256,128]{2,1,0:T(8,128)(2,1)S(1)} %get-tuple-element.202.refs_0_, ...), custom_call_target="tpu_custom_call" | custom-call | flops 4831838208 | bytes 6291456 | tf_op jit(solution)/shard_map/weight_grad_part/pallas_call | solution.py:90
  246.0 3.6 collective-permute-done.27.refs_4_
  249.7 7.9 %weight_grad_part.7 = (bf16[3,1024,128]{2,1,0:T(8,128)(2,1)S(1)}, bf16[3,1024,128]{2,1,0:T(8,128)(2,1)S(1)}, bf16[3,1024,128]{2,1,0:T(8,128)(2,1)S(1)}, bf16[3,5...) custom-call(s32[3]{0:T(128)S(1)} %pad_add_fusion.1.ids, bf16[3,512,128]{2,1,0:T(8,128)(2,1)S(1)} %get-tuple-element.206.refs_0_, ...), custom_call_target="tpu_custom_call" | custom-call | flops 4831838208 | bytes 6291456 | tf_op jit(solution)/shard_map/weight_grad_part/pallas_call | solution.py:90
  258.3 1.5 plane_sums.5
  259.8 1.8 relay_sums.6
  261.7 16.4 %unit_grads_1.1.refs_0_ = bf16[768,2048]{1,0:T(8,128)(2,1)} custom-call(s32[3]{0:T(128)S(1)} %pad_add_fusion.1.ids, bf16[3,1024,128]{2,1,0:T(8,128)(2,1)} %get-tuple-element.217.refs_0_, bf16[6,2,128,512]{3,2,1,0:T(8,128)(2,1)S(1)} %copy-done.47, bf16[6,2,128,512]{3,2,1,0:T(8,128)(2,1)S(1)} %copy-done.50, bf16[6,2,128,512]{3,2,1,0:T(8,128)(2,1)S(1)} %copy-done.44, ...), custom_call_target="tpu_custom_call" | custom-call | flops 9663676416 | bytes 12582912 | tf_op jit(solution)/shard_map/unit_grads_1/pallas_call | solution.py:90
  278.1 1.9 collective-permute-start.32
  280.1 1.9 collective-permute-start.37
  282.2 7.9 %collective-permute-done.32.refs_3_ = bf16[3,512,128]{2,1,0:T(8,128)(2,1)S(1)} collective-permute-done((bf16[3,512,128]{2,1,0:T(8,128)(2,1)S(1)}, bf16[3,512,128]{2,1,0:T(8,128)(2,1)S(1)}, u32[]{:S(2)}, u32[]{:S(2)}) %collective-permute-start.32) | collective-permute-done | bytes 393248 | tf_op jit(solution)/shard_map/ppermute | solution.py:937
  292.7 4.5 %collective-permute-done.34.refs_2_ = bf16[3,256,128]{2,1,0:T(8,128)(2,1)S(1)} collective-permute-done((bf16[3,256,128]{2,1,0:T(8,128)(2,1)S(1)}, bf16[3,256,128]{2,1,0:T(8,128)(2,1)S(1)}, u32[]{:S(2)}, u32[]{:S(2)}) %collective-permute-start.34) | collective-permute-done | bytes 196640 | tf_op jit(solution)/shard_map/ppermute | solution.py:937
  299.0 7.1 %collective-permute-done.35.refs_3_ = bf16[3,256,128]{2,1,0:T(8,128)(2,1)S(1)} collective-permute-done((bf16[3,256,128]{2,1,0:T(8,128)(2,1)S(1)}, bf16[3,256,128]{2,1,0:T(8,128)(2,1)S(1)}, u32[]{:S(2)}, u32[]{:S(2)}) %collective-permute-start.35) | collective-permute-done | bytes 196640 | tf_op jit(solution)/shard_map/ppermute | solution.py:937
  306.8 3.8 collective-permute-start.36
  318.1 1.5 total_of.3.refs_0_.refs_1_
  320.9 1.7 plane_sums.6
  329.7 14.8 %unit_grads_0.1.refs_0_.refs_1_ = f32[768,2048]{1,0:T(8,128)S(1)} custom-call(s32[3]{0:T(128)S(1)} %pad_add_fusion.1.ids, bf16[3,256,128]{2,1,0:T(8,128)(2,1)S(1)} %get-tuple-element.231.refs_0_, bf16[6,2,128,512]{3,2,1,0:T(8,128)(2,1)S(1)} %copy-done.48, bf16[6,2,128,512]{3,2,1,0:T(8,128)(2,1)S(1)} %copy-done.51, bf16[6,2,128,512]{3,2,1,0:T(8,128)(2,1)S(1)} %copy-done.45, ...), custom_call_target="tpu_custom_call" | custom-call | flops 9663676416 | bytes 12582912 | tf_op jit(solution)/shard_map/unit_grads_0/pallas_call | solution.py:90
  345.5 11.5 %norm_grads.1 = (f32[2,4,96,2048]{3,2,1,0:T(8,128)}, f32[8,2048]{1,0:T(8,128)S(1)}) custom-call(s32[3]{0:T(128)S(1)} %pad_add_fusion.1.ids, bf16[3,256,128]{2,1,0:T(8,128)(2,1)S(1)} %get-tuple-element.234.refs_0_, f32[768,2048]{1,0:T(8,128)S(1)} %unit_grads_0.1.refs_0_.refs_1_, bf16[768,2048]{1,0:T(8,128)(2,1)S(1)} %collective-permute-done.41.refs_2_, ...), custom_call_target="tpu_custom_call" | custom-call | flops 31457280 | bytes 12582912 | tf_op jit(solution)/shard_map/norm_grads/pallas_call | solution.py:90
  357.9 3.4 collective-permute-done.50
  362.6 3.1 collective-permute-done.51
  366.7 3.2 collective-permute-done.52
  370.0 3.4 collective-permute-start.53
  373.4 3.5 collective-permute-start.48
  377.0 12.6 %collective-permute-done.45.refs_5_ = bf16[3,256,128]{2,1,0:T(8,128)(2,1)S(1)} collective-permute-done((bf16[3,256,128]{2,1,0:T(8,128)(2,1)S(1)}, bf16[3,256,128]{2,1,0:T(8,128)(2,1)S(1)}, u32[]{:S(2)}, u32[]{:S(2)}) %collective-permute-start.45) | collective-permute-done | bytes 196640 | tf_op jit(solution)/shard_map/ppermute | solution.py:937
  389.6 8.0 %activations_of.1.refs_0_ = f32[2,4,96,2048]{3,2,1,0:T(8,128)} custom-call(s32[3]{0:T(128)S(1)} %pad_add_fusion.1.ids, f32[8,2048]{1,0:T(8,128)S(1)} %get-tuple-element.235.refs_0_, bf16[2,4,96,2048]{3,2,1,0:T(8,128)(2,1)} %bitcast.58, bf16[4,2,768,128]{3,2,1,0:T(8,128)(2,1)} %get-tuple-element.236.refs_2_, ...), custom_call_target="tpu_custom_call" | custom-call | flops 1572864 | bytes 12582912 | tf_op jit(solution)/shard_map/activations_of/pallas_call | solution.py:68
  397.7 2.8 copy-done
  400.5 2.0 assemble.1
  (263 shorter events, 47.2 us)
Async XLA Ops:
  7.2 153.3 %all-gather.6.cloned.1.call-start = ((), (), s32[]{:S(2)}) async-start(), calls=%async_computation | async-start | bytes 6684672 | tf_op jit(solution)/shard_map/all_gather | solution.py:1068
  7.2 15.4 %collective-permute-start.2 = (bf16[2,384,2048]{2,1,0:T(8,128)(2,1)}, bf16[2,384,2048]{2,1,0:T(8,128)(2,1)}, u32[]{:S(2)}, u32[]{:S(2)}) collective-permute-start(bf16[2,384,2048]{2,1,0:T(8,128)(2,1)} %param.10), channel_id=1, source_target_pairs={{0,1},{1,0},{2,3},{3,2},{4,5},{5,4},{6,7},{7,6},{8,9},{9,8},{10,11... | collective-permute-start | bytes 9437192 | tf_op jit(solution)/shard_map/ppermute | solution.py:937
  11.1 4.4 %collective-permute-start = (bf16[256,3072]{1,0:T(8,128)(2,1)}, bf16[256,3072]{1,0:T(8,128)(2,1)}, u32[]{:S(2)}, u32[]{:S(2)}) collective-permute-start(bf16[256,3072]{1,0:T(8,128)(2,1)} %get-tuple-element.128), channel_id=1, source_target_pairs={{0,1},{1,0},{2,3},{3,2},{4,5},{5,4},{6,7},{7,6},{8,9},{9,8},{10,11... | collective-permute-start | bytes 4718600 | tf_op jit(solution)/shard_map/ppermute | solution.py:937
  13.4 9.3 %collective-permute-start.1 = (bf16[2,384,1024]{2,1,0:T(8,128)(2,1)S(1)}, bf16[2,384,1024]{2,1,0:T(8,128)(2,1)S(1)}, u32[]{:S(2)}, u32[]{:S(2)}) collective-permute-start(bf16[2,384,1024]{2,1,0:T(8,128)(2,1)S(1)} %pad_maximum_fusion), channel_id=1, source_target_pairs={{0,1},{1,0},{2,3},{3,2},{4,5},{5,4},{6,7},{7,6},{8,9},{9,8},{10,11... | collective-permute-start | bytes 4718600 | tf_op jit(solution)/shard_map/ppermute | solution.py:937
  17.1 18.2 %collective-permute-start.3 = (bf16[128,768]{1,0:T(8,128)(2,1)S(1)}, bf16[128,768]{1,0:T(8,128)(2,1)S(1)}, u32[]{:S(2)}, u32[]{:S(2)}) collective-permute-start(bf16[128,768]{1,0:T(8,128)(2,1)S(1)} %get-tuple-element.131), channel_id=1, source_target_pairs={{0,6},{1,7},{2,0},{3,1},{4,2},{5,3},{6,4},{7,5},{8,14},{9,15},{10,... | collective-permute-start | bytes 589832 | tf_op jit(solution)/shard_map/ppermute | solution.py:937
  17.6 17.7 %collective-permute-start.4 = (bf16[128,768]{1,0:T(8,128)(2,1)S(1)}, bf16[128,768]{1,0:T(8,128)(2,1)S(1)}, u32[]{:S(2)}, u32[]{:S(2)}) collective-permute-start(bf16[128,768]{1,0:T(8,128)(2,1)S(1)} %get-tuple-element.131), channel_id=1, source_target_pairs={{0,4},{1,5},{2,6},{3,7},{4,0},{5,1},{6,2},{7,3},{8,12},{9,13},{10,... | collective-permute-start | bytes 589832 | tf_op jit(solution)/shard_map/ppermute | solution.py:937
  20.2 16.9 %collective-permute-start.5 = (bf16[128,768]{1,0:T(8,128)(2,1)S(1)}, bf16[128,768]{1,0:T(8,128)(2,1)S(1)}, u32[]{:S(2)}, u32[]{:S(2)}) collective-permute-start(bf16[128,768]{1,0:T(8,128)(2,1)S(1)} %get-tuple-element.131), channel_id=1, source_target_pairs={{0,2},{1,3},{2,4},{3,5},{4,6},{5,7},{6,0},{7,1},{8,10},{9,11},{10,... | collective-permute-start | bytes 589832 | tf_op jit(solution)/shard_map/ppermute | solution.py:937
  39.5 21.1 %copy-start.4 = (bf16[384,768]{1,0:T(8,128)(2,1)}, bf16[384,768]{1,0:T(8,128)(2,1)S(1)}, u32[]{:S(2)}) copy-start(bf16[384,768]{1,0:T(8,128)(2,1)S(1)} %plane_pieces_0.1.refs_0_.refs_5_) | copy-start | bytes 1769476
  41.0 2.9 collective-permute-start.13
  41.2 18.6 %collective-permute-start.6 = (bf16[384,768]{1,0:T(8,128)(2,1)S(1)}, bf16[384,768]{1,0:T(8,128)(2,1)S(1)}, u32[]{:S(2)}, u32[]{:S(2)}) collective-permute-start(bf16[384,768]{1,0:T(8,128)(2,1)S(1)} %plane_pieces_0.1.refs_0_.refs_5_), channel_id=1, source_target_pairs={{0,8},{1,9},{2,10},{3,11},{4,12},{5,13},{6,14},{7,15},{8,0},{9,1},... | collective-permute-start | bytes 1769480 | tf_op jit(solution)/shard_map/ppermute | solution.py:937
  41.8 18.2 %collective-permute-start.7 = (bf16[384,768]{1,0:T(8,128)(2,1)S(1)}, bf16[384,768]{1,0:T(8,128)(2,1)S(1)}, u32[]{:S(2)}, u32[]{:S(2)}) collective-permute-start(bf16[384,768]{1,0:T(8,128)(2,1)S(1)} %plane_pieces_0.1.refs_0_.refs_5_), channel_id=1, source_target_pairs={{0,16},{1,17},{2,18},{3,19},{4,20},{5,21},{6,22},{7,23},{8,24},{9,... | collective-permute-start | bytes 1769480 | tf_op jit(solution)/shard_map/ppermute | solution.py:937
  43.9 32.4 %copy-start.58 = (s32[2,2]{1,0:T(2,128)}, s32[2,2]{1,0:T(2,128)S(1)}, u32[]{:S(2)}) copy-start(s32[2,2]{1,0:T(2,128)S(1)} %get-tuple-element.270) | copy-start | bytes 52
  44.1 20.7 %collective-permute-start.10 = (bf16[128,768]{1,0:T(8,128)(2,1)S(1)}, bf16[128,768]{1,0:T(8,128)(2,1)S(1)}, u32[]{:S(2)}, u32[]{:S(2)}) collective-permute-start(bf16[128,768]{1,0:T(8,128)(2,1)S(1)} %get-tuple-element.129.refs_0_), channel_id=1, source_target_pairs={{0,2},{1,3},{2,4},{3,5},{4,6},{5,7},{6,0},{7,1},{8,10},{9,11},{10,... | collective-permute-start | bytes 589832 | tf_op jit(solution)/shard_map/ppermute | solution.py:937
  46.6 19.4 %collective-permute-start.8 = (bf16[128,768]{1,0:T(8,128)(2,1)S(1)}, bf16[128,768]{1,0:T(8,128)(2,1)S(1)}, u32[]{:S(2)}, u32[]{:S(2)}) collective-permute-start(bf16[128,768]{1,0:T(8,128)(2,1)S(1)} %get-tuple-element.129.refs_0_), channel_id=1, source_target_pairs={{0,6},{1,7},{2,0},{3,1},{4,2},{5,3},{6,4},{7,5},{8,14},{9,15},{10,... | collective-permute-start | bytes 589832 | tf_op jit(solution)/shard_map/ppermute | solution.py:937
  46.6 25.3 %collective-permute-start.9 = (bf16[128,768]{1,0:T(8,128)(2,1)S(1)}, bf16[128,768]{1,0:T(8,128)(2,1)S(1)}, u32[]{:S(2)}, u32[]{:S(2)}) collective-permute-start(bf16[128,768]{1,0:T(8,128)(2,1)S(1)} %get-tuple-element.129.refs_0_), channel_id=1, source_target_pairs={{0,4},{1,5},{2,6},{3,7},{4,0},{5,1},{6,2},{7,3},{8,12},{9,13},{10,... | collective-permute-start | bytes 589832 | tf_op jit(solution)/shard_map/ppermute | solution.py:937
  60.6 14.8 %collective-permute-start.11 = (bf16[384,384]{1,0:T(8,128)(2,1)S(1)}, bf16[384,384]{1,0:T(8,128)(2,1)S(1)}, u32[]{:S(2)}, u32[]{:S(2)}) collective-permute-start(bf16[384,384]{1,0:T(8,128)(2,1)S(1)} %get-tuple-element.135), channel_id=1, source_target_pairs={{0,8},{1,9},{2,10},{3,11},{4,12},{5,13},{6,14},{7,15},{8,0},{9,1},... | collective-permute-start | bytes 884744 | tf_op jit(solution)/shard_map/ppermute | solution.py:937
  62.2 13.2 %collective-permute-start.12 = (bf16[384,384]{1,0:T(8,128)(2,1)S(1)}, bf16[384,384]{1,0:T(8,128)(2,1)S(1)}, u32[]{:S(2)}, u32[]{:S(2)}) collective-permute-start(bf16[384,384]{1,0:T(8,128)(2,1)S(1)} %get-tuple-element.133.refs_0_), channel_id=1, source_target_pairs={{0,16},{1,17},{2,18},{3,19},{4,20},{5,21},{6,22},{7,23},{8,24},{9,... | collective-permute-start | bytes 884744 | tf_op jit(solution)/shard_map/ppermute | solution.py:937
  73.3 24.0 %collective-permute-start.14 = (bf16[384,768]{1,0:T(8,128)(2,1)}, bf16[384,768]{1,0:T(8,128)(2,1)}, u32[]{:S(2)}, u32[]{:S(2)}) collective-permute-start(bf16[384,768]{1,0:T(8,128)(2,1)} %plane_pieces_1.1.refs_0_.refs_5_), channel_id=1, source_target_pairs={{0,8},{1,9},{2,10},{3,11},{4,12},{5,13},{6,14},{7,15},{8,0},{9,1},... | collective-permute-start | bytes 1769480 | tf_op jit(solution)/shard_map/ppermute | solution.py:937
  74.8 22.6 %collective-permute-start.15 = (bf16[384,768]{1,0:T(8,128)(2,1)}, bf16[384,768]{1,0:T(8,128)(2,1)}, u32[]{:S(2)}, u32[]{:S(2)}) collective-permute-start(bf16[384,768]{1,0:T(8,128)(2,1)} %plane_pieces_1.1.refs_0_.refs_5_), channel_id=1, source_target_pairs={{0,16},{1,17},{2,18},{3,19},{4,20},{5,21},{6,22},{7,23},{8,24},{9,... | collective-permute-start | bytes 1769480 | tf_op jit(solution)/shard_map/ppermute | solution.py:937
  99.5 7.0 %collective-permute-start.16 = (bf16[384,384]{1,0:T(8,128)(2,1)}, bf16[384,384]{1,0:T(8,128)(2,1)}, u32[]{:S(2)}, u32[]{:S(2)}) collective-permute-start(bf16[384,384]{1,0:T(8,128)(2,1)} %get-tuple-element.138), channel_id=1, source_target_pairs={{0,8},{1,9},{2,10},{3,11},{4,12},{5,13},{6,14},{7,15},{8,0},{9,1},... | collective-permute-start | bytes 884744 | tf_op jit(solution)/shard_map/ppermute | solution.py:937
  101.3 7.0 %collective-permute-start.17 = (bf16[384,384]{1,0:T(8,128)(2,1)}, bf16[384,384]{1,0:T(8,128)(2,1)}, u32[]{:S(2)}, u32[]{:S(2)}) collective-permute-start(bf16[384,384]{1,0:T(8,128)(2,1)} %get-tuple-element.137.refs_0_), channel_id=1, source_target_pairs={{0,16},{1,17},{2,18},{3,19},{4,20},{5,21},{6,22},{7,23},{8,24},{9,... | collective-permute-start | bytes 884744 | tf_op jit(solution)/shard_map/ppermute | solution.py:937
  158.4 12.6 %collective-permute-start.18 = (bf16[3,512,128]{2,1,0:T(8,128)(2,1)}, bf16[3,512,128]{2,1,0:T(8,128)(2,1)S(1)}, u32[]{:S(2)}, u32[]{:S(2)}) collective-permute-start(bf16[3,512,128]{2,1,0:T(8,128)(2,1)} %get-tuple-element.169), channel_id=1, source_target_pairs={{0,8},{1,9},{2,10},{3,11},{4,12},{5,13},{6,14},{7,15},{8,0},{9,1},... | collective-permute-start | bytes 1179656 | tf_op jit(solution)/shard_map/ppermute | solution.py:937
  158.6 12.4 %collective-permute-start.19 = (bf16[3,512,128]{2,1,0:T(8,128)(2,1)}, bf16[3,512,128]{2,1,0:T(8,128)(2,1)S(1)}, u32[]{:S(2)}, u32[]{:S(2)}) collective-permute-start(bf16[3,512,128]{2,1,0:T(8,128)(2,1)} %get-tuple-element.165.refs_0_), channel_id=1, source_target_pairs={{0,16},{1,17},{2,18},{3,19},{4,20},{5,21},{6,22},{7,23},{8,24},{9,... | collective-permute-start | bytes 1179656 | tf_op jit(solution)/shard_map/ppermute | solution.py:937
  171.8 55.2 %collective-permute-start.23 = (bf16[3,1024,128]{2,1,0:T(8,128)(2,1)S(1)}, bf16[3,1024,128]{2,1,0:T(8,128)(2,1)S(1)}, u32[]{:S(2)}, u32[]{:S(2)}) collective-permute-start(bf16[3,1024,128]{2,1,0:T(8,128)(2,1)S(1)} %get-tuple-element.170.refs_0_), channel_id=1, source_target_pairs={{0,16},{1,17},{2,18},{3,19},{4,20},{5,21},{6,22},{7,23},{8,24},{9,... | collective-permute-start | bytes 2359304 | tf_op jit(solution)/shard_map/ppermute | solution.py:937
  192.0 35.0 %collective-permute-start.22 = (bf16[3,1024,128]{2,1,0:T(8,128)(2,1)S(1)}, bf16[3,1024,128]{2,1,0:T(8,128)(2,1)S(1)}, u32[]{:S(2)}, u32[]{:S(2)}) collective-permute-start(bf16[3,1024,128]{2,1,0:T(8,128)(2,1)S(1)} %get-tuple-element.201), channel_id=1, source_target_pairs={{0,8},{1,9},{2,10},{3,11},{4,12},{5,13},{6,14},{7,15},{8,0},{9,1},... | collective-permute-start | bytes 2359304 | tf_op jit(solution)/shard_map/ppermute | solution.py:937
  200.1 24.1 %collective-permute-start.20 = (bf16[3,512,128]{2,1,0:T(8,128)(2,1)S(1)}, bf16[3,512,128]{2,1,0:T(8,128)(2,1)S(1)}, u32[]{:S(2)}, u32[]{:S(2)}) collective-permute-start(bf16[3,512,128]{2,1,0:T(8,128)(2,1)S(1)} %get-tuple-element.198), channel_id=1, source_target_pairs={{0,8},{1,9},{2,10},{3,11},{4,12},{5,13},{6,14},{7,15},{8,0},{9,1},... | collective-permute-start | bytes 1179656 | tf_op jit(solution)/shard_map/ppermute | solution.py:937
  202.0 22.2 %collective-permute-start.21 = (bf16[3,512,128]{2,1,0:T(8,128)(2,1)S(1)}, bf16[3,512,128]{2,1,0:T(8,128)(2,1)S(1)}, u32[]{:S(2)}, u32[]{:S(2)}) collective-permute-start(bf16[3,512,128]{2,1,0:T(8,128)(2,1)S(1)} %get-tuple-element.172.refs_0_), channel_id=1, source_target_pairs={{0,16},{1,17},{2,18},{3,19},{4,20},{5,21},{6,22},{7,23},{8,24},{9,... | collective-permute-start | bytes 1179656 | tf_op jit(solution)/shard_map/ppermute | solution.py:937
  212.9 48.7 %copy-start.52 = (bf16[6,2,128,512]{3,2,1,0:T(8,128)(2,1)}, bf16[6,2,128,512]{3,2,1,0:T(8,128)(2,1)S(1)}, u32[]{:S(2)}) copy-start(bf16[6,2,128,512]{3,2,1,0:T(8,128)(2,1)S(1)} %get-tuple-element.205.refs_4_.refs_6_) | copy-start | bytes 4718596
  224.1 37.5 %copy-start.41 = (f32[6,2,128,512]{3,2,1,0:T(8,128)}, f32[6,2,128,512]{3,2,1,0:T(8,128)S(1)}, u32[]{:S(2)}) copy-start(f32[6,2,128,512]{3,2,1,0:T(8,128)S(1)} %get-tuple-element.219.refs_8_) | copy-start | bytes 9437188
  224.1 37.5 %copy-start.54 = (bf16[6,2,128,512]{3,2,1,0:T(8,128)(2,1)}, bf16[6,2,128,512]{3,2,1,0:T(8,128)(2,1)S(1)}, u32[]{:S(2)}) copy-start(bf16[6,2,128,512]{3,2,1,0:T(8,128)(2,1)S(1)} %get-tuple-element.203.refs_2_.refs_4_) | copy-start | bytes 4718596
  224.1 37.5 %copy-start.56 = (bf16[6,2,128,512]{3,2,1,0:T(8,128)(2,1)}, bf16[6,2,128,512]{3,2,1,0:T(8,128)(2,1)S(1)}, u32[]{:S(2)}) copy-start(bf16[6,2,128,512]{3,2,1,0:T(8,128)(2,1)S(1)} %get-tuple-element.204.refs_3_.refs_5_) | copy-start | bytes 4718596
  224.9 33.4 %collective-permute-start.28 = (bf16[3,1024,128]{2,1,0:T(8,128)(2,1)S(1)}, bf16[3,1024,128]{2,1,0:T(8,128)(2,1)S(1)}, u32[]{:S(2)}, u32[]{:S(2)}) collective-permute-start(bf16[3,1024,128]{2,1,0:T(8,128)(2,1)S(1)} %get-tuple-element.212), channel_id=1, source_target_pairs={{0,8},{1,9},{2,10},{3,11},{4,12},{5,13},{6,14},{7,15},{8,0},{9,1},... | collective-permute-start | bytes 2359304 | tf_op jit(solution)/shard_map/ppermute | solution.py:937
  225.1 33.2 %collective-permute-start.29 = (bf16[3,1024,128]{2,1,0:T(8,128)(2,1)S(1)}, bf16[3,1024,128]{2,1,0:T(8,128)(2,1)S(1)}, u32[]{:S(2)}, u32[]{:S(2)}) collective-permute-start(bf16[3,1024,128]{2,1,0:T(8,128)(2,1)S(1)} %get-tuple-element.199.refs_0_), channel_id=1, source_target_pairs={{0,16},{1,17},{2,18},{3,19},{4,20},{5,21},{6,22},{7,23},{8,24},{9,... | collective-permute-start | bytes 2359304 | tf_op jit(solution)/shard_map/ppermute | solution.py:937
  227.9 16.6 %collective-permute-start.25 = (bf16[3,256,128]{2,1,0:T(8,128)(2,1)S(1)}, bf16[3,256,128]{2,1,0:T(8,128)(2,1)S(1)}, u32[]{:S(2)}, u32[]{:S(2)}) collective-permute-start(bf16[3,256,128]{2,1,0:T(8,128)(2,1)S(1)} %get-tuple-element.209), channel_id=1, source_target_pairs={{0,3},{1,2},{2,5},{3,4},{4,7},{5,6},{6,1},{7,0},{8,11},{9,10},{10,... | collective-permute-start | bytes 589832 | tf_op jit(solution)/shard_map/ppermute | solution.py:937
  227.9 17.9 %collective-permute-start.26 = (bf16[3,256,128]{2,1,0:T(8,128)(2,1)S(1)}, bf16[3,256,128]{2,1,0:T(8,128)(2,1)S(1)}, u32[]{:S(2)}, u32[]{:S(2)}) collective-permute-start(bf16[3,256,128]{2,1,0:T(8,128)(2,1)S(1)} %get-tuple-element.210), channel_id=1, source_target_pairs={{0,5},{1,4},{2,7},{3,6},{4,1},{5,0},{6,3},{7,2},{8,13},{9,12},{10,... | collective-permute-start | bytes 589832 | tf_op jit(solution)/shard_map/ppermute | solution.py:937
  235.6 14.0 %collective-permute-start.27 = (bf16[3,256,128]{2,1,0:T(8,128)(2,1)S(1)}, bf16[3,256,128]{2,1,0:T(8,128)(2,1)S(1)}, u32[]{:S(2)}, u32[]{:S(2)}) collective-permute-start(bf16[3,256,128]{2,1,0:T(8,128)(2,1)S(1)} %get-tuple-element.202.refs_0_), channel_id=1, source_target_pairs={{0,7},{1,6},{2,1},{3,0},{4,3},{5,2},{6,5},{7,4},{8,15},{9,14},{10,... | collective-permute-start | bytes 589832 | tf_op jit(solution)/shard_map/ppermute | solution.py:937
  244.5 13.2 %collective-permute-start.24 = (f32[3,256,128]{2,1,0:T(8,128)S(1)}, f32[3,256,128]{2,1,0:T(8,128)S(1)}, u32[]{:S(2)}, u32[]{:S(2)}) collective-permute-start(f32[3,256,128]{2,1,0:T(8,128)S(1)} %get-tuple-element.208), channel_id=1, source_target_pairs={{0,1},{1,0},{2,3},{3,2},{4,5},{5,4},{6,7},{7,6},{8,9},{9,8},{10,11... | collective-permute-start | bytes 1179656 | tf_op jit(solution)/shard_map/ppermute | solution.py:937
  245.9 13.9 %collective-permute-start.30 = (bf16[3,512,128]{2,1,0:T(8,128)(2,1)S(1)}, bf16[3,512,128]{2,1,0:T(8,128)(2,1)S(1)}, u32[]{:S(2)}, u32[]{:S(2)}) collective-permute-start(bf16[3,512,128]{2,1,0:T(8,128)(2,1)S(1)} %get-tuple-element.216), channel_id=1, source_target_pairs={{0,8},{1,9},{2,10},{3,11},{4,12},{5,13},{6,14},{7,15},{8,0},{9,1},... | collective-permute-start | bytes 1179656 | tf_op jit(solution)/shard_map/ppermute | solution.py:937
  249.6 10.2 %collective-permute-start.31 = (bf16[3,512,128]{2,1,0:T(8,128)(2,1)S(1)}, bf16[3,512,128]{2,1,0:T(8,128)(2,1)S(1)}, u32[]{:S(2)}, u32[]{:S(2)}) collective-permute-start(bf16[3,512,128]{2,1,0:T(8,128)(2,1)S(1)} %get-tuple-element.206.refs_0_), channel_id=1, source_target_pairs={{0,16},{1,17},{2,18},{3,19},{4,20},{5,21},{6,22},{7,23},{8,24},{9,... | collective-permute-start | bytes 1179656 | tf_op jit(solution)/shard_map/ppermute | solution.py:937
  261.7 37.3 %copy-start.59 = (s32[2,2]{1,0:T(2,128)S(1)}, s32[2,2]{1,0:T(2,128)}, u32[]{:S(2)}) copy-start(s32[2,2]{1,0:T(2,128)} %copy-done.58) | copy-start | bytes 52
  261.7 48.9 %copy-start.66 = (s32[4]{0:T(128)S(1)}, s32[4]{0:T(128)}, u32[]{:S(2)}) copy-start(s32[4]{0:T(128)} %copy-done.65) | copy-start | bytes 52
  278.1 67.3 %collective-permute-start.41 = (bf16[768,2048]{1,0:T(8,128)(2,1)}, bf16[768,2048]{1,0:T(8,128)(2,1)S(1)}, u32[]{:S(2)}, u32[]{:S(2)}) collective-permute-start(bf16[768,2048]{1,0:T(8,128)(2,1)} %unit_grads_1.1.refs_0_), channel_id=1, source_target_pairs={{0,1},{1,0},{2,3},{3,2},{4,5},{5,4},{6,7},{7,6},{8,9},{9,8},{10,11... | collective-permute-start | bytes 9437192 | tf_op jit(solution)/shard_map/ppermute | solution.py:937
  278.1 12.0 %collective-permute-start.32 = (bf16[3,512,128]{2,1,0:T(8,128)(2,1)S(1)}, bf16[3,512,128]{2,1,0:T(8,128)(2,1)S(1)}, u32[]{:S(2)}, u32[]{:S(2)}) collective-permute-start(bf16[3,512,128]{2,1,0:T(8,128)(2,1)S(1)} %get-tuple-element.224), channel_id=1, source_target_pairs={{0,8},{1,9},{2,10},{3,11},{4,12},{5,13},{6,14},{7,15},{8,0},{9,1},... | collective-permute-start | bytes 1179656 | tf_op jit(solution)/shard_map/ppermute | solution.py:937
  280.0 11.9 %collective-permute-start.33 = (bf16[3,512,128]{2,1,0:T(8,128)(2,1)S(1)}, bf16[3,512,128]{2,1,0:T(8,128)(2,1)S(1)}, u32[]{:S(2)}, u32[]{:S(2)}) collective-permute-start(bf16[3,512,128]{2,1,0:T(8,128)(2,1)S(1)} %get-tuple-element.207.refs_0_), channel_id=1, source_target_pairs={{0,16},{1,17},{2,18},{3,19},{4,20},{5,21},{6,22},{7,23},{8,24},{9,... | collective-permute-start | bytes 1179656 | tf_op jit(solution)/shard_map/ppermute | solution.py:937
  280.1 39.5 %collective-permute-start.37 = (bf16[3,1024,128]{2,1,0:T(8,128)(2,1)}, bf16[3,1024,128]{2,1,0:T(8,128)(2,1)}, u32[]{:S(2)}, u32[]{:S(2)}) collective-permute-start(bf16[3,1024,128]{2,1,0:T(8,128)(2,1)} %get-tuple-element.230), channel_id=1, source_target_pairs={{0,8},{1,9},{2,10},{3,11},{4,12},{5,13},{6,14},{7,15},{8,0},{9,1},... | collective-permute-start | bytes 2359304 | tf_op jit(solution)/shard_map/ppermute | solution.py:937
  282.0 38.9 %collective-permute-start.38 = (bf16[3,1024,128]{2,1,0:T(8,128)(2,1)}, bf16[3,1024,128]{2,1,0:T(8,128)(2,1)}, u32[]{:S(2)}, u32[]{:S(2)}) collective-permute-start(bf16[3,1024,128]{2,1,0:T(8,128)(2,1)} %get-tuple-element.217.refs_0_), channel_id=1, source_target_pairs={{0,16},{1,17},{2,18},{3,19},{4,20},{5,21},{6,22},{7,23},{8,24},{9,... | collective-permute-start | bytes 2359304 | tf_op jit(solution)/shard_map/ppermute | solution.py:937
  290.9 6.3 %collective-permute-start.34 = (bf16[3,256,128]{2,1,0:T(8,128)(2,1)S(1)}, bf16[3,256,128]{2,1,0:T(8,128)(2,1)S(1)}, u32[]{:S(2)}, u32[]{:S(2)}) collective-permute-start(bf16[3,256,128]{2,1,0:T(8,128)(2,1)S(1)} %get-tuple-element.227), channel_id=1, source_target_pairs={{0,2},{1,3},{2,4},{3,5},{4,6},{5,7},{6,0},{7,1},{8,10},{9,11},{10,... | collective-permute-start | bytes 589832 | tf_op jit(solution)/shard_map/ppermute | solution.py:937
  292.7 80.7 %collective-permute-start.42 = (bf16[4,2,768,128]{3,2,1,0:T(8,128)(2,1)}, bf16[4,2,768,128]{3,2,1,0:T(8,128)(2,1)}, u32[]{:S(2)}, u32[]{:S(2)}) collective-permute-start(bf16[4,2,768,128]{3,2,1,0:T(8,128)(2,1)} %get-tuple-element.237), channel_id=1, source_target_pairs={{0,1},{1,0},{2,3},{3,2},{4,5},{5,4},{6,7},{7,6},{8,9},{9,8},{10,11... | collective-permute-start | bytes 4718600 | tf_op jit(solution)/shard_map/ppermute | solution.py:937
  297.8 8.2 %collective-permute-start.35 = (bf16[3,256,128]{2,1,0:T(8,128)(2,1)S(1)}, bf16[3,256,128]{2,1,0:T(8,128)(2,1)S(1)}, u32[]{:S(2)}, u32[]{:S(2)}) collective-permute-start(bf16[3,256,128]{2,1,0:T(8,128)(2,1)S(1)} %get-tuple-element.228), channel_id=1, source_target_pairs={{0,4},{1,5},{2,6},{3,7},{4,0},{5,1},{6,2},{7,3},{8,12},{9,13},{10,... | collective-permute-start | bytes 589832 | tf_op jit(solution)/shard_map/ppermute | solution.py:937
  306.8 10.8 %collective-permute-start.36 = (bf16[3,256,128]{2,1,0:T(8,128)(2,1)}, bf16[3,256,128]{2,1,0:T(8,128)(2,1)}, u32[]{:S(2)}, u32[]{:S(2)}) collective-permute-start(bf16[3,256,128]{2,1,0:T(8,128)(2,1)} %get-tuple-element.213.refs_0_), channel_id=1, source_target_pairs={{0,6},{1,7},{2,0},{3,1},{4,2},{5,3},{6,4},{7,5},{8,14},{9,15},{10,... | collective-permute-start | bytes 589832 | tf_op jit(solution)/shard_map/ppermute | solution.py:937
  317.5 27.0 %collective-permute-start.40 = (bf16[3,1024,128]{2,1,0:T(8,128)(2,1)S(1)}, bf16[3,1024,128]{2,1,0:T(8,128)(2,1)S(1)}, u32[]{:S(2)}, u32[]{:S(2)}) collective-permute-start(bf16[3,1024,128]{2,1,0:T(8,128)(2,1)S(1)} %get-tuple-element.225.refs_0_), channel_id=1, source_target_pairs={{0,16},{1,17},{2,18},{3,19},{4,20},{5,21},{6,22},{7,23},{8,24},{9,... | collective-permute-start | bytes 2359304 | tf_op jit(solution)/shard_map/ppermute | solution.py:937
  319.7 24.8 %collective-permute-start.39 = (bf16[3,1024,128]{2,1,0:T(8,128)(2,1)S(1)}, bf16[3,1024,128]{2,1,0:T(8,128)(2,1)S(1)}, u32[]{:S(2)}, u32[]{:S(2)}) collective-permute-start(bf16[3,1024,128]{2,1,0:T(8,128)(2,1)S(1)} %get-tuple-element.233), channel_id=1, source_target_pairs={{0,8},{1,9},{2,10},{3,11},{4,12},{5,13},{6,14},{7,15},{8,0},{9,1},... | collective-permute-start | bytes 2359304 | tf_op jit(solution)/shard_map/ppermute | solution.py:937
  356.9 4.3 %collective-permute-start.50 = (f32[8,2048]{1,0:T(8,128)S(1)}, f32[8,2048]{1,0:T(8,128)S(1)}, u32[]{:S(2)}, u32[]{:S(2)}) collective-permute-start(f32[8,2048]{1,0:T(8,128)S(1)} %get-tuple-element.235.refs_0_), channel_id=1, source_target_pairs={{0,8},{1,9},{2,10},{3,11},{4,12},{5,13},{6,14},{7,15},{8,0},{9,1},... | collective-permute-start | bytes 196616 | tf_op jit(solution)/shard_map/ppermute | solution.py:937
  357.9 15.5 %collective-permute-start.43 = (bf16[3,256,128]{2,1,0:T(8,128)(2,1)S(1)}, bf16[3,256,128]{2,1,0:T(8,128)(2,1)S(1)}, u32[]{:S(2)}, u32[]{:S(2)}) collective-permute-start(bf16[3,256,128]{2,1,0:T(8,128)(2,1)S(1)} %get-tuple-element.240), channel_id=1, source_target_pairs={{0,2},{1,3},{2,4},{3,5},{4,6},{5,7},{6,0},{7,1},{8,10},{9,11},{10,... | collective-permute-start | bytes 589832 | tf_op jit(solution)/shard_map/ppermute | solution.py:937
  361.3 4.3 %collective-permute-start.51 = (f32[8,2048]{1,0:T(8,128)S(1)}, f32[8,2048]{1,0:T(8,128)S(1)}, u32[]{:S(2)}, u32[]{:S(2)}) collective-permute-start(f32[8,2048]{1,0:T(8,128)S(1)} %add.50), channel_id=1, source_target_pairs={{0,16},{1,17},{2,18},{3,19},{4,20},{5,21},{6,22},{7,23},{8,24},{9,... | collective-permute-start | bytes 196616 | tf_op jit(solution)/shard_map/ppermute | solution.py:937
  362.2 11.2 %collective-permute-start.44 = (bf16[3,256,128]{2,1,0:T(8,128)(2,1)S(1)}, bf16[3,256,128]{2,1,0:T(8,128)(2,1)S(1)}, u32[]{:S(2)}, u32[]{:S(2)}) collective-permute-start(bf16[3,256,128]{2,1,0:T(8,128)(2,1)S(1)} %get-tuple-element.241), channel_id=1, source_target_pairs={{0,4},{1,5},{2,6},{3,7},{4,0},{5,1},{6,2},{7,3},{8,12},{9,13},{10,... | collective-permute-start | bytes 589832 | tf_op jit(solution)/shard_map/ppermute | solution.py:937
  362.6 35.1 %collective-permute-start.46 = (f32[3,256,128]{2,1,0:T(8,128)S(1)}, f32[3,256,128]{2,1,0:T(8,128)S(1)}, u32[]{:S(2)}, u32[]{:S(2)}) collective-permute-start(f32[3,256,128]{2,1,0:T(8,128)S(1)} %get-tuple-element.242), channel_id=1, source_target_pairs={{0,1},{1,0},{2,3},{3,2},{4,5},{5,4},{6,7},{7,6},{8,9},{9,8},{10,11... | collective-permute-start | bytes 1179656 | tf_op jit(solution)/shard_map/ppermute | solution.py:937
  365.6 4.3 %collective-permute-start.52 = (f32[8,2048]{1,0:T(8,128)S(1)}, f32[8,2048]{1,0:T(8,128)S(1)}, u32[]{:S(2)}, u32[]{:S(2)}) collective-permute-start(f32[8,2048]{1,0:T(8,128)S(1)} %add.51), channel_id=1, source_target_pairs={{0,2},{1,3},{2,0},{3,1},{4,6},{5,7},{6,4},{7,5},{8,10},{9,11},{10,... | collective-permute-start | bytes 196616 | tf_op jit(solution)/shard_map/ppermute | solution.py:937
  370.0 7.0 %collective-permute-start.53 = (f32[8,2048]{1,0:T(8,128)S(1)}, f32[8,2048]{1,0:T(8,128)S(1)}, u32[]{:S(2)}, u32[]{:S(2)}) collective-permute-start(f32[8,2048]{1,0:T(8,128)S(1)} %add.52), channel_id=1, source_target_pairs={{0,4},{1,5},{2,6},{3,7},{4,0},{5,1},{6,2},{7,3},{8,12},{9,13},{10,... | collective-permute-start | bytes 196616 | tf_op jit(solution)/shard_map/ppermute | solution.py:937
  373.4 16.3 %collective-permute-start.45 = (bf16[3,256,128]{2,1,0:T(8,128)(2,1)S(1)}, bf16[3,256,128]{2,1,0:T(8,128)(2,1)S(1)}, u32[]{:S(2)}, u32[]{:S(2)}) collective-permute-start(bf16[3,256,128]{2,1,0:T(8,128)(2,1)S(1)} %get-tuple-element.234.refs_0_), channel_id=1, source_target_pairs={{0,6},{1,7},{2,0},{3,1},{4,2},{5,3},{6,4},{7,5},{8,14},{9,15},{10,... | collective-permute-start | bytes 589832 | tf_op jit(solution)/shard_map/ppermute | solution.py:937
  373.4 24.3 %collective-permute-start.47 = (bf16[3,256,128]{2,1,0:T(8,128)(2,1)S(1)}, bf16[3,256,128]{2,1,0:T(8,128)(2,1)S(1)}, u32[]{:S(2)}, u32[]{:S(2)}) collective-permute-start(bf16[3,256,128]{2,1,0:T(8,128)(2,1)S(1)} %get-tuple-element.243), channel_id=1, source_target_pairs={{0,3},{1,2},{2,5},{3,4},{4,7},{5,6},{6,1},{7,0},{8,11},{9,10},{10,... | collective-permute-start | bytes 589832 | tf_op jit(solution)/shard_map/ppermute | solution.py:937
  373.4 24.2 %collective-permute-start.48 = (bf16[3,256,128]{2,1,0:T(8,128)(2,1)S(1)}, bf16[3,256,128]{2,1,0:T(8,128)(2,1)S(1)}, u32[]{:S(2)}, u32[]{:S(2)}) collective-permute-start(bf16[3,256,128]{2,1,0:T(8,128)(2,1)S(1)} %get-tuple-element.244), channel_id=1, source_target_pairs={{0,5},{1,4},{2,7},{3,6},{4,1},{5,0},{6,3},{7,2},{8,13},{9,12},{10,... | collective-permute-start | bytes 589832 | tf_op jit(solution)/shard_map/ppermute | solution.py:937
  377.0 20.7 %collective-permute-start.49 = (bf16[3,256,128]{2,1,0:T(8,128)(2,1)S(1)}, bf16[3,256,128]{2,1,0:T(8,128)(2,1)S(1)}, u32[]{:S(2)}, u32[]{:S(2)}) collective-permute-start(bf16[3,256,128]{2,1,0:T(8,128)(2,1)S(1)} %get-tuple-element.231.refs_0_), channel_id=1, source_target_pairs={{0,7},{1,6},{2,1},{3,0},{4,3},{5,2},{6,5},{7,4},{8,15},{9,14},{10,... | collective-permute-start | bytes 589832 | tf_op jit(solution)/shard_map/ppermute | solution.py:937
  389.6 12.8 %collective-permute-start.54 = (f32[8,2048]{1,0:T(8,128)S(1)}, f32[8,2048]{1,0:T(8,128)S(1)}, u32[]{:S(2)}, u32[]{:S(2)}) collective-permute-start(f32[8,2048]{1,0:T(8,128)S(1)} %add.53), channel_id=1, source_target_pairs={{0,1},{1,0},{2,3},{3,2},{4,5},{5,4},{6,7},{7,6},{8,9},{9,8},{10,11... | collective-permute-start | bytes 196616 | tf_op jit(solution)/shard_map/ppermute | solution.py:937
  (61 other events, 300.4 us)
Sparse Core Ops, SparseCore 0:
  41.1 113.5 all-gather.5

commit v3 on v2

--- a/solution.py
+++ b/solution.py
@@ -125,15 +125,14 @@
     )
 
 
-def quarter_kernel(ids, mine, recv, out, p0, p1):
+def quarter_kernel(ids, mine, recv, out, p0):
     q, c = ids[0], ids[2]
     half = out.shape[0]
     at = pl.ds(pl.multiple_of(lax.rem(q, 2) * half, half), half)
     first = (lax.div(q, 2) == c).astype(jnp.int32) == 1
     val = jnp.where(first, mine[at, :], recv[at, :])
     out[...] = val[:, 1536:]
-    p0[...] = val[:, :768]
-    p1[...] = val[:, 768:1536]
+    p0[...] = val[:, :1536]
 
 
 def quarter_of(ids, deps, mine, recv):
@@ -141,7 +140,7 @@
     half = rows // 2
     return call_flat(
         quarter_kernel, "quarter_of", ids, deps, [mine, recv], [NEAR, NEAR],
-        [sds((half, 1536), BF), sds((half, 768), BF), sds((half, 768), BF)], 16,
+        [sds((half, 1536), BF)] * 2, 8,
         cost(0, rows * cols * 4),
     )
 
@@ -157,19 +156,48 @@
     )
 
 
-def plane_kernel(ids, *refs):
+def gate_kernel(ids, *refs):
+    pass
+
+
+def gate(ids, deps, values, hold=None):
+    shape = {None: sds, "far": far, "near": near}[hold]
+    held = {None: lambda *v: list(v), "far": far_in, "near": near_in}[hold]
+    return call_flat(
+        gate_kernel, "gate", ids, deps, held(*values), [ANY] * len(values),
+        [shape(v.shape, v.dtype) for v in values], 4, cost(0, 1), out_specs=[ANY] * len(values),
+        aliases={n: n for n in range(len(values))},
+    )
+
+
+def add_kernel(ids, *refs):
+    total = refs[0][...]
+    for ref in refs[1:-1]:
+        total = total + ref[...]
+    refs[-1][...] = total
+
+
+def add_up(ids, deps, *values):
+    a = values[0]
+    return call_flat(
+        add_kernel, "add_up", ids, deps, list(values), [NEAR] * len(values), sds(a.shape, a.dtype),
+        4, cost(a.size, a.size * 4 * len(values)),
+    )
+
+
+def plane_kernel(s, ids, *refs):
     rel = refs[-1]
     row = 0
     for ref in refs[:-1]:
-        rel[row : row + ref.shape[0], :] = ref[...]
+        rel[row : row + ref.shape[0], :] = ref[:, s * 768 : (s + 1) * 768]
         row += ref.shape[0]
 
 
 def plane_pieces(s, ids, deps, parts):
     rows = sum(p.shape[0] for p in parts)
     return call_flat(
-        plane_kernel, f"plane_pieces_{s}", ids, deps, list(parts), [NEAR] * len(parts),
-        sds((rows, 768), BF), 16, cost(0, rows * 768 * 4),
+        functools.partial(plane_kernel, s), f"plane_pieces_{s}", ids, deps, list(parts),
+        [NEAR] * len(parts), sds((rows, 768), BF), 8, cost(0, rows * 768 * 4),
     )
 
 
@@ -387,14 +415,14 @@
     if s % 2:
         args.append(before)
         in_specs.append(NEAR)
-    out_shape = [near(shape, F32)] * 3 + [sds((32, 256), F32), sds((2, 8, 256), F32)]
+    out_shape = [near(shape, F32)] * 3 + [near((32, 256), F32), near((2, 8, 256), F32)]
     out_specs = [NEAR] * 5
     if not joined:
         out_shape.append(far((width, 768), BF))
         out_specs.append(ANY)
     return call_flat(
         functools.partial(proj_kernel, s, nz, joined), f"project_{s}", ids, deps, args, in_specs,
-        out_shape, 16, cost(2 * rows * width * 768, rows * width * 2 + width * 768 * 4),
+        out_shape, 12, cost(2 * rows * width * 768, rows * width * 2 + width * 768 * 4),
         scratch=[
             pltpu.VMEM((256, 1024), F32),
             pltpu.VMEM((16, 256), F32),
@@ -421,16 +449,16 @@
 
 def state_kernel(a, count, held, ids, *refs):
     fwd = (refs[0:4], refs[4:8])
-    ub, cot_own, cot_oth, lim, scl, vr, br, got = refs[8:16]
-    rest = refs[16 + (2 if held else 0) :]
+    ub, ulo, cot_own, cot_oth, lim, scl, vr, br, got = refs[8:17]
+    rest = refs[17 + (2 if held else 0) :]
     hown, hoth = rest[:2]
-    out = (rest[2:6], rest[6:10])
-    dzr, uu, lbs, summ, acc, st, pp, lb, ac, scr = rest[10:]
+    out = (rest[2:5], rest[5:8])
+    dzr, uu, lbs, summ, acc, st, pp, lb, ac, scr = rest[8:]
     tiles = dzr.shape[0]
     q, c = ids[0], ids[2]
     for n in range(2):
         cand, decay, rpre, plin = fwd[n]
-        bc, src, dstate, du0 = out[n]
+        bc, dstate, du0 = out[n]
         lanes = slice(n * 256, n * 256 + 256)
         carry = enter(got, n, True, q, count)
         for ks in range(4):
@@ -443,7 +471,7 @@
         lb[...] = jnp.zeros_like(lb)
         ac[...] = jnp.zeros_like(ac)
 
-        def tile(u0, u1, own0, own1, oth0, oth1, ho, ht):
+        def tile(u0, u1, ul, own0, own1, oth0, oth1, ho, ht):
             i = pl.program_id(0)
             for k, pair in enumerate(((own0, own1), (oth0, oth1))):
                 for b, ref in enumerate(pair):
@@ -470,7 +498,7 @@
                 state = jnp.concatenate(states, axis=0)
                 low = jnp.concatenate([u0[0, k, at, :], u1[0, k, at, :]], axis=1)
                 uu[i, k, at, lanes] = low
-                u = low.astype(F32)
+                u = low.astype(F32) + ul[0, k, at, :].astype(F32)
                 live = lim[row : row + 16, :] > i * STEPS
                 sc = jnp.where(live, scl[row : row + 16, :], 0.0)
                 gy = jnp.concatenate(
@@ -486,9 +514,8 @@
                 drl = ds * (1.0 - r) * gap
                 sr = dec * ds + wr * drl
                 dstate[i, k, at, :] = ds
-                src[i, k, at, :] = sr
                 bc[i, k, at, :] = before - cd
-                du0[i, k, at, :] = gy - ds
+                du0[i, k, at, :] = (gy - ds).astype(BF)
                 dzr[i, k, at, lanes] = drl.astype(BF)
                 for d, v in zip(halves(dec), halves(sr)):
                     l[k] = l[k] + p[k] * v
@@ -510,6 +537,9 @@
                 (1, 2, 128, BLK), lambda i: (i, 0, 0, (2 * n + mm) * 4 + 2 * c + a)
             )
 
+        def tail():
+            return pl.BlockSpec((1, 2, 128, 256), lambda i: (i, 0, 0, 2 * a + n))
+
         def nat_own(mm):
             return pl.BlockSpec(
                 (*nat, STEPS, BLK), lambda i: (0, 0, i, (2 * n + mm) * 4 + 2 * c + a)
@@ -522,9 +552,9 @@
         pltpu.emit_pipeline(
             tile,
             grid=(tiles,),
-            in_specs=[unit(0), unit(1), nat_own(0), nat_own(1), nat_oth(0), nat_oth(1)],
+            in_specs=[unit(0), unit(1), tail(), nat_own(0), nat_own(1), nat_oth(0), nat_oth(1)],
             out_specs=[hspec, hspec],
-        )(ub, ub, cot_own, cot_own, cot_oth, cot_oth, hown, hoth)
+        )(ub, ub, ulo, cot_own, cot_own, cot_oth, cot_oth, hown, hoth)
         acc[n] = ac[...]
         lbs[n] = lb[...]
         for k in range(2):
@@ -535,7 +565,7 @@
                 summ[n, 4 + ks : 5 + ks, :] = tl
 
 
-def states(a, count, ids, deps, fwd, ub, cot_own, cot_oth, lim, scl, vr, br, got, held):
+def states(a, count, ids, deps, fwd, ub, ulo, cot_own, cot_oth, lim, scl, vr, br, got, held):
     tiles = ub.shape[0]
     rows = tiles * 128
     one = (tiles, 2, 128, 256)
@@ -545,37 +575,37 @@
     for f in fwd:
         args += near_in(*f[:3]) + [f[3]]
         in_specs += [NEAR] * 4
-    args += far_in(ub, cot_own, cot_oth) + [lim, scl, vr[:, chan], br[:, chan], got]
-    in_specs += [ANY] * 3 + [NEAR] * 5
+    args += far_in(ub, ulo, cot_own, cot_oth) + [lim, scl, vr[:, chan], br[:, chan], got]
+    in_specs += [ANY] * 4 + [NEAR] * 5
     aliases = {}
     if held:
         aliases = {len(args): 0, len(args) + 1: 1}
         args += far_in(*held)
         in_specs += [ANY] * 2
-    small = sds((2, 16, 256), F32)
+    small = near((2, 16, 256), F32)
     return call_flat(
         functools.partial(state_kernel, a, count, bool(held)), f"states_{a}", ids, deps, args,
         in_specs,
         [far((4, 2, rows, BLK), BF)] * 2
-        + [near(one, F32)] * 8
+        + [near(one, F32), near(one, F32), near(one, BF)] * 2
         + [near(two, BF)] * 2
-        + [small, sds((2, 8, 256), F32), small],
-        16, cost(rows * 1024 * 60, rows * 1024 * 10, rows * 1024 * 2),
+        + [small, near((2, 8, 256), F32), small],
+        10, cost(rows * 1024 * 60, rows * 1024 * 10, rows * 1024 * 2),
         scratch=[pltpu.VMEM((16, 256), F32)] * 4 + [pltpu.VMEM((2, 256, BLK), F32)],
-        out_specs=[ANY] * 2 + [NEAR] * 13,
+        out_specs=[ANY] * 2 + [NEAR] * 11,
         aliases=aliases,
     )
 
 
 def adjoint_kernel(count, ids, *refs):
-    ins = (refs[0:6], refs[6:12])
-    uu, vf, lbs, got, du, dzc, dzf, acc, adj = refs[12:]
+    ins = (refs[0:5], refs[5:10])
+    dzr, uu, vf, vr, lbs, got, du, dzc, dzf, acc, adj = refs[10:]
     tiles = du.shape[0]
     q = ids[0]
     for n in range(2):
-        decay, bc, src, dstate, du0, plin = ins[n]
+        decay, bc, dstate, du0, plin = ins[n]
         lanes = slice(n * 256, n * 256 + 256)
-        wf = vf[:, lanes]
+        wf, wr = vf[:, lanes], vr[:, lanes]
         after = enter(got, n, False, q, count)
         for ks in range(4):
             cc = after[ks : ks + 1]
@@ -591,7 +621,7 @@
                 at = slice(r0, r0 + 16)
                 dec = decay[i, k, at, :]
                 ds = dstate[i, k, at, :]
-                sr = src[i, k, at, :]
+                sr = dec * ds + wr * dzr[i, k, at, lanes].astype(F32)
                 late = ds[8:] + cur[k]
                 cur[k] = dec[8:] * cur[k] + sr[8:]
                 early = ds[:8] + cur[k]
@@ -600,7 +630,7 @@
                 dfl = dcand * bc[i, k, at, :] * dec
                 dzc[i, k, at, lanes] = dcand.astype(BF)
                 dzf[i, k, at, lanes] = dfl.astype(BF)
-                du[i, k, at, lanes] = du0[i, k, at, :] + dfl * wf
+                du[i, k, at, lanes] = (du0[i, k, at, :].astype(F32) + dfl * wf).astype(BF)
                 w = dfl * uu[i, k, at, lanes].astype(F32)
                 peep = peep + (w[:8] + w[8:])
                 bias = bias + (dfl[:8] + dfl[8:])
@@ -612,23 +642,33 @@
         acc[n, 8:16, :] = end[3]
 
 
-def adjoints(a, count, ids, deps, fwd, mid, uu, vf, lbs, got):
+def adjoints(a, count, ids, deps, fwd, mid, dzr, uu, vf, vr, lbs, got):
     tiles = uu.shape[0]
     rows = tiles * 128
     shape = (tiles, 2, 128, 512)
     args = []
     for f, m in zip(fwd, mid):
         args += near_in(f[1], *m) + [f[3]]
-    args += near_in(uu) + [vf[:, a * 512 : a * 512 + 512], lbs, got]
+    chan = slice(a * 512, a * 512 + 512)
+    args += near_in(dzr, uu) + [vf[:, chan], vr[:, chan], lbs, got]
     return call_flat(
         functools.partial(adjoint_kernel, count), f"adjoints_{a}", ids, deps, args,
         [NEAR] * len(args),
-        [near(shape, F32), near(shape, BF), near(shape, BF), sds((2, 16, 256), F32)],
-        16, cost(rows * 1024 * 20, rows * 1024 * 4), scratch=[pltpu.VMEM((16, 256), F32)],
-    )
-
-
-def wgrad_kernel(which, nz, ids, ubt, dzc, dzf, dzr, own, xp, yp, da, db, scr):
+        [near(shape, BF)] * 3 + [near((2, 16, 256), F32)],
+        6, cost(rows * 1024 * 20, rows * 1024 * 4), scratch=[pltpu.VMEM((16, 256), F32)],
+    )
+
+
+def wgrad_kernel(which, nz, n_kept, ids, ubt, dzc, dzf, dzr, *rest):
+    kept, rest = rest[: max(n_kept - 3, 0)], rest[max(n_kept - 3, 0) :]
+    own, xp, yp, da, db = rest[:5]
+    scr, sems = rest[5 + n_kept :]
+    copies = [
+        pltpu.make_async_copy(src, dst, sems.at[n])
+        for n, (src, dst) in enumerate(zip((dzc, dzf, dzr, *kept), rest[5 : 5 + n_kept]))
+    ]
+    for copy in copies:
+        copy.start()
     q, c = ids[0], ids[2]
     rh = 1 - c if which == "other" else c
     half = scr.shape[0]
@@ -665,17 +705,23 @@
     pltpu.emit_pipeline(
         tile, grid=(nz,), in_specs=[pl.BlockSpec((half, rows), lambda i: (2 * i + rh, 0))]
     )(ubt)
-
-
-def weight_grad_part(which, nz, ids, deps, ubt, dz):
+    for copy in copies:
+        copy.wait()
+
+
+def weight_grad_part(which, nz, ids, deps, ubt, dz, keep=()):
     width, rows = ubt.shape
     half = width // nz // 2
-    return call_flat(
-        functools.partial(wgrad_kernel, which, nz), "weight_grad_part", ids, deps,
-        [*far_in(ubt), *near_in(*dz)], [ANY] + [NEAR] * 3,
-        [sds((3, nz * half, BLK), BF)] * 3 + [sds((3, nz * half // 2, BLK), BF)] * 2,
-        16, cost(2 * rows * nz * half * 1536, rows * width + width * 1536),
-        scratch=[pltpu.VMEM((half, 1536), BF)],
+    kept = (*dz, *keep) if keep else ()
+    return call_flat(
+        functools.partial(wgrad_kernel, which, nz, len(kept)), "weight_grad_part", ids, deps,
+        [*far_in(ubt), *near_in(*dz, *keep)], [ANY] + [NEAR] * (3 + len(keep)),
+        [sds((3, nz * half, BLK), BF)] * 3
+        + [sds((3, nz * half // 2, BLK), BF)] * 2
+        + [far(v.shape, v.dtype) for v in kept],
+        10, cost(2 * rows * nz * half * 1536, rows * width + width * 1536),
+        scratch=[pltpu.VMEM((half, 1536), BF), pltpu.SemaphoreType.DMA((4,))],
+        out_specs=[NEAR] * 5 + [ANY] * len(kept),
     )
 
 
@@ -713,17 +759,45 @@
     )
 
 
-def total_kernel(ids, *refs):
-    total = refs[0][...].astype(F32)
-    for ref in refs[1:-1]:
-        total = total + ref[...].astype(F32)
-    refs[-1][...] = total
-
-
-def total_of(ids, deps, parts):
-    return call_flat(
-        total_kernel, "total_of", ids, deps, list(parts), [NEAR] * len(parts),
-        sds(parts[0].shape, F32), 16, cost(parts[0].size * 4, parts[0].size * 14),
+def fold_kernel(sets, d, ids, *refs):
+    n = sum(len(g) for g in sets) if sets else 2
+    srcs, outs = refs[:n], refs[n:]
+    if sets:
+        groups, at = [], 0
+        for g in sets:
+            groups.append(srcs[at : at + len(g)])
+            at += len(g)
+    else:
+        groups = [[ref.at[g] for ref in srcs] for g in range(srcs[0].shape[0])]
+    half = groups[0][0].shape[1] // 2
+    bit = lax.rem(lax.div(ids[1], d), 2) if d else 0
+    for g, parts in enumerate(groups):
+        spots = ((outs[0], bit), (outs[1], 1 - bit)) if d else ((outs[g], None),)
+        for out, where in spots:
+            rows = slice(None) if where is None else pl.ds(pl.multiple_of(where * half, half), half)
+            total = parts[0][:, rows, :].astype(F32)
+            for part in parts[1:]:
+                total = total + part[:, rows, :].astype(F32)
+            if d:
+                out[g] = total.astype(out.dtype)
+            else:
+                out[...] = total
+
+
+def fold_z(d, ids, deps, sets):
+    stacked = not isinstance(sets[0], (list, tuple))
+    args = list(sets) if stacked else [v for g in sets for v in g]
+    count = sets[0].shape[0] if stacked else len(sets)
+    _, rows, _ = args[0].shape[-3:]
+    if d:
+        shape = (count, 3, rows // 2, BLK)
+        out_shape = [sds(shape, F32), sds(shape, BF)]
+    else:
+        out_shape = [sds((3, rows, BLK), F32)] * count
+    return call_flat(
+        functools.partial(fold_kernel, None if stacked else [tuple(g) for g in sets], d), "fold_z",
+        ids, deps, args, [NEAR] * len(args), out_shape, 8,
+        cost(rows * 768 * count, rows * 384 * 10 * count),
     )
 
 
@@ -731,58 +805,97 @@
 TILE_N = 512
 
 
-def unit_kernel(k, ids, c0, f0, r0, c1, f1, r1, e0, e1, w0, w1, w2, out, lhs, acc):
+def unit_kernel(k, ids, *refs):
+    first, second, ws = refs[0:4], refs[4:8], refs[8:11]
+    far_out, out, lhs, e0, wbuf, sems, wsems, osems = refs[12 if k == 0 else 11 :]
     c = ids[2]
-    rows = acc.shape[0]
-    for a, refs in enumerate(((c0, f0, r0), (c1, f1, r1))):
-        for mp in range(2):
-            for g, ref in enumerate(refs):
-                dst = a * 1536 + mp * 768 + g * 256
-                val = ref[:, k, :, mp * 256 : (mp + 1) * 256]
-                lhs[:, dst : dst + 256] = val.reshape(rows, 256)
-
-    def tile(wa, wb, wc):
-        m = pl.program_id(0)
-        acc[:, :TILE_N] = lax.dot_general(
-            lhs[:, :768], wa[...], DIMS, preferred_element_type=F32
-        ) + lax.dot_general(lhs[:, 768:1536], wb[...], DIMS, preferred_element_type=F32)
-        acc[:, :TILE_N] += lax.dot_general(lhs[:, 1536:], wc[...], DIMS, preferred_element_type=F32)
-        for a, ref in enumerate((e0, e1)):
-            val = ref[:, k, :, pl.ds(pl.multiple_of(m * BLK, BLK), BLK)]
-            acc[:, pl.ds(core_lane(a, 0, c), BLK)] += val.reshape(rows, BLK)
-        out[:, pl.ds(pl.multiple_of(m * TILE_N, TILE_N), TILE_N)] = acc[...].astype(out.dtype)
-
-    blk = lambda w: pl.BlockSpec((TILE_N, w.shape[1]), lambda i: (i, 0))
-    pltpu.emit_pipeline(
-        tile, grid=(w0.shape[0] // TILE_N,), in_specs=[blk(w0), blk(w1), blk(w2)]
-    )(w0, w1, w2)
-
-
-def unit_grads(k, ids, deps, dz0, dz1, e0, e1, ws):
-    tiles = e0.shape[0]
+    rows = out.shape[0]
+    tiles = ws[0].shape[0] // TILE_N
+
+    def fetch(m):
+        slot, lane, copies = m % 2, 0, []
+        for n, w in enumerate(ws):
+            cols = w.shape[1]
+            dst = wbuf.at[slot, :, lane : lane + cols]
+            src = w.at[m * TILE_N : (m + 1) * TILE_N, :]
+            copies.append(pltpu.make_async_copy(src, dst, wsems.at[slot, n]))
+            lane += cols
+        return copies
+
+    copies = [(first[3].at[:, k], e0)]
+    for mp in range(2):
+        for g, ref in enumerate(first[:3]):
+            dst = mp * 768 + g * 256
+            src = ref.at[:, k, :, mp * 256 : (mp + 1) * 256]
+            copies.append((src, lhs.at[:, :, dst : dst + 256]))
+    copies = [pltpu.make_async_copy(a, b, sems.at[n]) for n, (a, b) in enumerate(copies)]
+    for copy in copies + fetch(0):
+        copy.start()
+    for mp in range(2):
+        for g, ref in enumerate(second[:3]):
+            dst = 1536 + mp * 768 + g * 256
+            lhs[:, :, dst : dst + 256] = ref[:, k, :, mp * 256 : (mp + 1) * 256]
+    for copy in copies:
+        copy.wait()
+    moved = []
+    for m in range(tiles):
+        if m + 1 < tiles:
+            for copy in fetch(m + 1):
+                copy.start()
+        for copy in fetch(m):
+            copy.wait()
+        lo = m * TILE_N
+        left = lhs[...].reshape(rows, 3072)
+        acc = lax.dot_general(left, wbuf[m % 2], DIMS, preferred_element_type=F32)
+        out[:, lo : lo + TILE_N] = acc.astype(out.dtype)
+        cols = slice(m * BLK, (m + 1) * BLK)
+        for a, val in enumerate((e0[:, :, cols], second[3][:, k, :, cols])):
+            lane = pl.ds(pl.multiple_of(lo + a * BLK + c * 256, BLK), BLK)
+            total = out[:, lane].astype(F32) + val.reshape(rows, BLK).astype(F32)
+            out[:, lane] = total.astype(out.dtype)
+        slot = 1 - c if k else c
+        done = pltpu.make_async_copy(
+            out.at[:, lo : lo + TILE_N], far_out.at[slot, :, lo : lo + TILE_N], osems.at[m]
+        )
+        done.start()
+        moved.append(done)
+    for done in moved:
+        done.wait()
+
+
+def unit_grads(k, ids, deps, first, second, ws, held):
+    tiles = first[0].shape[0]
     rows, width = tiles * 128, ws[0].shape[0]
-    return call_flat(
-        functools.partial(unit_kernel, k), f"unit_grads_{k}", ids, deps,
-        [*near_in(*dz0, *dz1, e0, e1), *far_in(*ws)], [NEAR] * 8 + [ANY] * 3,
-        near((rows, width), BF if k else F32), 24,
-        cost(2 * rows * width * 3072, width * 3072 * 2),
-        scratch=[pltpu.VMEM((rows, 3072), BF), pltpu.VMEM((rows, TILE_N), F32)],
-    )
-
-
-def norm_grad_kernel(ids, du_own, recv, tok, cot, lim, scl, gain, *rest):
+    args = [*far_in(*first), *near_in(*second), *far_in(*ws)]
+    return call_flat(
+        functools.partial(unit_kernel, k), f"unit_grads_{k}", ids, deps, args + far_in(*held),
+        [ANY] * 4 + [NEAR] * 4 + [ANY] * (3 + len(held)),
+        far((2, rows, width), BF), 24, cost(2 * rows * width * 3072, width * 3072 * 2),
+        scratch=[
+            pltpu.VMEM((rows, width), BF),
+            pltpu.VMEM((tiles, 128, 3072), BF),
+            pltpu.VMEM((tiles, 128, 512), BF),
+            pltpu.VMEM((2, TILE_N, 3072), BF),
+            pltpu.SemaphoreType.DMA((7,)),
+            pltpu.SemaphoreType.DMA((2, 3)),
+            pltpu.SemaphoreType.DMA((width // TILE_N,)),
+        ],
+        out_specs=ANY, aliases={len(args): 0} if held else {},
+    )
+
+
+def norm_grad_kernel(ids, du2, tok, cot, lim, scl, gain, *rest):
     accb, accc = rest[:2], rest[2:4]
     out, sums, ga, ba, scr = rest[4:]
     c = ids[2]
     ga[...] = jnp.zeros_like(ga)
     ba[...] = jnp.zeros_like(ba)
 
-    def tile(tokr, cotr, outr):
+    def tile(dur, tokr, cotr, outr):
         i = pl.program_id(0)
-        rows = pl.ds(pl.multiple_of(i * 128, 128), 128)
         for j in range(scr.shape[0]):
             lanes = slice(j * BLK, (j + 1) * BLK)
-            scr[j] = du_own[rows, lanes] + recv[rows, lanes].astype(F32)
+            scr[j] = dur[0, :, lanes].astype(F32) + dur[1, :, lanes].astype(F32)
         step = lax.broadcasted_iota(jnp.int32, (STEPS, 1), 0) + i * STEPS
         gsum = jnp.zeros(ga.shape, F32)
         bsum = jnp.zeros(ba.shape, F32)
@@ -810,8 +923,11 @@
     seqs, parts, steps, width = tok.shape
     nat = pl.BlockSpec((seqs, parts, STEPS, width), lambda i: (0, 0, i, 0))
     pltpu.emit_pipeline(
-        tile, grid=(steps // STEPS,), in_specs=[nat, nat], out_specs=[nat]
-    )(tok, cot, out)
+        tile,
+        grid=(steps // STEPS,),
+        in_specs=[pl.BlockSpec((2, 128, width), lambda i: (0, i, 0)), nat, nat],
+        out_specs=[nat],
+    )(du2, tok, cot, out)
     sums[...] = jnp.zeros_like(sums)
     sums[4:5, :] = jnp.sum(ga[...], axis=0, keepdims=True)
     sums[5:6, :] = jnp.sum(ba[...], axis=0, keepdims=True)
@@ -830,14 +946,14 @@
                 sums[j : j + 1, lane] = val[:, mm * BLK : (mm + 1) * BLK]
 
 
-def norm_grads(ids, deps, du_own, recv, tok, cot, lim8, scale, gain, accb, accc):
-    rows, width = du_own.shape
+def norm_grads(ids, deps, du2, tok, cot, lim8, scale, gain, accb, accc):
+    _, rows, width = du2.shape
     n = rows * width
     return call_flat(
         norm_grad_kernel, "norm_grads", ids, deps,
-        [*near_in(du_own, recv), *far_in(tok, cot), lim8, scale, gain, *accb, *accc],
-        [NEAR] * 2 + [ANY] * 2 + [SMEM] * 2 + [NEAR] * 5,
-        [far(tok.shape, F32), sds((8, width), F32)], 20, cost(n * 20, n * 8),
+        [*far_in(du2, tok, cot), lim8, scale, gain, *accb, *accc],
+        [ANY] * 3 + [SMEM] * 2 + [NEAR] * 5,
+        [far(tok.shape, F32), sds((8, width), F32)], 14, cost(n * 20, n * 8),
         scratch=[
             pltpu.VMEM((8, width), F32),
             pltpu.VMEM((8, width), F32),
@@ -978,6 +1094,8 @@
     lim = spread_rows(lim16[:, None, :, None] - step_in_tile)
     scl = spread_rows(scale[:, None, None, None])
 
+    lim8, scale1 = lim16[0], scale[:1]
+
     def by_core(vec):
         v = lax.dynamic_slice_in_dim(vec.reshape(4, 4, BLK), 2 * c, 2, 1)
         return v.transpose(1, 0, 2).reshape(1, width // 2)
@@ -987,9 +1105,11 @@
 
     tail = [mine]
 
-    def run(kernel, *head, rest=(), token=-1, after=()):
+    def run(kernel, *head, rest=(), token=-1, after=(), big=False):
         out = kernel(*head, ids, (tail[0], *after), *rest)
         tail[0] = out[token] if isinstance(out, (list, tuple)) else out
+        if big:
+            (tail[0],) = far_in(tail[0])
         return out
 
     groups = [[cc + 2 * zz for zz in range(nz)] for cc in range(2)]
@@ -1019,102 +1139,114 @@
         return run(project, s, nz, rest=rest, token=4, after=after)
 
     def run_states(a, fwd, got, held, after=()):
-        rest = (fwd, ub, cot4, cot_oth, lim, scl, vr, brst, got, held)
+        rest = (fwd, ub, ulo, cot4, cot_oth, lim, scl, vr, brst, got, held)
         out = run(states, a, nseq, rest=rest, after=after)
         return {
-            "h": out[:2], "mid": (out[2:6], out[6:10]), "dzr": out[10], "u": out[11],
-            "lbs": out[12], "summ": out[13], "acc": out[14],
+            "h": out[:2], "mid": (out[2:5], out[5:8]), "dzr": out[8], "u": out[9],
+            "lbs": out[10], "summ": out[11], "acc": out[12],
         }
 
     def run_adjoints(a, fwd, m, got, after=()):
-        rest = (fwd, m["mid"], m["u"], vf, m["lbs"], got)
+        rest = (fwd, m["mid"], m["dzr"], m["u"], vf, vr, m["lbs"], got)
         du, dzc, dzf, acc = run(adjoints, a, nseq, rest=rest, after=after)
         return {"du": du, "dz": (dzc, dzf, m["dzr"]), "acc": acc}
 
-    def sum_1(which, dz, after=()):
-        own, xp, yp, da, db = run(weight_grad_part, which, nz, rest=(ubt, dz), after=after)
-        return own, xp, yp, send(da, to_x), send(db, to_y)
+    def sum_1(which, dz, keep=(), after=()):
+        own, xp, yp, da, db, *kept = run(
+            weight_grad_part, which, nz, rest=(ubt, dz, keep), token=3, after=after
+        )
+        return (own, xp, yp, send(da, to_x), send(db, to_y)), kept
 
     def sum_2(got):
         own, xp, yp, ra, rb = got
         s1, s2 = run(relay_sums, rest=(xp, yp, ra, rb))
         return own, send(s1, to_x), send(s2, to_y)
 
-    def sum_3(got, cross):
+    def fold(sets, d):
+        kept, out = run(fold_z, d, rest=(sets,))
+        return kept, send(out, lambda qq, zz, cc: (qq, zz ^ d, cc))
+
+    def sum_3_now(got):
         if nz > 4:
-            own, r1, r2 = got
-            total = own.astype(F32) + r1.astype(F32) + r2.astype(F32)
-            total = lax.psum_scatter(
-                total, "dp", scatter_dimension=1, axis_index_groups=groups, tiled=True
-            )
-            return [send(total, to_core) if cross else total]
+            got, d = [got], nz // 2
+            while d:
+                got, d = fold(got, d), d // 2
+            return run(fold_z, 0, rest=(got,))
         parts = list(run(plane_sums, nz, rest=got))
-        if cross:
-            return [send(parts[k], shift_zc(k)) for k in range(nz)]
         return parts[:1] + [send(parts[k], shift_z(k)) for k in range(1, nz)]
 
-    def sum_4(got):
-        return [run(total_of, rest=(got,))]
-
-    last, p0, p1 = run(quarter_of, rest=(mine, recv))
-    z0 = along_z(p0)
-    z1 = along_z(p1)
-    ub, ubt, ulo = run(norm_tokens, rest=(tok4, tok_oth, gain, bias), after=(cot_oth,))
-    g0 = gather_1(0, z0)
+    def fold_rest(got):
+        d = nz // 4
+        while d:
+            got, d = fold(got, d), d // 2
+        return got
+
+    last, low = run(quarter_of, rest=(mine, recv), after=(tok_oth, cot_oth, len_oth))
+    along = along_z(low)
+    ub, ubt, ulo = run(
+        norm_tokens, rest=(tok4, tok_oth, gain, bias), big=True, after=(lim8, scale1)
+    )
+    g0 = gather_1(0, along)
     every = [
         [qq * ndp + zz * 2 + cc for zz in range(nz) for qq in range(nseq)] for cc in range(2)
     ]
     last = run(hand_on, rest=(last,))
     w_hi = lax.all_gather(last, axes, axis=0, tiled=True, axis_index_groups=every)
     g0 = gather_2(0, g0)
-    g1 = gather_1(1, z1)
+    g1 = gather_1(1, along)
     f0 = run_project(0, (mine, recv, *g0))
     g1 = gather_2(1, g1)
     f1 = run_project(1, (mine, recv, *g1), f0[4])
     m0 = run_states(0, (f0, f1), spread(f1[4]), ())
     d0 = run_adjoints(0, (f0, f1), m0, spread(m0["summ"]))
-    s0 = sum_1("other", d0["dz"])
+    s0, _ = sum_1("other", d0["dz"])
+    s1, first = sum_1("own", d0["dz"], (d0["du"],))
+    s0 = sum_2(s0)
     f2 = run_project(2, (w_hi,))
-    s0 = sum_2(s0)
+    s1 = sum_2(s1)
     f3 = run_project(3, (w_hi,), f2[4])
-    got = spread(f3[4])
-    s1 = sum_1("own", d0["dz"], after=(got,))
-    m1 = run_states(1, (f2, f3), got, m0["h"])
-    got = spread(m1["summ"])
+    m1 = run_states(1, (f2, f3), spread(f3[4]), m0["h"], after=s0[1:])
+    s01 = fold([s0, s1], nz // 2)
+    hrcv = send(run(gate, rest=(m1["h"][1:], "far"))[0], to_core)
+    got = spread(run(hand_on, rest=(m1["summ"],)))
     d1 = run_adjoints(1, (f2, f3), m1, got)
-    s1 = sum_2(s1)
-    s0 = sum_3(s0, True)
-    s2 = sum_1("other", d1["dz"])
-    s3 = sum_1("own", d1["dz"])
-    s0 = sum_4(s0)
-    s1 = sum_3(s1, False)
+    s2, _ = sum_1("other", d1["dz"])
+    s3, _ = sum_1("own", d1["dz"], after=(hrcv,))
     s2 = sum_2(s2)
-    parts = (d0["dz"], d1["dz"], d0["du"], d1["du"], (f0[5], f1[5], w_hi))
-    dur = send(run(unit_grads, 1, rest=parts), to_core)
+    s01 = fold_rest(s01)
+    second = (*d1["dz"], d1["du"])
+    ws = (f0[5], f1[5], w_hi)
+    du2 = run(unit_grads, 1, rest=(first, second, ws, ()), big=True)
     s3 = sum_2(s3)
-    s1 = sum_4(s1)
-    s2 = sum_3(s2, True)
-    own = run(unit_grads, 0, rest=parts)
-    s3 = sum_3(s3, False)
+    s2 = fold([s2], nz // 2)
+    du2 = run(unit_grads, 0, rest=(first, second, ws, (du2,)), big=True)
+    s0, s1 = run(fold_z, 0, rest=(s01,))
+    s0 = send(s0, to_core)
+    cores = [[2 * zz, 2 * zz + 1] for zz in range(nz)]
+    du2 = lax.all_to_all(du2, "dp", 0, 0, axis_index_groups=cores, tiled=True)
+    activations = run(activations_of, rest=(tok4, m1["h"][0], hrcv), big=True)
+    s2 = fold_rest(s2)
     input_grad, sums = run(
         norm_grads,
         rest=(
-            own, dur, tok4, cot4, lim16[0], scale[:1], gain, (m0["acc"], m1["acc"]),
-            (d0["acc"], d1["acc"]),
+            du2, tok4, cot4, lim8, scale1, gain, (m0["acc"], m1["acc"]), (d0["acc"], d1["acc"])
         ),
-    )
-    hrcv = send(m1["h"][1], to_core)
-    bit = 1
-    while bit < nseq:
-        sums = sums + send(sums, lambda qq, zz, cc, b=bit: (qq ^ b, zz, cc))
-        bit *= 2
-    bit = 1
-    while bit < nz:
-        sums = sums + send(sums, lambda qq, zz, cc, b=bit: (qq, zz ^ b, cc))
-        bit *= 2
-    sums = sums + send(sums, to_core)
-    activations = run(activations_of, rest=(tok4, m1["h"][0], hrcv))
-    weight_grad = run(assemble, rest=((s1, s3, s0, s2),))
+        after=(s0,),
+    )
+    if nz <= 4:
+        moved = [send(sums, shift_z(k)) for k in range(1, nz)]
+    s3 = sum_3_now(s3)
+    s2 = send(run(fold_z, 0, rest=(s2,))[0], to_core)
+    if nz <= 4:
+        sums = run(add_up, rest=(sums, *moved))
+    hops = [lambda qq, zz, cc, b=1 << b: (qq ^ b, zz, cc) for b in range((nseq - 1).bit_length())]
+    hops.append(to_core)
+    if nz > 4:
+        hops += [lambda qq, zz, cc, b=1 << b: (qq, zz ^ b, cc) for b in range((nz - 1).bit_length())]
+    for hop in hops:
+        sums = run(add_up, rest=(sums, send(sums, hop)))
+    s3 = run(fold_z, 0, rest=([s3],))
+    weight_grad = run(assemble, rest=(([s1], s3, [s0], [s2]),))
     shape = tokens.shape
     return (
         activations.reshape(shape),

time: 414 us -> 403 us (0.973)
  local copies, waits for them, and re-layouts: 26.5 us -> 10.2 us
  starting transfers between devices: 55.8 us -> 44.1 us
  blocking collectives: 34.1 us -> 45.5 us
  Pallas kernels: 191 us -> 200 us
  waiting for transfers between devices: 86.6 us -> 78.8 us
    unnamed x138 -> x56, local copies, waits for them, and re-layouts: 22.3 us -> 6.18 us
    ppermute x55 -> x47, starting transfers between devices: 55.7 us -> 44.1 us  [send(): return lax.ppermute(value, axes, table(move))]
    all_to_all x0 -> x1, blocking collectives: none -> 9.98 us  [local(): du2 = lax.all_to_all(du2, 'dp', 0, 0, axis_index_groups=cores, tiled=True)]
    pallas_call x32 -> x40, Pallas kernels: 166 us -> 175 us  [call_flat(): pl.pallas_call(body, in_specs=[SMEM] + dep_specs + in_specs, out_specs=ou...]
    ppermute x55 -> x47, waiting for transfers between devices: 86.6 us -> 78.8 us  [send(): return lax.ppermute(value, axes, table(move))]
  transfers between devices with their start and end apart: 56 -> 48, of which waited for: 20 -> 21; matrix products, arithmetic and copies ran while one was open for 1% -> 1% of each run, Pallas kernels for 41% -> 48%
where the time goes in v3:
time: 403 us; the launch traced here: 396 us
  Pallas kernels  200 us (50%)
  waiting for transfers between devices  78.8 us (20%)
  blocking collectives  45.5 us (11%)
  starting transfers between devices  44.1 us (11%)
  between operations  15.2 us (4%)
  local copies, waits for them, and re-layouts  10.2 us (3%)
    pallas_call x40, Pallas kernels, call_flat(): pl.pallas_call(body, in_specs=[SMEM] + dep_specs + in_specs, out_specs=ou...  175 us
    ppermute x47, waiting for transfers between devices, send(): return lax.ppermute(value, axes, table(move))  78.8 us
    ppermute x47, starting transfers between devices, send(): return lax.ppermute(value, axes, table(move))  44.1 us
    all_gather x4, blocking collectives, spread(): return lax.all_gather(both, 'seq')  35.5 us
    pallas_call x3, Pallas kernels, call(): pl.pallas_call(body, grid_spec=pltpu.PrefetchScalarGridSpec(num_scalar_pr...  25 us
    all_to_all x1, blocking collectives, local(): du2 = lax.all_to_all(du2, 'dp', 0, 0, axis_index_groups=cores, tiled=True)  9.98 us
  transfers between devices with their start and end apart: 48, of which 21 were waited for; matrix products, arithmetic and copies ran while one was open for 1% of the time, Pallas kernels for 48%

profile of v3, /device:TPU:10, one launch (start us, length us, event | category | flops | bytes accessed | tf_op | source)
XLA Modules:
  0.0 395.5 jit_solution(1730105505673821355)
XLA Ops:
  7.3 1.5 constant_dynamic-slice_fusion.3
  8.8 1.4 pad_maximum_fusion
  10.7 3.7 split_weight.1
  15.0 2.6 collective-permute-done.2.refs_3_
  18.2 2.3 quarter_of.1
  21.2 1.6 collective-permute-start.6
  24.1 1.8 collective-permute-start.4
  26.0 12.6 %norm_tokens.1 = (bf16[6,2,128,2048]{3,2,1,0:T(8,128)(2,1)}, bf16[2048,1536]{1,0:T(8,128)(2,1)}, bf16[6,2,128,1024]{3,2,1,0:T(8,128)(2,1)}) custom-call(s32[3]{0:T(128)S(1)} %pad_add_fusion.1.ids, bf16[128,1536]{1,0:T(8,128)(2,1)} %get-tuple-element.126.refs_0_, s32[8]{0:T(128)S(1)} %squeeze.21.refs_1_.refs_5_, f32[1]{0:T(128)S(1)} %bitcast.50, ...), custom_call_target="tpu_custom_call" | custom-call | flops 31457280 | bytes 22020096 | tf_op jit(solution)/shard_map/norm_tokens/pallas_call | solution.py:68
  38.7 10.6 %collective-permute-done.6.refs_3_ = bf16[128,1536]{1,0:T(8,128)(2,1)S(1)} collective-permute-done((bf16[128,1536]{1,0:T(8,128)(2,1)}, bf16[128,1536]{1,0:T(8,128)(2,1)S(1)}, u32[]{:S(2)}, u32[]{:S(2)}) %collective-permute-start.6) | collective-permute-done | bytes 393248 | tf_op jit(solution)/shard_map/ppermute | solution.py:1053
  49.3 8.0 %collective-permute-done.5.refs_2_ = bf16[128,1536]{1,0:T(8,128)(2,1)S(1)} collective-permute-done((bf16[128,1536]{1,0:T(8,128)(2,1)}, bf16[128,1536]{1,0:T(8,128)(2,1)S(1)}, u32[]{:S(2)}, u32[]{:S(2)}) %collective-permute-start.5) | collective-permute-done | bytes 393248 | tf_op jit(solution)/shard_map/ppermute | solution.py:1053
  57.3 1.7 collective-permute-done.4.refs_1_
  60.0 1.3 hand_on.2.refs_0_
  61.5 1.6 collective-permute-start.8
  64.9 14.7 %collective-permute-done.8.refs_2_.refs_7_ = bf16[384,768]{1,0:T(8,128)(2,1)S(1)} collective-permute-done((bf16[384,768]{1,0:T(8,128)(2,1)S(1)}, bf16[384,768]{1,0:T(8,128)(2,1)S(1)}, u32[]{:S(2)}, u32[]{:S(2)}) %collective-permute-start.8) | collective-permute-done | bytes 589856 | tf_op jit(solution)/shard_map/ppermute | solution.py:1053
  79.7 1.2 collective-permute-done.7.refs_1_.refs_6_
  80.9 1.3 cross_pieces_0.1
  83.3 1.4 plane_pieces_1.1.refs_0_.refs_5_
  84.7 1.5 collective-permute-start.12
  86.2 1.5 collective-permute-start.11
  87.8 4.6 %collective-permute-done.9.refs_8_ = bf16[384,384]{1,0:T(8,128)(2,1)S(1)} collective-permute-done((bf16[384,384]{1,0:T(8,128)(2,1)}, bf16[384,384]{1,0:T(8,128)(2,1)S(1)}, u32[]{:S(2)}, u32[]{:S(2)}) %collective-permute-start.9) | collective-permute-done | bytes 294944 | tf_op jit(solution)/shard_map/ppermute | solution.py:1053
  93.4 11.3 %project_0.1 = (f32[6,2,128,256]{3,2,1,0:T(8,128)S(1)}, f32[6,2,128,256]{3,2,1,0:T(8,128)S(1)}, f32[6,2,128,256]{3,2,1,0:T(8,128)S(1)}, f32[32,256]{1,0:T(8,128)...) custom-call(s32[3]{0:T(128)S(1)} %pad_add_fusion.1.ids, bf16[384,768]{1,0:T(8,128)(2,1)} %plane_pieces_1.1.refs_0_.refs_5_, ...), custom_call_target="tpu_custom_call" | custom-call | flops 4831838208 | bytes 12582912 | tf_op jit(solution)/shard_map/project_0/pallas_call | solution.py:90
  105.9 2.9 collective-permute-done.12.refs_2_.refs_7_
  108.7 5.6 %collective-permute-done.11.refs_1_.refs_6_ = bf16[384,768]{1,0:T(8,128)(2,1)} collective-permute-done((bf16[384,768]{1,0:T(8,128)(2,1)}, bf16[384,768]{1,0:T(8,128)(2,1)}, u32[]{:S(2)}, u32[]{:S(2)}) %collective-permute-start.11) | collective-permute-done | bytes 589856 | tf_op jit(solution)/shard_map/ppermute | solution.py:1053
  114.3 2.1 cross_pieces_1.1
  117.5 6.0 %collective-permute-done.13.refs_8_ = bf16[384,384]{1,0:T(8,128)(2,1)} collective-permute-done((bf16[384,384]{1,0:T(8,128)(2,1)}, bf16[384,384]{1,0:T(8,128)(2,1)}, u32[]{:S(2)}, u32[]{:S(2)}) %collective-permute-start.13) | collective-permute-done | bytes 294944 | tf_op jit(solution)/shard_map/ppermute | solution.py:1053
  124.0 11.4 %project_1.1 = (f32[6,2,128,256]{3,2,1,0:T(8,128)S(1)}, f32[6,2,128,256]{3,2,1,0:T(8,128)S(1)}, f32[6,2,128,256]{3,2,1,0:T(8,128)S(1)}, f32[32,256]{1,0:T(8,128)...) custom-call(s32[3]{0:T(128)S(1)} %pad_add_fusion.1.ids, bf16[384,384]{1,0:T(8,128)(2,1)} %get-tuple-element.133.refs_0_, ...), custom_call_target="tpu_custom_call" | custom-call | flops 4831838208 | bytes 12582912 | tf_op jit(solution)/shard_map/project_1/pallas_call | solution.py:90
  135.4 8.7 %all-gather = f32[8,8,256]{2,1,0:T(8,128)S(1)} all-gather(f32[2,8,256]{2,1,0:T(8,128)S(1)} %get-tuple-element.135.refs_0_), channel_id=2, replica_groups=mesh['seq'=4,'dp'=8] {'seq'}, dimensions={0}, use_global_device_ids=true | all-gather | bytes 81920 | tf_op jit(solution)/shard_map/all_gather | solution.py:1135
  144.2 11.4 %states_0.1 = (bf16[4,2,768,128]{3,2,1,0:T(8,128)(2,1)}, bf16[4,2,768,128]{3,2,1,0:T(8,128)(2,1)}, f32[6,2,128,256]{3,2,1,0:T(8,128)S(1)}, f32[6,2,128,256]{3,2,...) custom-call(s32[3]{0:T(128)S(1)} %pad_add_fusion.1.ids, ...), custom_call_target="tpu_custom_call" | custom-call | flops 47185920 | bytes 7864320 | tf_op jit(solution)/shard_map/states_0/pallas_call | solution.py:90
  155.7 7.8 %all-gather.1 = f32[8,8,256]{2,1,0:T(8,128)S(1)} all-gather(f32[2,8,256]{2,1,0:T(8,128)S(1)} %get-tuple-element.154), channel_id=3, replica_groups=mesh['seq'=4,'dp'=8] {'seq'}, dimensions={0}, use_global_device_ids=true | all-gather | bytes 81920 | tf_op jit(solution)/shard_map/all_gather | solution.py:1135
  163.5 2.7 adjoints_0.1
  166.2 7.9 %weight_grad_part.4 = (bf16[3,1024,128]{2,1,0:T(8,128)(2,1)S(1)}, bf16[3,1024,128]{2,1,0:T(8,128)(2,1)S(1)}, bf16[3,1024,128]{2,1,0:T(8,128)(2,1)S(1)}, bf16[3,5...) custom-call(s32[3]{0:T(128)S(1)} %pad_add_fusion.1.ids, f32[2,16,256]{2,1,0:T(8,128)S(1)} %get-tuple-element.155.refs_0_.refs_10_, ...), custom_call_target="tpu_custom_call" | custom-call | flops 4831838208 | bytes 6291456 | tf_op jit(solution)/shard_map/weight_grad_part/pallas_call | solution.py:90
  176.2 9.4 %weight_grad_part.5 = (bf16[3,1024,128]{2,1,0:T(8,128)(2,1)S(1)}, bf16[3,1024,128]{2,1,0:T(8,128)(2,1)S(1)}, bf16[3,1024,128]{2,1,0:T(8,128)(2,1)S(1)}, bf16[3,5...) custom-call(s32[3]{0:T(128)S(1)} %pad_add_fusion.1.ids, ...), custom_call_target="tpu_custom_call" | custom-call | flops 4831838208 | bytes 6291456 | tf_op jit(solution)/shard_map/weight_grad_part/pallas_call | solution.py:90
  189.5 1.8 relay_sums.4
  193.3 10.5 %project_2.1 = (f32[6,2,128,256]{3,2,1,0:T(8,128)S(1)}, f32[6,2,128,256]{3,2,1,0:T(8,128)S(1)}, f32[6,2,128,256]{3,2,1,0:T(8,128)S(1)}, f32[32,256]{1,0:T(8,128)S(1)}, f32[2,8,256]{2,1,0:T(8,128)S(1)}) custom-call(s32[3]{0:T(128)S(1)} %pad_add_fusion.1.ids, bf16[3,1024,128]{2,1,0:T(8,128)(2,1)} %get-tuple-element.165.refs_0_, ...), custom_call_target="tpu_custom_call" | custom-call | flops 4831838208 | bytes 12582912 | tf_op jit(solution)/shard_map/project_2/pallas_call | solution.py:90
  203.9 1.3 relay_sums.5
  207.3 10.5 %project_3.1 = (f32[6,2,128,256]{3,2,1,0:T(8,128)S(1)}, f32[6,2,128,256]{3,2,1,0:T(8,128)S(1)}, f32[6,2,128,256]{3,2,1,0:T(8,128)S(1)}, f32[32,256]{1,0:T(8,128)S(1)}, f32[2,8,256]{2,1,0:T(8,128)S(1)}) custom-call(s32[3]{0:T(128)S(1)} %pad_add_fusion.1.ids, bf16[3,1024,128]{2,1,0:T(8,128)(2,1)S(1)} %get-tuple-element.170.refs_0_, ...), custom_call_target="tpu_custom_call" | custom-call | flops 4831838208 | bytes 12582912 | tf_op jit(solution)/shard_map/project_3/pallas_call | solution.py:90
  217.8 10.4 %all-gather.2 = f32[8,8,256]{2,1,0:T(8,128)S(1)} all-gather(f32[2,8,256]{2,1,0:T(8,128)S(1)} %get-tuple-element.171.refs_0_), channel_id=4, replica_groups=mesh['seq'=4,'dp'=8] {'seq'}, dimensions={0}, use_global_device_ids=true | all-gather | bytes 81920 | tf_op jit(solution)/shard_map/all_gather | solution.py:1135
  228.2 11.4 %states_1.1 = (bf16[4,2,768,128]{3,2,1,0:T(8,128)(2,1)}, bf16[4,2,768,128]{3,2,1,0:T(8,128)(2,1)}, f32[6,2,128,256]{3,2,1,0:T(8,128)S(1)}, f32[6,2,128,256]{3,2,...) custom-call(s32[3]{0:T(128)S(1)} %pad_add_fusion.1.ids, ...), custom_call_target="tpu_custom_call", output_to_operand_aliasing={{0}: (21, {}), {1}: (22, {})} | custom-call | flops 47185920 | bytes 7864320 | tf_op jit(solution)/shard_map/states_1/pallas_call | solution.py:90
  242.1 1.4 copy-done.1
  244.0 8.7 %all-gather.3 = f32[8,8,256]{2,1,0:T(8,128)S(1)} all-gather(f32[2,8,256]{2,1,0:T(8,128)S(1)} %hand_on.3.refs_0_), channel_id=5, replica_groups=mesh['seq'=4,'dp'=8] {'seq'}, dimensions={0}, use_global_device_ids=true | all-gather | bytes 81920 | tf_op jit(solution)/shard_map/all_gather | solution.py:1135
  252.7 2.7 adjoints_1.1
  255.4 7.9 %weight_grad_part.6 = (bf16[3,1024,128]{2,1,0:T(8,128)(2,1)S(1)}, bf16[3,1024,128]{2,1,0:T(8,128)(2,1)S(1)}, bf16[3,1024,128]{2,1,0:T(8,128)(2,1)S(1)}, bf16[3,5...) custom-call(s32[3]{0:T(128)S(1)} %pad_add_fusion.1.ids, f32[2,16,256]{2,1,0:T(8,128)S(1)} %get-tuple-element.199.refs_0_.refs_11_, ...), custom_call_target="tpu_custom_call" | custom-call | flops 4831838208 | bytes 6291456 | tf_op jit(solution)/shard_map/weight_grad_part/pallas_call | solution.py:90
  263.5 1.9 collective-permute-start.24
  265.4 8.1 %weight_grad_part.7 = (bf16[3,1024,128]{2,1,0:T(8,128)(2,1)S(1)}, bf16[3,1024,128]{2,1,0:T(8,128)(2,1)S(1)}, bf16[3,1024,128]{2,1,0:T(8,128)(2,1)S(1)}, bf16[3,5...) custom-call(s32[3]{0:T(128)S(1)} %pad_add_fusion.1.ids, bf16[3,512,128]{2,1,0:T(8,128)(2,1)S(1)} %get-tuple-element.202.refs_0_, ...), custom_call_target="tpu_custom_call" | custom-call | flops 4831838208 | bytes 6291456 | tf_op jit(solution)/shard_map/weight_grad_part/pallas_call | solution.py:90
  273.7 1.9 collective-permute-start.27
  277.4 2.0 collective-permute-start.29
  279.4 16.1 %unit_grads_1.1.refs_0_.refs_12_ = bf16[2,768,2048]{2,1,0:T(8,128)(2,1)} custom-call(s32[3]{0:T(128)S(1)} %pad_add_fusion.1.ids, bf16[2,3,256,128]{3,2,1,0:T(8,128)(2,1)S(1)} %get-tuple-element.209.refs_0_, bf16[6,2,128,512]{3,2,1,0:T(8,128)(2,1)} %get-tuple-element.210.refs_1_, bf16[6,2,128,512]{3,2,1,0:T(8,128)(2,1)} %get-tuple-element.211.refs_2_, ...), custom_call_target="tpu_custom_call" | custom-call | flops 9663676416 | bytes 12582912 | tf_op jit(solution)/shard_map/unit_grads_1/pallas_call | solution.py:90
  296.4 1.9 collective-permute-start.35
  298.4 3.6 collective-permute-done.29.refs_2_
  303.8 16.3 %unit_grads_0.1.refs_0_ = bf16[2,768,2048]{2,1,0:T(8,128)(2,1)} custom-call(s32[3]{0:T(128)S(1)} %pad_add_fusion.1.ids, bf16[1,3,512,128]{3,2,1,0:T(8,128)(2,1)S(1)} %get-tuple-element.223.refs_0_, bf16[6,2,128,512]{3,2,1,0:T(8,128)(2,1)} %get-tuple-element.210.refs_1_, ...), custom_call_target="tpu_custom_call", output_to_operand_aliasing={{}: (13, {})} | custom-call | flops 9663676416 | bytes 12582912 | tf_op jit(solution)/shard_map/unit_grads_0/pallas_call | solution.py:90
  320.9 8.6 %activations_of.1.refs_0_ = f32[2,4,96,2048]{3,2,1,0:T(8,128)} custom-call(s32[3]{0:T(128)S(1)} %pad_add_fusion.1.ids, f32[3,256,128]{2,1,0:T(8,128)S(1)} %get-tuple-element.225.refs_0_.refs_1_, bf16[2,4,96,2048]{3,2,1,0:T(8,128)(2,1)} %bitcast.59, bf16[4,2,768,128]{3,2,1,0:T(8,128)(2,1)} %get-tuple-element.226.refs_2_, bf16[4,2,768,128]{3,2,1,0:T(8,128)(2,1)} %copy-done.4), custom_call_target="tpu_custom_call" | custom-call | flops 1572864 | bytes 12582912 | tf_op jit(solution)/shard_map/activations_of/pallas_call | solution.py:68
  330.3 10.0 %all_to_all.5.refs_2_ = bf16[2,768,2048]{2,1,0:T(8,128)(2,1)} all-to-all(bf16[2,768,2048]{2,1,0:T(8,128)(2,1)S(1)} %bitcast.54), channel_id=1, replica_groups={{0,1},{2,3},{4,5},{6,7},{8,9},{10,11},{12,13},{14,15},{16,17},{18,19},{..., dimensions={0} | all-to-all | bytes 12582912 | tf_op jit(solution)/shard_map/all_to_all | solution.py:1226
  340.3 12.5 %norm_grads.1 = (f32[2,4,96,2048]{3,2,1,0:T(8,128)}, f32[8,2048]{1,0:T(8,128)S(1)}) custom-call(s32[3]{0:T(128)S(1)} %pad_add_fusion.1.ids, bf16[1,3,256,128]{3,2,1,0:T(8,128)(2,1)S(1)} %get-tuple-element.228.refs_0_, f32[3,256,128]{2,1,0:T(8,128)S(1)} %collective-permute-done.33.refs_1_.refs_3_, bf16[2,768,2048]{2,1,0:T(8,128)(2,1)} %all_to_all.5.refs_2_, ...), custom_call_target="tpu_custom_call" | custom-call | flops 31457280 | bytes 12582912 | tf_op jit(solution)/shard_map/norm_grads/pallas_call | solution.py:90
  352.7 2.0 collective-permute-start.39
  354.8 1.9 collective-permute-start.38
  359.1 1.8 collective-permute-done.38.refs_3_
  362.0 2.5 collective-permute-start.40
  364.6 2.5 collective-permute-start.43
  367.0 2.1 collective-permute-start.44
  369.9 4.2 %collective-permute-done.41.refs_2_ = f32[8,2048]{1,0:T(8,128)S(1)} collective-permute-done((f32[8,2048]{1,0:T(8,128)S(1)}, f32[8,2048]{1,0:T(8,128)S(1)}, u32[]{:S(2)}, u32[]{:S(2)}) %collective-permute-start.41) | collective-permute-done | bytes 65568 | tf_op jit(solution)/shard_map/ppermute | solution.py:1053
  376.5 4.3 %collective-permute-done.43.refs_2_ = bf16[3,256,128]{2,1,0:T(8,128)(2,1)S(1)} collective-permute-done((bf16[3,256,128]{2,1,0:T(8,128)(2,1)S(1)}, bf16[3,256,128]{2,1,0:T(8,128)(2,1)S(1)}, u32[]{:S(2)}, u32[]{:S(2)}) %collective-permute-start.43) | collective-permute-done | bytes 196640 | tf_op jit(solution)/shard_map/ppermute | solution.py:1053
  380.8 3.0 collective-permute-done.44.refs_3_
  383.7 1.3 collective-permute-done.45.refs_4_
  386.3 1.9 assemble.1
  (170 shorter events, 39.0 us)
Async XLA Ops:
  7.2 186.1 %all-gather.6.cloned.1.call-start = ((), (), s32[]{:S(2)}) async-start(), calls=%async_computation.1 | async-start | bytes 6684672 | tf_op jit(solution)/shard_map/all_gather | solution.py:1194
  7.2 11.0 %collective-permute-start = (bf16[2,384,2048]{2,1,0:T(8,128)(2,1)}, bf16[2,384,2048]{2,1,0:T(8,128)(2,1)}, u32[]{:S(2)}, u32[]{:S(2)}) collective-permute-start(bf16[2,384,2048]{2,1,0:T(8,128)(2,1)} %param.10), channel_id=1, source_target_pairs={{0,1},{1,0},{2,3},{3,2},{4,5},{5,4},{6,7},{7,6},{8,9},{9,8},{10,11... | collective-permute-start | bytes 9437192 | tf_op jit(solution)/shard_map/ppermute | solution.py:1053
  10.2 7.5 %collective-permute-start.1 = (bf16[2,384,1024]{2,1,0:T(8,128)(2,1)}, bf16[2,384,1024]{2,1,0:T(8,128)(2,1)S(1)}, u32[]{:S(2)}, u32[]{:S(2)}) collective-permute-start(bf16[2,384,1024]{2,1,0:T(8,128)(2,1)} %pad_maximum_fusion), channel_id=1, source_target_pairs={{0,1},{1,0},{2,3},{3,2},{4,5},{5,4},{6,7},{7,6},{8,9},{9,8},{10,11... | collective-permute-start | bytes 4718600 | tf_op jit(solution)/shard_map/ppermute | solution.py:1053
  10.7 3.8 copy-start.23
  14.4 6.0 %copy-start.2 = (bf16[256,3072]{1,0:T(8,128)(2,1)}, bf16[256,3072]{1,0:T(8,128)(2,1)S(1)}, u32[]{:S(2)}) copy-start(bf16[256,3072]{1,0:T(8,128)(2,1)S(1)} %get-tuple-element.124.refs_0_.refs_4_.refs_3_) | copy-start | bytes 4718596
  14.4 3.8 collective-permute-start.3
  14.5 3.0 collective-permute-start.2
  17.7 2.8 copy-start
  18.2 7.8 %copy-start.15 = (f32[2048]{0:T(1024)S(1)}, f32[2048]{0:T(1024)}, u32[]{:S(2)}) copy-start(f32[2048]{0:T(1024)} %param.17) | copy-start | bytes 24580
  18.2 7.8 %copy-start.16 = (f32[2048]{0:T(1024)S(1)}, f32[2048]{0:T(1024)}, u32[]{:S(2)}) copy-start(f32[2048]{0:T(1024)} %param.18) | copy-start | bytes 24580
  21.2 28.1 %collective-permute-start.6 = (bf16[128,1536]{1,0:T(8,128)(2,1)}, bf16[128,1536]{1,0:T(8,128)(2,1)S(1)}, u32[]{:S(2)}, u32[]{:S(2)}) collective-permute-start(bf16[128,1536]{1,0:T(8,128)(2,1)} %get-tuple-element.126.refs_0_), channel_id=1, source_target_pairs={{0,2},{1,3},{2,4},{3,5},{4,6},{5,7},{6,0},{7,1},{8,10},{9,11},{10,... | collective-permute-start | bytes 1179656 | tf_op jit(solution)/shard_map/ppermute | solution.py:1053
  22.8 34.5 %collective-permute-start.5 = (bf16[128,1536]{1,0:T(8,128)(2,1)}, bf16[128,1536]{1,0:T(8,128)(2,1)S(1)}, u32[]{:S(2)}, u32[]{:S(2)}) collective-permute-start(bf16[128,1536]{1,0:T(8,128)(2,1)} %get-tuple-element.126.refs_0_), channel_id=1, source_target_pairs={{0,4},{1,5},{2,6},{3,7},{4,0},{5,1},{6,2},{7,3},{8,12},{9,13},{10,... | collective-permute-start | bytes 1179656 | tf_op jit(solution)/shard_map/ppermute | solution.py:1053
  24.1 34.9 %collective-permute-start.4 = (bf16[128,1536]{1,0:T(8,128)(2,1)}, bf16[128,1536]{1,0:T(8,128)(2,1)S(1)}, u32[]{:S(2)}, u32[]{:S(2)}) collective-permute-start(bf16[128,1536]{1,0:T(8,128)(2,1)} %get-tuple-element.126.refs_0_), channel_id=1, source_target_pairs={{0,6},{1,7},{2,0},{3,1},{4,2},{5,3},{6,4},{7,5},{8,14},{9,15},{10,... | collective-permute-start | bytes 1179656 | tf_op jit(solution)/shard_map/ppermute | solution.py:1053
  59.6 22.6 %copy-start.3 = (bf16[384,768]{1,0:T(8,128)(2,1)}, bf16[384,768]{1,0:T(8,128)(2,1)S(1)}, u32[]{:S(2)}) copy-start(bf16[384,768]{1,0:T(8,128)(2,1)S(1)} %plane_pieces_0.1.refs_0_.refs_5_) | copy-start | bytes 1769476
  61.5 18.1 %collective-permute-start.8 = (bf16[384,768]{1,0:T(8,128)(2,1)S(1)}, bf16[384,768]{1,0:T(8,128)(2,1)S(1)}, u32[]{:S(2)}, u32[]{:S(2)}) collective-permute-start(bf16[384,768]{1,0:T(8,128)(2,1)S(1)} %plane_pieces_0.1.refs_0_.refs_5_), channel_id=1, source_target_pairs={{0,16},{1,17},{2,18},{3,19},{4,20},{5,21},{6,22},{7,23},{8,24},{9,... | collective-permute-start | bytes 1769480 | tf_op jit(solution)/shard_map/ppermute | solution.py:1053
  63.1 17.8 %collective-permute-start.7 = (bf16[384,768]{1,0:T(8,128)(2,1)S(1)}, bf16[384,768]{1,0:T(8,128)(2,1)S(1)}, u32[]{:S(2)}, u32[]{:S(2)}) collective-permute-start(bf16[384,768]{1,0:T(8,128)(2,1)S(1)} %plane_pieces_0.1.refs_0_.refs_5_), channel_id=1, source_target_pairs={{0,8},{1,9},{2,10},{3,11},{4,12},{5,13},{6,14},{7,15},{8,0},{9,1},... | collective-permute-start | bytes 1769480 | tf_op jit(solution)/shard_map/ppermute | solution.py:1053
  79.7 5.0 %copy-start.11 = (bf16[384,768]{1,0:T(8,128)(2,1)}, bf16[384,768]{1,0:T(8,128)(2,1)S(1)}, u32[]{:S(2)}) copy-start(bf16[384,768]{1,0:T(8,128)(2,1)S(1)} %collective-permute-done.8.refs_2_.refs_7_) | copy-start | bytes 1769476
  80.9 3.8 copy-start.12
  82.2 10.2 %collective-permute-start.9 = (bf16[384,384]{1,0:T(8,128)(2,1)}, bf16[384,384]{1,0:T(8,128)(2,1)S(1)}, u32[]{:S(2)}, u32[]{:S(2)}) collective-permute-start(bf16[384,384]{1,0:T(8,128)(2,1)} %get-tuple-element.131), channel_id=1, source_target_pairs={{0,8},{1,9},{2,10},{3,11},{4,12},{5,13},{6,14},{7,15},{8,0},{9,1},... | collective-permute-start | bytes 884744 | tf_op jit(solution)/shard_map/ppermute | solution.py:1053
  82.8 9.9 %collective-permute-start.10 = (bf16[384,384]{1,0:T(8,128)(2,1)S(1)}, bf16[384,384]{1,0:T(8,128)(2,1)S(1)}, u32[]{:S(2)}, u32[]{:S(2)}) collective-permute-start(bf16[384,384]{1,0:T(8,128)(2,1)S(1)} %get-tuple-element.129.refs_0_), channel_id=1, source_target_pairs={{0,16},{1,17},{2,18},{3,19},{4,20},{5,21},{6,22},{7,23},{8,24},{9,... | collective-permute-start | bytes 884744 | tf_op jit(solution)/shard_map/ppermute | solution.py:1053
  84.7 24.0 %collective-permute-start.12 = (bf16[384,768]{1,0:T(8,128)(2,1)}, bf16[384,768]{1,0:T(8,128)(2,1)}, u32[]{:S(2)}, u32[]{:S(2)}) collective-permute-start(bf16[384,768]{1,0:T(8,128)(2,1)} %plane_pieces_1.1.refs_0_.refs_5_), channel_id=1, source_target_pairs={{0,16},{1,17},{2,18},{3,19},{4,20},{5,21},{6,22},{7,23},{8,24},{9,... | collective-permute-start | bytes 1769480 | tf_op jit(solution)/shard_map/ppermute | solution.py:1053
  86.2 28.1 %collective-permute-start.11 = (bf16[384,768]{1,0:T(8,128)(2,1)}, bf16[384,768]{1,0:T(8,128)(2,1)}, u32[]{:S(2)}, u32[]{:S(2)}) collective-permute-start(bf16[384,768]{1,0:T(8,128)(2,1)} %plane_pieces_1.1.refs_0_.refs_5_), channel_id=1, source_target_pairs={{0,8},{1,9},{2,10},{3,11},{4,12},{5,13},{6,14},{7,15},{8,0},{9,1},... | collective-permute-start | bytes 1769480 | tf_op jit(solution)/shard_map/ppermute | solution.py:1053
  116.5 7.0 %collective-permute-start.13 = (bf16[384,384]{1,0:T(8,128)(2,1)}, bf16[384,384]{1,0:T(8,128)(2,1)}, u32[]{:S(2)}, u32[]{:S(2)}) collective-permute-start(bf16[384,384]{1,0:T(8,128)(2,1)} %get-tuple-element.134), channel_id=1, source_target_pairs={{0,8},{1,9},{2,10},{3,11},{4,12},{5,13},{6,14},{7,15},{8,0},{9,1},... | collective-permute-start | bytes 884744 | tf_op jit(solution)/shard_map/ppermute | solution.py:1053
  117.0 7.0 %collective-permute-start.14 = (bf16[384,384]{1,0:T(8,128)(2,1)}, bf16[384,384]{1,0:T(8,128)(2,1)}, u32[]{:S(2)}, u32[]{:S(2)}) collective-permute-start(bf16[384,384]{1,0:T(8,128)(2,1)} %get-tuple-element.133.refs_0_), channel_id=1, source_target_pairs={{0,16},{1,17},{2,18},{3,19},{4,20},{5,21},{6,22},{7,23},{8,24},{9,... | collective-permute-start | bytes 884744 | tf_op jit(solution)/shard_map/ppermute | solution.py:1053
  124.0 20.2 %copy-start.6 = (f32[6,2,128,256]{3,2,1,0:T(8,128)S(1)}, f32[6,2,128,256]{3,2,1,0:T(8,128)}, u32[]{:S(2)}) copy-start(f32[6,2,128,256]{3,2,1,0:T(8,128)} %copy-done.5) | copy-start | bytes 4718596
  174.1 15.3 %collective-permute-start.16 = (bf16[3,512,128]{2,1,0:T(8,128)(2,1)S(1)}, bf16[3,512,128]{2,1,0:T(8,128)(2,1)S(1)}, u32[]{:S(2)}, u32[]{:S(2)}) collective-permute-start(bf16[3,512,128]{2,1,0:T(8,128)(2,1)S(1)} %get-tuple-element.164), channel_id=1, source_target_pairs={{0,16},{1,17},{2,18},{3,19},{4,20},{5,21},{6,22},{7,23},{8,24},{9,... | collective-permute-start | bytes 1179656 | tf_op jit(solution)/shard_map/ppermute | solution.py:1053
  175.3 14.2 %collective-permute-start.15 = (bf16[3,512,128]{2,1,0:T(8,128)(2,1)S(1)}, bf16[3,512,128]{2,1,0:T(8,128)(2,1)S(1)}, u32[]{:S(2)}, u32[]{:S(2)}) collective-permute-start(bf16[3,512,128]{2,1,0:T(8,128)(2,1)S(1)} %get-tuple-element.159.refs_0_), channel_id=1, source_target_pairs={{0,8},{1,9},{2,10},{3,11},{4,12},{5,13},{6,14},{7,15},{8,0},{9,1},... | collective-permute-start | bytes 1179656 | tf_op jit(solution)/shard_map/ppermute | solution.py:1053
  187.4 5.9 %copy-start.17 = (f32[1,256]{1,0:T(1,128)S(1)}, f32[1,256]{1,0:T(1,128)}, u32[]{:S(2)}) copy-start(f32[1,256]{1,0:T(1,128)} %get-tuple-element.256.refs_6_) | copy-start | bytes 3076
  187.4 5.9 %copy-start.18 = (f32[1,256]{1,0:T(1,128)S(1)}, f32[1,256]{1,0:T(1,128)}, u32[]{:S(2)}) copy-start(f32[1,256]{1,0:T(1,128)} %get-tuple-element.260.refs_5_) | copy-start | bytes 3076
  187.4 16.4 %collective-permute-start.18 = (bf16[3,512,128]{2,1,0:T(8,128)(2,1)}, bf16[3,512,128]{2,1,0:T(8,128)(2,1)}, u32[]{:S(2)}, u32[]{:S(2)}) collective-permute-start(bf16[3,512,128]{2,1,0:T(8,128)(2,1)} %get-tuple-element.169), channel_id=1, source_target_pairs={{0,16},{1,17},{2,18},{3,19},{4,20},{5,21},{6,22},{7,23},{8,24},{9,... | collective-permute-start | bytes 1179656 | tf_op jit(solution)/shard_map/ppermute | solution.py:1053
  188.5 15.3 %collective-permute-start.17 = (bf16[3,512,128]{2,1,0:T(8,128)(2,1)}, bf16[3,512,128]{2,1,0:T(8,128)(2,1)}, u32[]{:S(2)}, u32[]{:S(2)}) collective-permute-start(bf16[3,512,128]{2,1,0:T(8,128)(2,1)} %get-tuple-element.161.refs_0_), channel_id=1, source_target_pairs={{0,8},{1,9},{2,10},{3,11},{4,12},{5,13},{6,14},{7,15},{8,0},{9,1},... | collective-permute-start | bytes 1179656 | tf_op jit(solution)/shard_map/ppermute | solution.py:1053
  191.3 37.0 %collective-permute-start.19 = (bf16[3,1024,128]{2,1,0:T(8,128)(2,1)}, bf16[3,1024,128]{2,1,0:T(8,128)(2,1)S(1)}, u32[]{:S(2)}, u32[]{:S(2)}) collective-permute-start(bf16[3,1024,128]{2,1,0:T(8,128)(2,1)} %get-tuple-element.172), channel_id=1, source_target_pairs={{0,8},{1,9},{2,10},{3,11},{4,12},{5,13},{6,14},{7,15},{8,0},{9,1},... | collective-permute-start | bytes 2359304 | tf_op jit(solution)/shard_map/ppermute | solution.py:1053
  192.4 35.8 %collective-permute-start.20 = (bf16[3,1024,128]{2,1,0:T(8,128)(2,1)}, bf16[3,1024,128]{2,1,0:T(8,128)(2,1)S(1)}, u32[]{:S(2)}, u32[]{:S(2)}) collective-permute-start(bf16[3,1024,128]{2,1,0:T(8,128)(2,1)} %get-tuple-element.165.refs_0_), channel_id=1, source_target_pairs={{0,16},{1,17},{2,18},{3,19},{4,20},{5,21},{6,22},{7,23},{8,24},{9,... | collective-permute-start | bytes 2359304 | tf_op jit(solution)/shard_map/ppermute | solution.py:1053
  193.3 10.6 %copy-start.8 = (bf16[3,1024,128]{2,1,0:T(8,128)(2,1)S(1)}, bf16[3,1024,128]{2,1,0:T(8,128)(2,1)}, u32[]{:S(2)}) copy-start(bf16[3,1024,128]{2,1,0:T(8,128)(2,1)} %copy-done.7) | copy-start | bytes 2359300
  193.3 10.6 %copy-start.10 = (bf16[3,1024,128]{2,1,0:T(8,128)(2,1)S(1)}, bf16[3,1024,128]{2,1,0:T(8,128)(2,1)}, u32[]{:S(2)}) copy-start(bf16[3,1024,128]{2,1,0:T(8,128)(2,1)} %copy-done.9) | copy-start | bytes 2359300
  205.2 34.4 %collective-permute-start.21 = (bf16[3,1024,128]{2,1,0:T(8,128)(2,1)S(1)}, bf16[3,1024,128]{2,1,0:T(8,128)(2,1)S(1)}, u32[]{:S(2)}, u32[]{:S(2)}) collective-permute-start(bf16[3,1024,128]{2,1,0:T(8,128)(2,1)S(1)} %get-tuple-element.186), channel_id=1, source_target_pairs={{0,8},{1,9},{2,10},{3,11},{4,12},{5,13},{6,14},{7,15},{8,0},{9,1},... | collective-permute-start | bytes 2359304 | tf_op jit(solution)/shard_map/ppermute | solution.py:1053
  206.4 33.3 %collective-permute-start.22 = (bf16[3,1024,128]{2,1,0:T(8,128)(2,1)S(1)}, bf16[3,1024,128]{2,1,0:T(8,128)(2,1)S(1)}, u32[]{:S(2)}, u32[]{:S(2)}) collective-permute-start(bf16[3,1024,128]{2,1,0:T(8,128)(2,1)S(1)} %get-tuple-element.170.refs_0_), channel_id=1, source_target_pairs={{0,16},{1,17},{2,18},{3,19},{4,20},{5,21},{6,22},{7,23},{8,24},{9,... | collective-permute-start | bytes 2359304 | tf_op jit(solution)/shard_map/ppermute | solution.py:1053
  241.4 24.0 %collective-permute-start.23 = (bf16[4,2,768,128]{3,2,1,0:T(8,128)(2,1)}, bf16[4,2,768,128]{3,2,1,0:T(8,128)(2,1)S(1)}, u32[]{:S(2)}, u32[]{:S(2)}) collective-permute-start(bf16[4,2,768,128]{3,2,1,0:T(8,128)(2,1)} %gate.1.refs_0_), channel_id=1, source_target_pairs={{0,1},{1,0},{2,3},{3,2},{4,5},{5,4},{6,7},{7,6},{8,9},{9,8},{10,11... | collective-permute-start | bytes 4718600 | tf_op jit(solution)/shard_map/ppermute | solution.py:1053
  241.5 35.1 %collective-permute-start.26 = (bf16[2,3,512,128]{3,2,1,0:T(8,128)(2,1)S(1)}, bf16[2,3,512,128]{3,2,1,0:T(8,128)(2,1)S(1)}, u32[]{:S(2)}, u32[]{:S(2)}) collective-permute-start(bf16[2,3,512,128]{3,2,1,0:T(8,128)(2,1)S(1)} %get-tuple-element.187.refs_0_), channel_id=1, source_target_pairs={{0,4},{1,5},{2,6},{3,7},{4,0},{5,1},{6,2},{7,3},{8,12},{9,13},{10,... | collective-permute-start | bytes 2359304 | tf_op jit(solution)/shard_map/ppermute | solution.py:1053
  263.3 12.3 %collective-permute-start.25 = (bf16[3,512,128]{2,1,0:T(8,128)(2,1)S(1)}, bf16[3,512,128]{2,1,0:T(8,128)(2,1)S(1)}, u32[]{:S(2)}, u32[]{:S(2)}) collective-permute-start(bf16[3,512,128]{2,1,0:T(8,128)(2,1)S(1)} %get-tuple-element.206), channel_id=1, source_target_pairs={{0,16},{1,17},{2,18},{3,19},{4,20},{5,21},{6,22},{7,23},{8,24},{9,... | collective-permute-start | bytes 1179656 | tf_op jit(solution)/shard_map/ppermute | solution.py:1053
  263.5 12.2 %collective-permute-start.24 = (bf16[3,512,128]{2,1,0:T(8,128)(2,1)S(1)}, bf16[3,512,128]{2,1,0:T(8,128)(2,1)S(1)}, u32[]{:S(2)}, u32[]{:S(2)}) collective-permute-start(bf16[3,512,128]{2,1,0:T(8,128)(2,1)S(1)} %get-tuple-element.202.refs_0_), channel_id=1, source_target_pairs={{0,8},{1,9},{2,10},{3,11},{4,12},{5,13},{6,14},{7,15},{8,0},{9,1},... | collective-permute-start | bytes 1179656 | tf_op jit(solution)/shard_map/ppermute | solution.py:1053
  265.4 8.1 %copy-start.4 = (bf16[4,2,768,128]{3,2,1,0:T(8,128)(2,1)}, bf16[4,2,768,128]{3,2,1,0:T(8,128)(2,1)S(1)}, u32[]{:S(2)}) copy-start(bf16[4,2,768,128]{3,2,1,0:T(8,128)(2,1)S(1)} %collective-permute-done.23.refs_1_.refs_3_) | copy-start | bytes 4718596
  273.6 21.9 %collective-permute-start.28 = (bf16[3,512,128]{2,1,0:T(8,128)(2,1)S(1)}, bf16[3,512,128]{2,1,0:T(8,128)(2,1)S(1)}, u32[]{:S(2)}, u32[]{:S(2)}) collective-permute-start(bf16[3,512,128]{2,1,0:T(8,128)(2,1)S(1)} %get-tuple-element.219), channel_id=1, source_target_pairs={{0,16},{1,17},{2,18},{3,19},{4,20},{5,21},{6,22},{7,23},{8,24},{9,... | collective-permute-start | bytes 1179656 | tf_op jit(solution)/shard_map/ppermute | solution.py:1053
  273.7 21.8 %collective-permute-start.27 = (bf16[3,512,128]{2,1,0:T(8,128)(2,1)S(1)}, bf16[3,512,128]{2,1,0:T(8,128)(2,1)S(1)}, u32[]{:S(2)}, u32[]{:S(2)}) collective-permute-start(bf16[3,512,128]{2,1,0:T(8,128)(2,1)S(1)} %get-tuple-element.203.refs_0_), channel_id=1, source_target_pairs={{0,8},{1,9},{2,10},{3,11},{4,12},{5,13},{6,14},{7,15},{8,0},{9,1},... | collective-permute-start | bytes 1179656 | tf_op jit(solution)/shard_map/ppermute | solution.py:1053
  276.4 25.5 %collective-permute-start.30 = (bf16[3,1024,128]{2,1,0:T(8,128)(2,1)S(1)}, bf16[3,1024,128]{2,1,0:T(8,128)(2,1)S(1)}, u32[]{:S(2)}, u32[]{:S(2)}) collective-permute-start(bf16[3,1024,128]{2,1,0:T(8,128)(2,1)S(1)} %get-tuple-element.207.refs_0_), channel_id=1, source_target_pairs={{0,16},{1,17},{2,18},{3,19},{4,20},{5,21},{6,22},{7,23},{8,24},{9,... | collective-permute-start | bytes 2359304 | tf_op jit(solution)/shard_map/ppermute | solution.py:1053
  277.3 42.9 %collective-permute-start.31 = (bf16[2,3,256,128]{3,2,1,0:T(8,128)(2,1)S(1)}, bf16[2,3,256,128]{3,2,1,0:T(8,128)(2,1)S(1)}, u32[]{:S(2)}, u32[]{:S(2)}) collective-permute-start(bf16[2,3,256,128]{3,2,1,0:T(8,128)(2,1)S(1)} %get-tuple-element.209.refs_0_), channel_id=1, source_target_pairs={{0,2},{1,3},{2,0},{3,1},{4,6},{5,7},{6,4},{7,5},{8,10},{9,11},{10,... | collective-permute-start | bytes 1179656 | tf_op jit(solution)/shard_map/ppermute | solution.py:1053
  277.4 24.5 %collective-permute-start.29 = (bf16[3,1024,128]{2,1,0:T(8,128)(2,1)S(1)}, bf16[3,1024,128]{2,1,0:T(8,128)(2,1)S(1)}, u32[]{:S(2)}, u32[]{:S(2)}) collective-permute-start(bf16[3,1024,128]{2,1,0:T(8,128)(2,1)S(1)} %get-tuple-element.222), channel_id=1, source_target_pairs={{0,8},{1,9},{2,10},{3,11},{4,12},{5,13},{6,14},{7,15},{8,0},{9,1},... | collective-permute-start | bytes 2359304 | tf_op jit(solution)/shard_map/ppermute | solution.py:1053
  296.3 60.4 %collective-permute-start.34 = (bf16[3,1024,128]{2,1,0:T(8,128)(2,1)S(1)}, bf16[3,1024,128]{2,1,0:T(8,128)(2,1)S(1)}, u32[]{:S(2)}, u32[]{:S(2)}) collective-permute-start(bf16[3,1024,128]{2,1,0:T(8,128)(2,1)S(1)} %get-tuple-element.233), channel_id=1, source_target_pairs={{0,8},{1,9},{2,10},{3,11},{4,12},{5,13},{6,14},{7,15},{8,0},{9,1},... | collective-permute-start | bytes 2359304 | tf_op jit(solution)/shard_map/ppermute | solution.py:1053
  296.4 61.2 %collective-permute-start.35 = (bf16[3,1024,128]{2,1,0:T(8,128)(2,1)S(1)}, bf16[3,1024,128]{2,1,0:T(8,128)(2,1)S(1)}, u32[]{:S(2)}, u32[]{:S(2)}) collective-permute-start(bf16[3,1024,128]{2,1,0:T(8,128)(2,1)S(1)} %get-tuple-element.220.refs_0_), channel_id=1, source_target_pairs={{0,16},{1,17},{2,18},{3,19},{4,20},{5,21},{6,22},{7,23},{8,24},{9,... | collective-permute-start | bytes 2359304 | tf_op jit(solution)/shard_map/ppermute | solution.py:1053
  302.8 26.8 %collective-permute-start.32 = (bf16[1,3,512,128]{3,2,1,0:T(8,128)(2,1)S(1)}, bf16[1,3,512,128]{3,2,1,0:T(8,128)(2,1)S(1)}, u32[]{:S(2)}, u32[]{:S(2)}) collective-permute-start(bf16[1,3,512,128]{3,2,1,0:T(8,128)(2,1)S(1)} %get-tuple-element.223.refs_0_), channel_id=1, source_target_pairs={{0,4},{1,5},{2,6},{3,7},{4,0},{5,1},{6,2},{7,3},{8,12},{9,13},{10,... | collective-permute-start | bytes 1179656 | tf_op jit(solution)/shard_map/ppermute | solution.py:1053
  320.2 10.1 %slice-start = ((s8[6291456]{0:T(1024)(128)(4,1)}), s8[4194304]{0:T(1024)(128)(4,1)S(1)}, s32[]{:S(2)}) async-start(s8[6291456]{0:T(1024)(128)(4,1)} %bitcast.53), calls=%async_computation.2 | async-start | bytes 8388608
  320.8 19.4 %collective-permute-start.33 = (f32[3,256,128]{2,1,0:T(8,128)S(1)}, f32[3,256,128]{2,1,0:T(8,128)S(1)}, u32[]{:S(2)}, u32[]{:S(2)}) collective-permute-start(f32[3,256,128]{2,1,0:T(8,128)S(1)} %get-tuple-element.229), channel_id=1, source_target_pairs={{0,1},{1,0},{2,3},{3,2},{4,5},{5,4},{6,7},{7,6},{8,9},{9,8},{10,11... | collective-permute-start | bytes 1179656 | tf_op jit(solution)/shard_map/ppermute | solution.py:1053
  320.9 9.4 %slice-start.1 = ((s8[6291456]{0:T(1024)(128)(4,1)}), s8[2097152]{0:T(1024)(128)(4,1)S(1)}, s32[]{:S(2)}) async-start(s8[6291456]{0:T(1024)(128)(4,1)} %bitcast.53), calls=%async_computation.3 | async-start | bytes 4194304
  330.2 28.3 %collective-permute-start.36 = (bf16[1,3,256,128]{3,2,1,0:T(8,128)(2,1)S(1)}, bf16[1,3,256,128]{3,2,1,0:T(8,128)(2,1)S(1)}, u32[]{:S(2)}, u32[]{:S(2)}) collective-permute-start(bf16[1,3,256,128]{3,2,1,0:T(8,128)(2,1)S(1)} %get-tuple-element.228.refs_0_), channel_id=1, source_target_pairs={{0,2},{1,3},{2,0},{3,1},{4,6},{5,7},{6,4},{7,5},{8,10},{9,11},{10,... | collective-permute-start | bytes 589832 | tf_op jit(solution)/shard_map/ppermute | solution.py:1053
  352.7 6.3 %collective-permute-start.39 = (f32[8,2048]{1,0:T(8,128)S(1)}, f32[8,2048]{1,0:T(8,128)S(1)}, u32[]{:S(2)}, u32[]{:S(2)}) collective-permute-start(f32[8,2048]{1,0:T(8,128)S(1)} %get-tuple-element.231.refs_0_.refs_1_), channel_id=1, source_target_pairs={{0,6},{1,7},{2,0},{3,1},{4,2},{5,3},{6,4},{7,5},{8,14},{9,15},{10,... | collective-permute-start | bytes 196616 | tf_op jit(solution)/shard_map/ppermute | solution.py:1053
  354.8 6.1 %collective-permute-start.38 = (f32[8,2048]{1,0:T(8,128)S(1)}, f32[8,2048]{1,0:T(8,128)S(1)}, u32[]{:S(2)}, u32[]{:S(2)}) collective-permute-start(f32[8,2048]{1,0:T(8,128)S(1)} %get-tuple-element.231.refs_0_.refs_1_), channel_id=1, source_target_pairs={{0,4},{1,5},{2,6},{3,7},{4,0},{5,1},{6,2},{7,3},{8,12},{9,13},{10,... | collective-permute-start | bytes 196616 | tf_op jit(solution)/shard_map/ppermute | solution.py:1053
  356.7 4.8 %collective-permute-start.37 = (f32[8,2048]{1,0:T(8,128)S(1)}, f32[8,2048]{1,0:T(8,128)S(1)}, u32[]{:S(2)}, u32[]{:S(2)}) collective-permute-start(f32[8,2048]{1,0:T(8,128)S(1)} %get-tuple-element.231.refs_0_.refs_1_), channel_id=1, source_target_pairs={{0,2},{1,3},{2,4},{3,5},{4,6},{5,7},{6,0},{7,1},{8,10},{9,11},{10,... | collective-permute-start | bytes 196616 | tf_op jit(solution)/shard_map/ppermute | solution.py:1053
  362.0 7.2 %collective-permute-start.40 = (f32[8,2048]{1,0:T(8,128)S(1)}, f32[8,2048]{1,0:T(8,128)S(1)}, u32[]{:S(2)}, u32[]{:S(2)}) collective-permute-start(f32[8,2048]{1,0:T(8,128)S(1)} %add_up.4.refs_0_.refs_1_), channel_id=1, source_target_pairs={{0,8},{1,9},{2,10},{3,11},{4,12},{5,13},{6,14},{7,15},{8,0},{9,1},... | collective-permute-start | bytes 196616 | tf_op jit(solution)/shard_map/ppermute | solution.py:1053
  364.6 16.2 %collective-permute-start.43 = (bf16[3,256,128]{2,1,0:T(8,128)(2,1)S(1)}, bf16[3,256,128]{2,1,0:T(8,128)(2,1)S(1)}, u32[]{:S(2)}, u32[]{:S(2)}) collective-permute-start(bf16[3,256,128]{2,1,0:T(8,128)(2,1)S(1)} %get-tuple-element.237), channel_id=1, source_target_pairs={{0,2},{1,3},{2,4},{3,5},{4,6},{5,7},{6,0},{7,1},{8,10},{9,11},{10,... | collective-permute-start | bytes 589832 | tf_op jit(solution)/shard_map/ppermute | solution.py:1053
  367.0 16.7 %collective-permute-start.44 = (bf16[3,256,128]{2,1,0:T(8,128)(2,1)S(1)}, bf16[3,256,128]{2,1,0:T(8,128)(2,1)S(1)}, u32[]{:S(2)}, u32[]{:S(2)}) collective-permute-start(bf16[3,256,128]{2,1,0:T(8,128)(2,1)S(1)} %get-tuple-element.238), channel_id=1, source_target_pairs={{0,4},{1,5},{2,6},{3,7},{4,0},{5,1},{6,2},{7,3},{8,12},{9,13},{10,... | collective-permute-start | bytes 589832 | tf_op jit(solution)/shard_map/ppermute | solution.py:1053
  369.2 15.9 %collective-permute-start.45 = (bf16[3,256,128]{2,1,0:T(8,128)(2,1)S(1)}, bf16[3,256,128]{2,1,0:T(8,128)(2,1)S(1)}, u32[]{:S(2)}, u32[]{:S(2)}) collective-permute-start(bf16[3,256,128]{2,1,0:T(8,128)(2,1)S(1)} %get-tuple-element.234.refs_0_), channel_id=1, source_target_pairs={{0,6},{1,7},{2,0},{3,1},{4,2},{5,3},{6,4},{7,5},{8,14},{9,15},{10,... | collective-permute-start | bytes 589832 | tf_op jit(solution)/shard_map/ppermute | solution.py:1053
  369.8 4.3 %collective-permute-start.41 = (f32[8,2048]{1,0:T(8,128)S(1)}, f32[8,2048]{1,0:T(8,128)S(1)}, u32[]{:S(2)}, u32[]{:S(2)}) collective-permute-start(f32[8,2048]{1,0:T(8,128)S(1)} %add_up.5.refs_0_.refs_1_), channel_id=1, source_target_pairs={{0,16},{1,17},{2,18},{3,19},{4,20},{5,21},{6,22},{7,23},{8,24},{9,... | collective-permute-start | bytes 196616 | tf_op jit(solution)/shard_map/ppermute | solution.py:1053
  374.6 1.3 collective-permute-start.42
  374.7 11.6 %collective-permute-start.46 = (f32[3,256,128]{2,1,0:T(8,128)S(1)}, f32[3,256,128]{2,1,0:T(8,128)S(1)}, u32[]{:S(2)}, u32[]{:S(2)}) collective-permute-start(f32[3,256,128]{2,1,0:T(8,128)S(1)} %fold_z.12.refs_0_), channel_id=1, source_target_pairs={{0,1},{1,0},{2,3},{3,2},{4,5},{5,4},{6,7},{7,6},{8,9},{9,8},{10,11... | collective-permute-start | bytes 1179656 | tf_op jit(solution)/shard_map/ppermute | solution.py:1053
  (12 other events, 15.0 us)
Sparse Core Ops, SparseCore 0:
  61.5 105.2 all-gather.5
